TPU v7x, 512 devices: a whole 4x8x8 slice. The times are simulated.
512 devices in a mesh: snode: 64 (over x, z, core), grp: 8 (over y).
Axes of the slice: x: 4, y: 8, z: 8, core: 2. Of those that a mesh axis runs over, the one named last changes fastest.
Arguments:
- ancestor_inverse: float32 [256, 256, 256], P('snode', 'grp'), may hold values from -6 to 6
- panel: float32 [64, 8, 256, 256], P('snode', None, 'grp'), may hold values from -0.125 to 0.125
- need_list: int32 [64, 8, 8], P('snode'), may hold values from 0 to 255, as said below
- diag_factor: float32 [64, 256, 256], P('snode', 'grp'), may hold values from -6 to 6
Outputs:
- off_inverse: float32 [64, 8, 256, 256], P('snode', None, 'grp')
- diag_inverse: float32 [64, 256, 256], P('snode', 'grp')
Inputs may be any that keep to these rules, and one draw needn't show every extreme that they name: `need_list`: the entries of the supernodes of one index of snode name exactly 16 distinct blocks. Of these, at most 2 are held by any one owner o (block ids 4 * o to 4 * o + 3); at least one owner holds exactly 2, and other owners may hold 2 as well.
All inputs are finite; a program needn't handle non-finite values.
Results may differ from a plain program's by a relative error of at most 0.00007.
Values sent between devices are 32-bit elements; how exact they have to be, the bound alone decides.
No kernel may reach another device: no remote copies, remote signals or barrier semaphores. Data moves between devices by JAX's collectives and lax.ppermute only.
A program may use at most 64 MiB of HBM per device.

v0:
```python
import jax
import jax.numpy as jnp
from jax import lax
from jax.sharding import PartitionSpec as P


def per_device(ancestor_inverse, panel, need_list, diag_factor):
    sn_local, kcount, rows, width = panel.shape
    block_local = ancestor_inverse.shape[0]
    wanted = need_list.reshape(-1)
    total_req = wanted.shape[0]
    owners_count = lax.axis_size("snode")
    distinct = total_req // 4
    capacity = max(2, (distinct + owners_count - 1) // owners_count)
    owner = wanted // block_local
    all_ids = jnp.arange(owners_count * block_local, dtype=jnp.int32)
    present = jnp.any(wanted[:, None] == all_ids[None, :], axis=0).astype(jnp.int32)
    present = present.reshape(owners_count, block_local)
    rank = jnp.cumsum(present, axis=1) - present
    match = (present[:, :, None] == 1) & (
        rank[:, :, None] == jnp.arange(capacity, dtype=jnp.int32)[None, None, :]
    )
    local_ids = jnp.arange(block_local, dtype=jnp.int32)[None, :, None]
    outgoing = jnp.sum(jnp.where(match, local_ids, 0), axis=1)
    slot = rank.reshape(-1)[wanted]
    found = ancestor_inverse[
        lax.all_to_all(outgoing, "snode", split_axis=0, concat_axis=0, tiled=True)
    ]
    fetched = lax.all_to_all(found, "snode", split_axis=0, concat_axis=0, tiled=True)
    flat = fetched.reshape(owners_count * capacity, rows, width)
    blocks = flat[owner * capacity + slot]
    blocks = blocks.reshape(sn_local, kcount, kcount, rows, width)
    off_inverse = -jnp.einsum(
        "sabij,sbjk->saik",
        blocks,
        lax.all_gather(panel, "grp", axis=2, tiled=True),
        precision=lax.Precision.HIGHEST,
    )
    partial_update = jnp.einsum(
        "saji,sajk->sik", panel, off_inverse, precision=lax.Precision.HIGHEST
    )
    update = lax.psum_scatter(partial_update, "grp", scatter_dimension=1, tiled=True)
    diag_inverse = diag_factor - update
    return (off_inverse, diag_inverse)


def solution(mesh):
    return jax.shard_map(
        per_device,
        mesh=mesh,
        in_specs=(
            P("snode", "grp", None),
            P("snode", None, "grp", None),
            P("snode", None, None),
            P("snode", "grp", None),
        ),
        out_specs=(P("snode", None, "grp", None), P("snode", "grp", None)),
        check_vma=False,
    )
```

profile of v0, /device:TPU:1, one launch (start us, length us, event | category | flops | bytes accessed | tf_op | source)
XLA Modules:
  0.0 223.4 jit_solution(9275860335977405877)
XLA Ops:
  7.2 0.0 copy-start
  7.2 0.8 eq.39
  8.0 0.1 fusion.9
  8.1 0.1 reshape.194
  8.2 0.2 reduce_window_sum.13
  8.4 0.1 copy.19
  8.5 0.1 copy.18
  8.6 0.1 copy.20
  8.7 23.9 %all_to_all.17 = s32[64,1,2]{2,1,0:T(1,128)S(1)} all-to-all(s32[64,1,2]{2,1,0:T(1,128)S(1)} %copy.20), channel_id=1, replica_groups=mesh['snode'=64,'grp'=8] {'snode'}, dimensions={0} | all-to-all | bytes 1024 | tf_op jit(solution)/shard_map/all_to_all | solution.py:27
  32.6 0.1 copy.21
  32.7 0.1 copy.22
  32.8 0.1 reshape.197
  33.0 2.8 %gather_fusion = f32[128,32,256]{2,1,0:T(8,128)} fusion(f32[4,32,256]{2,1,0:T(8,128)S(1)} %copy-done, s32[1024]{0:T(1024)S(1)} %pad_clamp_fusion.2), kind=kCustom, calls=%fused_computation | custom fusion | bytes 8389120 | tf_op jit(solution)/shard_map/gather | solution.py:26
  35.7 5.8 %all-to-all-start.1 = ((f32[64,2,32,256]{3,2,1,0:T(8,128)}), f32[64,2,32,256]{3,2,1,0:T(8,128)}, u32[]{:S(2)}, u32[]{:S(2)}) async-start(f32[64,2,32,256]{3,2,1,0:T(8,128)} %bitcast.42), calls=%async_computation.1 | async-start | bytes 8388608 | tf_op jit(solution)/shard_map/all_to_all | solution.py:29
  41.6 0.0 all-gather.2.cloned.1.call-start
  41.6 0.7 all-gather.2.cloned.1.call-update
  42.3 0.0 all-reduce.3.cloned.1.call-start
  42.3 0.1 reduce_window_sum.14
  42.5 0.1 reshape.190
  42.6 0.8 gather_fusion.1
  43.4 94.1 %all-to-all-done.1 = f32[64,2,32,256]{3,2,1,0:T(8,128)} async-done(((f32[64,2,32,256]{3,2,1,0:T(8,128)}), f32[64,2,32,256]{3,2,1,0:T(8,128)}, u32[]{:S(2)}, u32[]{:S(2)}) %all-to-all-start.1) | async-done | bytes 4194336 | tf_op jit(solution)/shard_map/all_to_all | solution.py:29
  137.5 2.9 %gather_fusion.2 = f32[64,32,256]{2,1,0:T(8,128)S(1)} fusion(f32[128,32,256]{2,1,0:T(8,128)} %bitcast.3, s32[1024]{0:T(1024)S(1)} %pad_clamp_fusion), kind=kCustom, calls=%fused_computation.2 | custom fusion | bytes 4194560 | tf_op jit(solution)/shard_map/gather | solution.py:31
  140.4 0.0 all-gather.2.cloned.1.call-done
  140.4 3.5 %fusion.5 = f32[8,32,256]{2,1,0:T(8,128)S(1)} fusion(f32[8,8,32,256]{3,2,1,0:T(8,128)S(1)} %bitcast.43, f32[1,8,256,256]{3,2,1,0:T(8,128)} %all-gather.2.cloned.1.call-done), kind=kOutput, calls=%fused_computation.7 | convolution fusion | flops 1610678272 | bytes 4456448 | tf_op jit(solution)/shard_map/sabij,sbjk->saik/dot_general | solution.py:33
  144.0 0.0 copy-start.1
  144.0 0.6 convolution_bitcast_fusion
  144.6 0.8 copy.23
  145.4 0.0 all-reduce.3.cloned.1.call-update
  145.4 1.3 dynamic-slice
  147.4 67.7 %all-reduce.3.cloned.1.call-done = f32[1,256,256]{2,0,1:T(1,128)} async-done(((f32[1,256,256]{2,0,1:T(1,128)}), f32[1,256,256]{2,0,1:T(1,128)}) %all-reduce.3.cloned.1.call-update) | async-done | bytes 262160
  215.1 0.8 dynamic-slice_subtract_fusion
  215.9 0.6 copy.25
  (19 shorter events, 0.1 us)
Async XLA Ops:
  7.2 25.8 %copy-start = (f32[4,32,256]{2,1,0:T(8,128)S(1)}, f32[4,32,256]{2,1,0:T(8,128)}, u32[]{:S(2)}) copy-start(f32[4,32,256]{2,1,0:T(8,128)} %param.4) | copy-start | bytes 393220
  35.7 6.7 %copy-start.4 = (s32[1,8,8]{2,1,0:T(8,128)S(1)}, s32[1,8,8]{2,1,0:T(8,128)}, u32[]{:S(2)}) copy-start(s32[1,8,8]{2,1,0:T(8,128)} %param.6) | copy-start | bytes 772
  35.7 101.8 %all-to-all-start.1 = ((f32[64,2,32,256]{3,2,1,0:T(8,128)}), f32[64,2,32,256]{3,2,1,0:T(8,128)}, u32[]{:S(2)}, u32[]{:S(2)}) async-start(f32[64,2,32,256]{3,2,1,0:T(8,128)} %bitcast.42), calls=%async_computation.1 | async-start | bytes 8388608 | tf_op jit(solution)/shard_map/all_to_all | solution.py:29
  41.6 98.8 %all-gather.2.cloned.1.call-start = ((), (), s32[]{:S(2)}) async-start(), calls=%async_computation.2 | async-start | bytes 2359296 | tf_op jit(solution)/shard_map/all_gather | solution.py:36
  42.3 172.8 %all-reduce.3.cloned.1.call-start = ((), (), s32[]{:S(2)}) async-start(), calls=%async_computation.3 | async-start | bytes 524288
  140.4 3.5 %copy-start.2 = (f32[1,8,32,256]{3,2,1,0:T(8,128)S(1)}, f32[1,8,32,256]{3,2,1,0:T(8,128)}, u32[]{:S(2)}) copy-start(f32[1,8,32,256]{3,2,1,0:T(8,128)} %param.5) | copy-start | bytes 786436
  140.4 74.7 %copy-start.3 = (f32[1,32,256]{2,1,0:T(8,128)S(1)}, f32[1,32,256]{2,1,0:T(8,128)}, u32[]{:S(2)}) copy-start(f32[1,32,256]{2,1,0:T(8,128)} %param.7) | copy-start | bytes 98308
  144.0 72.6 %copy-start.1 = (f32[8,32,256]{2,1,0:T(8,128)}, f32[8,32,256]{2,1,0:T(8,128)S(1)}, u32[]{:S(2)}) copy-start(f32[8,32,256]{2,1,0:T(8,128)S(1)} %fusion.5) | copy-start | bytes 786436
Sparse Core Ops, SparseCore 0:
  44.5 41.0 all-gather.1
  145.5 69.4 all-reduce.2
where the time goes:
time: 228 us; the launch traced here: 223 us
  waiting for transfers between devices  163 us (71%)
  blocking collectives  23.9 us (10%)
  between operations  14.9 us (7%)
  local copies, waits for them, and re-layouts  10.8 us (5%)
  starting transfers between devices  5.89 us (3%)
  matrix products  4.11 us (2%)
    all_to_all x1, waiting for transfers between devices, per_device(): lax.all_to_all(found, 'snode', split_axis=0, concat_axis=0, tiled=True)  94.1 us
    unnamed x3, waiting for transfers between devices  68.4 us
    all_to_all x1, blocking collectives, per_device(): lax.all_to_all(outgoing, 'snode', split_axis=0, concat_axis=0, tiled=True)  23.9 us
    all_to_all x1, starting transfers between devices, per_device(): lax.all_to_all(found, 'snode', split_axis=0, concat_axis=0, tiled=True)  5.81 us
  transfers between devices with their start and end apart: 3, of which 2 were waited for; matrix products, arithmetic and copies ran while one was open for 2% of the time, Pallas kernels for 0%

commit v1 on v0

v1 whole, which is shorter than its diff:
```python
import jax
import jax.numpy as jnp
from jax import lax
from jax.experimental import pallas as pl
from jax.experimental.pallas import tpu as pltpu
from jax.sharding import PartitionSpec as P

NX, NZ, NC = 4, 8, 2
SLOTS = 16


def node(x, z, c):
    return ((x % NX) * NZ + z % NZ) * NC + c


EVERY = [(x, z, c) for x in range(NX) for z in range(NZ) for c in range(NC)]
TWIN = [(node(x, z, c), node(x, z, 1 - c)) for x, z, c in EVERY]
ROUND = [(node(x, z, c), node(x, z + 1 - 2 * c, c)) for x, z, c in EVERY]
X_ONE = [(node(x, z, c), node(x ^ 1, z, c)) for x, z, c in EVERY]
X_TWO = [(node(x, z, c), node(x ^ 2, z, c)) for x, z, c in EVERY]
X_LINES = [[node(x, z, c) for x in range(NX)] for z in range(NZ) for c in range(NC)]


def split(v):
    high = v.astype(jnp.bfloat16)
    return high, (v - high.astype(jnp.float32)).astype(jnp.bfloat16)


def dot3(a, b, dims):
    (ah, al), (bh, bl) = split(a), split(b)
    dot = lambda u, v: lax.dot_general(u, v, (dims, ((), ())), preferred_element_type=jnp.float32)
    return dot(ah, bh) + (dot(ah, bl) + dot(al, bh))


def products(pick_ref, pool_ref, whole_ref, own_ref, off_ref, update_ref):
    kcount, rows, width = own_ref.shape
    total = jnp.zeros((kcount * rows, width), jnp.float32)
    for b in range(kcount):
        left = jnp.concatenate([pool_ref[pick_ref[a * kcount + b]] for a in range(kcount)], axis=0)
        total += dot3(left, whole_ref[b], ((1,), (0,)))
    off = -total
    off_ref[...] = off.reshape(off_ref.shape)
    own = own_ref[...].reshape(kcount * rows, width)
    update_ref[...] = dot3(own, off, ((0,), (0,))).reshape(update_ref.shape)


def per_device(ancestor_inverse, panel, need_list, diag_factor):
    _, kcount, rows, width = panel.shape
    held = ancestor_inverse.shape[0]
    here = lax.axis_index("snode")
    x, z, c = here // (NZ * NC), here // NC % NZ, here % NC

    wanted = need_list.reshape(-1)
    ids = jnp.arange(NX * NZ * NC * held, dtype=jnp.int32)
    present = jnp.any(wanted[:, None] == ids[None, :], axis=0)
    slot = jnp.sum((present[None, :] & (ids[None, :] < wanted[:, None])).astype(jnp.int32), axis=1)
    order = jnp.arange(SLOTS, dtype=jnp.int32)
    distinct = jnp.max(jnp.where(slot[None, :] == order[:, None], wanted[None, :], 0), axis=1)

    pair = jnp.stack([distinct, lax.ppermute(distinct, "snode", X_ONE)])
    lists = jnp.concatenate([pair, lax.ppermute(pair, "snode", X_TWO)])

    whole = lax.all_gather(panel, "grp", axis=2, tiled=True)

    chip = jnp.concatenate([ancestor_inverse, lax.ppermute(ancestor_inverse, "snode", TWIN)])
    passed, ring = chip, []
    for step in range(NZ // 2):
        passed = lax.ppermute(passed if step < NZ // 2 - 1 else passed[:held], "snode", ROUND)
        ring.append(passed)
    ring = jnp.concatenate(ring)
    pool = jnp.concatenate([chip, ring, lax.ppermute(ring, "snode", TWIN)])

    asked = lists[jnp.arange(NX) ^ x]
    owner, k = asked // held, asked % held
    oz, oc = owner // NC % NZ, owner % NC
    dz = (oz - z) % NZ
    holder = jnp.where(dz == NZ // 2, oc, (dz < NZ // 2).astype(jnp.int32))
    step = jnp.where(dz < NZ // 2, dz, NZ - dz)
    inside = jnp.where(dz == NZ // 2, (step - 1) * 2 * held, (step - 1) * 2 * held + (oc ^ holder) * held) + k
    start = jnp.where(holder == c, 2 * held, 2 * held + ring.shape[0])
    place = jnp.where(dz == 0, (oc ^ c) * held + k, start + inside)
    place = jnp.where(owner // (NC * NZ) == x, place, 0)
    answers = lax.all_to_all(
        pool[place], "snode", split_axis=0, concat_axis=0, tiled=True, axis_index_groups=X_LINES
    )
    fetched = answers.reshape(NX * SLOTS, rows, width)
    pick = wanted // (held * NC * NZ) * SLOTS + slot

    vmem = pl.BlockSpec(memory_space=pltpu.VMEM)
    off, update = pl.pallas_call(
        products,
        out_shape=(
            jax.ShapeDtypeStruct((kcount, rows, width), jnp.float32),
            jax.ShapeDtypeStruct((width // rows, rows, width), jnp.float32),
        ),
        in_specs=[pl.BlockSpec(memory_space=pltpu.SMEM), vmem, vmem, vmem],
        out_specs=(vmem, vmem),
        compiler_params=pltpu.CompilerParams(vmem_limit_bytes=32 * 1024 * 1024),
        cost_estimate=pl.CostEstimate(flops=2_000_000_000, bytes_accessed=5_000_000, transcendentals=0),
    )(pick, fetched, whole[0], panel[0])
    parts = lax.all_to_all(update, "grp", split_axis=0, concat_axis=0, tiled=True)
    return off[None], diag_factor - jnp.sum(parts, axis=0)[None]


def solution(mesh):
    return jax.shard_map(
        per_device,
        mesh=mesh,
        in_specs=(
            P("snode", "grp", None),
            P("snode", None, "grp", None),
            P("snode", None, None),
            P("snode", "grp", None),
        ),
        out_specs=(P("snode", None, "grp", None), P("snode", "grp", None)),
        check_vma=False,
    )
```

time: 228 us -> 124 us (0.54); the launches traced: 223 us -> 123 us
  waiting for transfers between devices: 163 us -> 35.1 us
  starting transfers between devices: 5.89 us -> 44.7 us
  blocking collectives: 23.9 us -> 16.1 us
  matrix products: 4.11 us -> 0 us
  local copies, waits for them, and re-layouts: 10.8 us -> 7.25 us
  Pallas kernels: 0 us -> 2.34 us
    unnamed x3 -> x1, waiting for transfers between devices: 68.4 us -> 0.02 us
    all_to_all x1, waiting for transfers between devices: 94.1 us -> 25.7 us  [per_device(): lax.all_to_all(pool[place], 'snode', split_axis=0, concat_axis=0, tiled=T...]
    ppermute x0 -> x8, starting transfers between devices: none -> 40.5 us  [the longest x4 20.2 us: per_device(): lax.ppermute(passed if step < NZ // 2 - 1 else passed[:held], 'snode', RO...]
    ppermute x0 -> x8, waiting for transfers between devices: none -> 9.36 us  [the longest x4 4.83 us: per_device(): lax.ppermute(passed if step < NZ // 2 - 1 else passed[:held], 'snode', RO...]
    all_to_all x1, blocking collectives: 23.9 us -> 16.1 us  [per_device(): lax.all_to_all(update, 'grp', split_axis=0, concat_axis=0, tiled=True)]
    dot_general x2 -> x0, matrix products: 4.11 us -> none  [the longest x1 3.51 us: per_device(): jnp.einsum('sabij,sbjk->saik', blocks, lax.all_gather(panel, 'grp', axis=...]
    gather x3 -> x2, local copies, waits for them, and re-layouts: 6.44 us -> 2.54 us  [the longest x1 1.98 us: per_device(): pool[place]]
    pallas_call x0 -> x1, Pallas kernels: none -> 2.34 us  [per_device(): pl.pallas_call(products, out_shape=(jax.ShapeDtypeStruct((kcount, rows, w...]
  transfers between devices with their start and end apart: 3 -> 10, of which waited for: 2 -> 6; matrix products, arithmetic and copies ran while one was open for 2% -> 6% of each run, Pallas kernels for 0% -> 0%
where the time goes in v1:
time: 124 us; the launch traced here: 123 us
  starting transfers between devices  44.7 us (36%)
  waiting for transfers between devices  35.1 us (28%)
  blocking collectives  16.1 us (13%)
  between operations  14.3 us (12%)
  local copies, waits for them, and re-layouts  7.25 us (6%)
  other arithmetic  3.07 us (2%)
  Pallas kernels  2.34 us (2%)
    all_to_all x1, waiting for transfers between devices, per_device(): lax.all_to_all(pool[place], 'snode', split_axis=0, concat_axis=0, tiled=T...  25.7 us
    ppermute x4, starting transfers between devices, per_device(): lax.ppermute(passed if step < NZ // 2 - 1 else passed[:held], 'snode', RO...  20.2 us
    all_to_all x1, blocking collectives, per_device(): lax.all_to_all(update, 'grp', split_axis=0, concat_axis=0, tiled=True)  16.1 us
    ppermute x1, starting transfers between devices, per_device(): lax.ppermute(ancestor_inverse, 'snode', TWIN)  8.79 us
    ppermute x4, waiting for transfers between devices, per_device(): lax.ppermute(passed if step < NZ // 2 - 1 else passed[:held], 'snode', RO...  4.83 us
    ppermute x1, starting transfers between devices, per_device(): lists = jnp.concatenate([pair, lax.ppermute(pair, 'snode', X_TWO)])  4.61 us
    all_to_all x1, starting transfers between devices, per_device(): lax.all_to_all(pool[place], 'snode', split_axis=0, concat_axis=0, tiled=T...  4.14 us
    ppermute x1, starting transfers between devices, per_device(): pool = jnp.concatenate([chip, ring, lax.ppermute(ring, 'snode', TWIN)])  3.78 us
  transfers between devices with their start and end apart: 10, of which 6 were waited for; matrix products, arithmetic and copies ran while one was open for 6% of the time, Pallas kernels for 0%

profile of v1, /device:TPU:1, one launch (start us, length us, event | category | flops | bytes accessed | tf_op | source)
XLA Modules:
  0.0 122.8 jit_solution(3809313521987292583)
XLA Ops:
  7.2 0.0 all-gather.2.cloned.1.call-start
  7.2 8.8 %collective-permute-start = (f32[4,32,256]{2,1,0:T(8,128)}, f32[4,32,256]{2,1,0:T(8,128)S(1)}, u32[]{:S(2)}, u32[]{:S(2)}) collective-permute-start(f32[4,32,256]{2,1,0:T(8,128)} %param.4), channel_id=1, source_target_pairs={{0,8},{8,0},{16,24},{24,16},{32,40},{40,32},{48,56},{56,48},{64,72... | collective-permute-start | bytes 393224 | tf_op jit(solution)/shard_map/ppermute | solution.py:65
  16.0 1.2 collective-permute-done
  17.2 0.9 pad_maximum_fusion.1
  18.1 5.3 %collective-permute-start.1 = (f32[8,32,256]{2,1,0:T(8,128)S(1)}, f32[8,32,256]{2,1,0:T(8,128)S(1)}, u32[]{:S(2)}, u32[]{:S(2)}) collective-permute-start(f32[8,32,256]{2,1,0:T(8,128)S(1)} %pad_maximum_fusion.1), channel_id=1, source_target_pairs={{0,16},{8,120},{16,32},{24,8},{32,48},{40,24},{48,64},{56,40},{64,... | collective-permute-start | bytes 786440 | tf_op jit(solution)/shard_map/ppermute | solution.py:68
  23.4 0.0 all-gather.2.cloned.1.call-update
  23.4 0.8 reshape.339
  24.2 2.5 %collective-permute-done.1 = f32[8,32,256]{2,1,0:T(8,128)S(1)} collective-permute-done((f32[8,32,256]{2,1,0:T(8,128)S(1)}, f32[8,32,256]{2,1,0:T(8,128)S(1)}, u32[]{:S(2)}, u32[]{:S(2)}) %collective-permute-start.1) | collective-permute-done | bytes 262176 | tf_op jit(solution)/shard_map/ppermute | solution.py:68
  26.7 5.0 %collective-permute-start.2 = (f32[8,32,256]{2,1,0:T(8,128)S(1)}, f32[8,32,256]{2,1,0:T(8,128)S(1)}, u32[]{:S(2)}, u32[]{:S(2)}) collective-permute-start(f32[8,32,256]{2,1,0:T(8,128)S(1)} %collective-permute-done.1), channel_id=1, source_target_pairs={{0,16},{8,120},{16,32},{24,8},{32,48},{40,24},{48,64},{56,40},{64,... | collective-permute-start | bytes 786440 | tf_op jit(solution)/shard_map/ppermute | solution.py:68
  31.7 0.1 fusion
  31.8 0.2 convert_reduce_fusion
  32.0 0.1 select_reduce_fusion
  32.1 3.1 %collective-permute-start.6 = (s32[16]{0:T(128)S(1)}, s32[16]{0:T(128)S(1)}, u32[]{:S(2)}, u32[]{:S(2)}) collective-permute-start(s32[16]{0:T(128)S(1)} %select_reduce_fusion), channel_id=1, source_target_pairs={{0,128},{8,136},{16,144},{24,152},{32,160},{40,168},{48,176},{56,1... | collective-permute-start | bytes 200 | tf_op jit(solution)/shard_map/ppermute | solution.py:60
  35.3 4.8 %collective-permute-start.3 = (f32[8,32,256]{2,1,0:T(8,128)S(1)}, f32[8,32,256]{2,1,0:T(8,128)S(1)}, u32[]{:S(2)}, u32[]{:S(2)}) collective-permute-start(f32[8,32,256]{2,1,0:T(8,128)S(1)} %collective-permute-done.2), channel_id=1, source_target_pairs={{0,16},{8,120},{16,32},{24,8},{32,48},{40,24},{48,64},{56,40},{64,... | collective-permute-start | bytes 786440 | tf_op jit(solution)/shard_map/ppermute | solution.py:68
  40.1 0.9 constant_dynamic-update-slice_fusion.6
  41.0 2.3 %collective-permute-done.3 = f32[8,32,256]{2,1,0:T(8,128)S(1)} collective-permute-done((f32[8,32,256]{2,1,0:T(8,128)S(1)}, f32[8,32,256]{2,1,0:T(8,128)S(1)}, u32[]{:S(2)}, u32[]{:S(2)}) %collective-permute-start.3) | collective-permute-done | bytes 262176 | tf_op jit(solution)/shard_map/ppermute | solution.py:68
  43.3 5.2 %collective-permute-start.4 = (f32[4,32,256]{2,1,0:T(8,128)S(1)}, f32[4,32,256]{2,1,0:T(8,128)S(1)}, u32[]{:S(2)}, u32[]{:S(2)}) collective-permute-start(f32[4,32,256]{2,1,0:T(8,128)S(1)} %slice.8), channel_id=1, source_target_pairs={{0,16},{8,120},{16,32},{24,8},{32,48},{40,24},{48,64},{56,40},{64,... | collective-permute-start | bytes 393224 | tf_op jit(solution)/shard_map/ppermute | solution.py:68
  48.5 4.6 %collective-permute-start.7 = (s32[2,16]{1,0:T(2,128)S(1)}, s32[2,16]{1,0:T(2,128)S(1)}, u32[]{:S(2)}, u32[]{:S(2)}) collective-permute-start(s32[2,16]{1,0:T(2,128)S(1)} %pad_add_fusion.1), channel_id=1, source_target_pairs={{0,256},{8,264},{16,272},{24,280},{32,288},{40,296},{48,304},{56,3... | collective-permute-start | bytes 392 | tf_op jit(solution)/shard_map/ppermute | solution.py:61
  53.2 1.2 collective-permute-done.7
  54.4 0.6 gather_fusion
  54.9 1.0 pad_maximum_fusion
  56.0 3.8 %collective-permute-start.5 = (f32[28,32,256]{2,1,0:T(8,128)}, f32[28,32,256]{2,1,0:T(8,128)}, u32[]{:S(2)}, u32[]{:S(2)}) collective-permute-start(f32[28,32,256]{2,1,0:T(8,128)} %pad_maximum_fusion), channel_id=1, source_target_pairs={{0,8},{8,0},{16,24},{24,16},{32,40},{40,32},{48,56},{56,48},{64,72... | collective-permute-start | bytes 2752520 | tf_op jit(solution)/shard_map/ppermute | solution.py:71
  59.8 0.1 reshape.351
  60.0 2.2 %collective-permute-done.5 = f32[28,32,256]{2,1,0:T(8,128)} collective-permute-done((f32[28,32,256]{2,1,0:T(8,128)}, f32[28,32,256]{2,1,0:T(8,128)}, u32[]{:S(2)}, u32[]{:S(2)}) %collective-permute-start.5) | collective-permute-done | bytes 917536 | tf_op jit(solution)/shard_map/ppermute | solution.py:71
  62.2 1.2 %constant_dynamic-update-slice_fusion = f32[64,32,256]{2,1,0:T(8,128)S(1)} fusion(f32[64,32,256]{2,1,0:T(8,128)S(1)} %constant_dynamic-update-slice_fusion.1, f32[28,32,256]{2,1,0:T(8,128)} %collective-permute-done.5), kind=kLoop, calls=%fused_computation.10 | loop fusion | bytes 1835008 | tf_op jit(solution)/shard_map/concatenate | solution.py:71
  63.4 2.0 %gather_fusion.1 = f32[64,32,256]{2,1,0:T(8,128)} fusion(f32[64,32,256]{2,1,0:T(8,128)S(1)} %constant_dynamic-update-slice_fusion, s32[1024]{0:T(1024)S(1)} %pad_clamp_fusion), kind=kCustom, calls=%fused_computation.1 | custom fusion | bytes 4194560 | tf_op jit(solution)/shard_map/gather | solution.py:84
  65.4 4.1 %all-to-all-start = ((f32[4,16,32,256]{3,2,1,0:T(8,128)}), f32[4,16,32,256]{3,2,1,0:T(8,128)S(1)}, u32[]{:S(2)}, u32[]{:S(2)}) async-start(f32[4,16,32,256]{3,2,1,0:T(8,128)} %bitcast.34), calls=%async_computation | async-start | bytes 4194304 | tf_op jit(solution)/shard_map/all_to_all | solution.py:83
  69.6 25.7 %all-to-all-done = f32[4,16,32,256]{3,2,1,0:T(8,128)S(1)} async-done(((f32[4,16,32,256]{3,2,1,0:T(8,128)}), f32[4,16,32,256]{3,2,1,0:T(8,128)S(1)}, u32[]{:S(2)}, u32[]{:S(2)}) %all-to-all-start) | async-done | bytes 2097184 | tf_op jit(solution)/shard_map/all_to_all | solution.py:83
  95.3 1.6 %copy-done.1 = f32[1,8,256,256]{3,2,1,0:T(8,128)S(1)} copy-done((f32[1,8,256,256]{3,2,1,0:T(8,128)S(1)}, f32[1,8,256,256]{3,2,1,0:T(8,128)}, u32[]{:S(2)}) %copy-start.1) | copy-done | bytes 2097176
  96.9 2.3 %shard_map.59 = (f32[8,32,256]{2,1,0:T(8,128)}, f32[8,32,256]{2,1,0:T(8,128)S(1)}) custom-call(s32[64]{0:T(128)S(1)} %multiply_add_fusion.pick_ref, f32[64,32,256]{2,1,0:T(8,128)S(1)} %bitcast.31, f32[8,256,256]{2,1,0:T(8,128)S(1)} %bitcast.33, f32[8,32,256]{2,1,0:T(8,128)S(1)} %bitcast.32), custom_call_target="tpu_custom_call" | custom-call | flops 2000000000 | bytes 5000000 | tf_op jit(solution)/shard_map/pallas_call | solution.py:90
  99.3 16.1 %all_to_all.10 = f32[8,32,256]{2,1,0:T(8,128)S(1)} all-to-all(f32[8,32,256]{2,1,0:T(8,128)S(1)} %get-tuple-element.5), channel_id=1, replica_groups=mesh['snode'=64,'grp'=8] {'grp'}, dimensions={0} | all-to-all | bytes 524288 | tf_op jit(solution)/shard_map/all_to_all | solution.py:101
  115.4 0.6 bitcast_subtract_fusion
  (23 shorter events, 0.2 us)
Async XLA Ops:
  7.2 88.2 %all-gather.2.cloned.1.call-start = ((), (), s32[]{:S(2)}) async-start(), calls=%async_computation.2 | async-start | bytes 2359296 | tf_op jit(solution)/shard_map/all_gather | solution.py:63
  7.2 10.0 %collective-permute-start = (f32[4,32,256]{2,1,0:T(8,128)}, f32[4,32,256]{2,1,0:T(8,128)S(1)}, u32[]{:S(2)}, u32[]{:S(2)}) collective-permute-start(f32[4,32,256]{2,1,0:T(8,128)} %param.4), channel_id=1, source_target_pairs={{0,8},{8,0},{16,24},{24,16},{32,40},{40,32},{48,56},{56,48},{64,72... | collective-permute-start | bytes 393224 | tf_op jit(solution)/shard_map/ppermute | solution.py:65
  18.1 8.6 %collective-permute-start.1 = (f32[8,32,256]{2,1,0:T(8,128)S(1)}, f32[8,32,256]{2,1,0:T(8,128)S(1)}, u32[]{:S(2)}, u32[]{:S(2)}) collective-permute-start(f32[8,32,256]{2,1,0:T(8,128)S(1)} %pad_maximum_fusion.1), channel_id=1, source_target_pairs={{0,16},{8,120},{16,32},{24,8},{32,48},{40,24},{48,64},{56,40},{64,... | collective-permute-start | bytes 786440 | tf_op jit(solution)/shard_map/ppermute | solution.py:68
  26.7 8.6 %collective-permute-start.2 = (f32[8,32,256]{2,1,0:T(8,128)S(1)}, f32[8,32,256]{2,1,0:T(8,128)S(1)}, u32[]{:S(2)}, u32[]{:S(2)}) collective-permute-start(f32[8,32,256]{2,1,0:T(8,128)S(1)} %collective-permute-done.1), channel_id=1, source_target_pairs={{0,16},{8,120},{16,32},{24,8},{32,48},{40,24},{48,64},{56,40},{64,... | collective-permute-start | bytes 786440 | tf_op jit(solution)/shard_map/ppermute | solution.py:68
  32.1 16.4 %collective-permute-start.6 = (s32[16]{0:T(128)S(1)}, s32[16]{0:T(128)S(1)}, u32[]{:S(2)}, u32[]{:S(2)}) collective-permute-start(s32[16]{0:T(128)S(1)} %select_reduce_fusion), channel_id=1, source_target_pairs={{0,128},{8,136},{16,144},{24,152},{32,160},{40,168},{48,176},{56,1... | collective-permute-start | bytes 200 | tf_op jit(solution)/shard_map/ppermute | solution.py:60
  35.3 8.1 %collective-permute-start.3 = (f32[8,32,256]{2,1,0:T(8,128)S(1)}, f32[8,32,256]{2,1,0:T(8,128)S(1)}, u32[]{:S(2)}, u32[]{:S(2)}) collective-permute-start(f32[8,32,256]{2,1,0:T(8,128)S(1)} %collective-permute-done.2), channel_id=1, source_target_pairs={{0,16},{8,120},{16,32},{24,8},{32,48},{40,24},{48,64},{56,40},{64,... | collective-permute-start | bytes 786440 | tf_op jit(solution)/shard_map/ppermute | solution.py:68
  43.3 11.6 %collective-permute-start.4 = (f32[4,32,256]{2,1,0:T(8,128)S(1)}, f32[4,32,256]{2,1,0:T(8,128)S(1)}, u32[]{:S(2)}, u32[]{:S(2)}) collective-permute-start(f32[4,32,256]{2,1,0:T(8,128)S(1)} %slice.8), channel_id=1, source_target_pairs={{0,16},{8,120},{16,32},{24,8},{32,48},{40,24},{48,64},{56,40},{64,... | collective-permute-start | bytes 393224 | tf_op jit(solution)/shard_map/ppermute | solution.py:68
  48.5 5.8 %collective-permute-start.7 = (s32[2,16]{1,0:T(2,128)S(1)}, s32[2,16]{1,0:T(2,128)S(1)}, u32[]{:S(2)}, u32[]{:S(2)}) collective-permute-start(s32[2,16]{1,0:T(2,128)S(1)} %pad_add_fusion.1), channel_id=1, source_target_pairs={{0,256},{8,264},{16,272},{24,280},{32,288},{40,296},{48,304},{56,3... | collective-permute-start | bytes 392 | tf_op jit(solution)/shard_map/ppermute | solution.py:61
  56.0 6.2 %collective-permute-start.5 = (f32[28,32,256]{2,1,0:T(8,128)}, f32[28,32,256]{2,1,0:T(8,128)}, u32[]{:S(2)}, u32[]{:S(2)}) collective-permute-start(f32[28,32,256]{2,1,0:T(8,128)} %pad_maximum_fusion), channel_id=1, source_target_pairs={{0,8},{8,0},{16,24},{24,16},{32,40},{40,32},{48,56},{56,48},{64,72... | collective-permute-start | bytes 2752520 | tf_op jit(solution)/shard_map/ppermute | solution.py:71
  65.4 29.9 %copy-start = (f32[1,8,32,256]{3,2,1,0:T(8,128)S(1)}, f32[1,8,32,256]{3,2,1,0:T(8,128)}, u32[]{:S(2)}) copy-start(f32[1,8,32,256]{3,2,1,0:T(8,128)} %param.5) | copy-start | bytes 786436
  65.4 29.9 %all-to-all-start = ((f32[4,16,32,256]{3,2,1,0:T(8,128)}), f32[4,16,32,256]{3,2,1,0:T(8,128)S(1)}, u32[]{:S(2)}, u32[]{:S(2)}) async-start(f32[4,16,32,256]{3,2,1,0:T(8,128)} %bitcast.34), calls=%async_computation | async-start | bytes 4194304 | tf_op jit(solution)/shard_map/all_to_all | solution.py:83
  95.3 1.6 %copy-start.1 = (f32[1,8,256,256]{3,2,1,0:T(8,128)S(1)}, f32[1,8,256,256]{3,2,1,0:T(8,128)}, u32[]{:S(2)}) copy-start(f32[1,8,256,256]{3,2,1,0:T(8,128)} %all-gather.2.cloned.1.call-done) | copy-start | bytes 6291460
  96.9 18.4 %copy-start.2 = (f32[1,32,256]{2,1,0:T(8,128)S(1)}, f32[1,32,256]{2,1,0:T(8,128)}, u32[]{:S(2)}) copy-start(f32[1,32,256]{2,1,0:T(8,128)} %param.7) | copy-start | bytes 98308
Sparse Core Ops, SparseCore 0:
  23.6 36.9 all-gather.1

commit v2 on v1

v2 whole, which is shorter than its diff:
```python
import jax
import jax.numpy as jnp
from jax import lax
from jax.experimental import pallas as pl
from jax.experimental.pallas import tpu as pltpu
from jax.sharding import PartitionSpec as P

NX, NZ, NC, NY = 4, 8, 2, 8
SLOTS = 16
HALF = 4


def node(x, z, c):
    return ((x % NX) * NZ + z % NZ) * NC + c


EVERY = [(x, z, c) for x in range(NX) for z in range(NZ) for c in range(NC)]
TWIN = [(node(x, z, c), node(x, z, 1 - c)) for x, z, c in EVERY]
Z_ROUND = [(node(x, z, c), node(x, z + 1 - 2 * c, c)) for x, z, c in EVERY]
Y_ROUND = [
    (node(x, z, c) * NY + y, node(x, z, c) * NY + (y + 1 - 2 * c) % NY) for x, z, c in EVERY for y in range(NY)
]
X_ONE = [(node(x, z, c), node(x ^ 1, z, c)) for x, z, c in EVERY]
X_TWO = [(node(x, z, c), node(x ^ 2, z, c)) for x, z, c in EVERY]
X_LINES = [[node(x, z, c) for x in range(NX)] for z in range(NZ) for c in range(NC)]
VMEM = pl.BlockSpec(memory_space=pltpu.VMEM)
SMEM = pl.BlockSpec(memory_space=pltpu.SMEM)
PARAMS = pltpu.CompilerParams(vmem_limit_bytes=32 * 1024 * 1024)


def split(v):
    high = v.astype(jnp.bfloat16)
    return high, (v - high.astype(jnp.float32)).astype(jnp.bfloat16)


def dot3(a, b, dims):
    (ah, al), (bh, bl) = a, b
    dot = lambda u, v: lax.dot_general(u, v, (dims, ((), ())), preferred_element_type=jnp.float32)
    return dot(ah, bh) + (dot(ah, bl) + dot(al, bh))


def collect(place_ref, *refs):
    *pieces, answers_ref, pool_ref = refs
    at = 0
    for piece in pieces:
        count = piece.shape[0]
        pool_ref[at : at + count] = piece[...]
        at += count

    def one(s, carry):
        answers_ref[s] = pool_ref[place_ref[s]]
        return carry

    lax.fori_loop(0, answers_ref.shape[0], one, 0, unroll=4)


def assemble(rows_ref, own_ref, first_ref, *refs):
    *rest, high_ref, low_ref = refs
    leads, lags = rest[: HALF - 1], rest[HALF - 1 :]
    count, rows, _ = own_ref.shape
    pieces = [own_ref, first_ref] + [ref.at[pl.ds(0, count)] for ref in leads] + list(lags)
    for number, piece in enumerate(pieces):
        start = pl.multiple_of(rows_ref[number], rows)
        high, low = split(piece[...])
        high_ref[:, pl.ds(start, rows), :] = high
        low_ref[:, pl.ds(start, rows), :] = low


def products(pick_ref, fetched_ref, high_ref, low_ref, own_ref, off_ref, update_ref):
    kcount, rows, width = own_ref.shape
    total = jnp.zeros((kcount * rows, width), jnp.float32)
    for b in range(kcount):
        left = jnp.concatenate([fetched_ref[pick_ref[a * kcount + b]] for a in range(kcount)], axis=0)
        total += dot3(split(left), (high_ref[b], low_ref[b]), ((1,), (0,)))
    off = -total
    off_ref[...] = off.reshape(off_ref.shape)
    own = own_ref[...].reshape(kcount * rows, width)
    update_ref[...] = dot3(split(own), split(off), ((0,), (0,))).reshape(update_ref.shape)


def per_device(ancestor_inverse, panel, need_list, diag_factor):
    _, kcount, rows, width = panel.shape
    held = ancestor_inverse.shape[0]
    here, y = lax.axis_index("snode"), lax.axis_index("grp")
    x, z, c = here // (NZ * NC), here // NC % NZ, here % NC
    own = panel[0]
    twin = lambda v: lax.ppermute(v, "snode", TWIN)
    z_on = lambda v: lax.ppermute(v, "snode", Z_ROUND)
    y_on = lambda v: lax.ppermute(v, ("snode", "grp"), Y_ROUND)

    other = twin(ancestor_inverse)
    ring = [z_on(ancestor_inverse)]
    message = jnp.concatenate([ring[0], other])
    for _ in range(HALF - 1):
        message = z_on(message)
        ring.append(message)
    pieces = [ancestor_inverse, other] + ring + [twin(piece) for piece in ring]

    lead = y_on(own)
    message = jnp.concatenate([lead, twin(own)])
    both = []
    for _ in range(HALF - 1):
        message = y_on(message)
        both.append(message)
    lags = [twin(message[kcount:]) for message in both]

    wanted = need_list.reshape(-1)
    ids = jnp.arange(NX * NZ * NC * held, dtype=jnp.int32)
    present = jnp.any(wanted[:, None] == ids[None, :], axis=0)
    slot = jnp.sum((present[None, :] & (ids[None, :] < wanted[:, None])).astype(jnp.int32), axis=1)
    order = jnp.arange(SLOTS, dtype=jnp.int32)
    distinct = jnp.max(jnp.where(slot[None, :] == order[:, None], wanted[None, :], 0), axis=1)
    pair = jnp.stack([distinct, lax.ppermute(distinct, "snode", X_ONE)])
    lists = jnp.concatenate([pair, lax.ppermute(pair, "snode", X_TWO)])

    asked = lists[jnp.arange(NX) ^ x]
    owner, k = asked // held, asked % held
    oz, oc = owner // NC % NZ, owner % NC
    dz = (oz - z) % NZ
    holder = jnp.where(dz == HALF, oc, (dz < HALF).astype(jnp.int32))
    far = jnp.where(dz < HALF, dz, NZ - dz)
    lag = (oc != holder).astype(jnp.int32)
    arrived = far + lag
    inside = jnp.where(arrived == 1, 0, held + (arrived - 2) * 2 * held + lag * held) + k
    count = held + (HALF - 1) * 2 * held
    start = 2 * held + jnp.where(holder == c, 0, count)
    place = jnp.where(dz == 0, (oc ^ c) * held + k, start + inside)
    place = jnp.where(owner // (NC * NZ) == x, place, 0)

    block = (rows, width)
    answers = pl.pallas_call(
        collect,
        out_shape=jax.ShapeDtypeStruct((NX * SLOTS,) + block, jnp.float32),
        in_specs=[SMEM] + [VMEM] * len(pieces),
        out_specs=VMEM,
        scratch_shapes=[pltpu.VMEM((2 * held + 2 * count,) + block, jnp.float32)],
        compiler_params=PARAMS,
        cost_estimate=pl.CostEstimate(flops=0, bytes_accessed=4_000_000, transcendentals=0),
    )(place.reshape(-1), *pieces)
    fetched = lax.all_to_all(
        answers.reshape((NX, SLOTS) + block), "snode", split_axis=0, concat_axis=0, tiled=True, axis_index_groups=X_LINES
    ).reshape((NX * SLOTS,) + block)

    way = 2 * c - 1
    steps = jnp.array([0, 1, 2, 3, 4, -1, -2, -3], jnp.int32)
    high, low = pl.pallas_call(
        assemble,
        out_shape=(jax.ShapeDtypeStruct((kcount, NY * rows, width), jnp.bfloat16),) * 2,
        in_specs=[SMEM] + [VMEM] * (2 + len(both) + len(lags)),
        out_specs=(VMEM, VMEM),
        compiler_params=PARAMS,
        cost_estimate=pl.CostEstimate(flops=0, bytes_accessed=4_000_000, transcendentals=0),
    )((y + way * steps) % NY * rows, own, lead, *both, *lags)

    pick = wanted // (held * NC * NZ) * SLOTS + slot
    off, update = pl.pallas_call(
        products,
        out_shape=(
            jax.ShapeDtypeStruct((kcount,) + block, jnp.float32),
            jax.ShapeDtypeStruct((NY,) + block, jnp.float32),
        ),
        in_specs=[SMEM] + [VMEM] * 4,
        out_specs=(VMEM, VMEM),
        compiler_params=PARAMS,
        cost_estimate=pl.CostEstimate(flops=1_000_000_000, bytes_accessed=5_000_000, transcendentals=0),
    )(pick, fetched, high, low, own)
    parts = lax.all_to_all(update, "grp", split_axis=0, concat_axis=0, tiled=True)
    return off[None], diag_factor - jnp.sum(parts, axis=0)[None]


def solution(mesh):
    return jax.shard_map(
        per_device,
        mesh=mesh,
        in_specs=(
            P("snode", "grp", None),
            P("snode", None, "grp", None),
            P("snode", None, None),
            P("snode", "grp", None),
        ),
        out_specs=(P("snode", None, "grp", None), P("snode", "grp", None)),
        check_vma=False,
    )
```

time: 124 us -> 121 us (0.976)
  starting transfers between devices: 44.7 us -> 72.1 us
  waiting for transfers between devices: 35.1 us -> 13.1 us
  between operations: 14.3 us -> 1.05 us
  Pallas kernels: 2.34 us -> 5.93 us
  other arithmetic: 3.07 us -> 1.2 us
  local copies, waits for them, and re-layouts: 7.25 us -> 8.68 us
  blocking collectives: 16.1 us -> 17.4 us
    ppermute x6 -> x17, starting transfers between devices: 32.8 us -> 60.6 us  [the longest x9 21.4 us: per_device(): twin = lambda v: lax.ppermute(v, 'snode', TWIN)]
    all_to_all x1, waiting for transfers between devices: 25.7 us -> 0.01 us  [per_device(): lax.all_to_all(answers.reshape((NX, SLOTS) + block), 'snode', split_axis=...]
    ppermute x6 -> x17, waiting for transfers between devices: 8.16 us -> 13.1 us  [the longest x4 7.81 us: per_device(): y_on = lambda v: lax.ppermute(v, ('snode', 'grp'), Y_ROUND)]
    unnamed x12 -> x20, local copies, waits for them, and re-layouts: 2.6 us -> 6.26 us
    pallas_call x1 -> x3, Pallas kernels: 2.34 us -> 5.93 us  [the longest x1 2.33 us: per_device(): pl.pallas_call(products, out_shape=(jax.ShapeDtypeStruct((kcount,) + bloc...]
    gather x1 -> x0, local copies, waits for them, and re-layouts: 1.98 us -> none  [per_device(): pool[place]]
    concatenate x2, other arithmetic: 1.94 us -> 0.06 us  [the longest x1 0.04 us: per_device(): message = jnp.concatenate([lead, twin(own)])]
    all_to_all x1, blocking collectives: 16.1 us -> 17.4 us  [per_device(): lax.all_to_all(update, 'grp', split_axis=0, concat_axis=0, tiled=True)]
  transfers between devices with their start and end apart: 10 -> 20, of which waited for: 6 -> 7; matrix products, arithmetic and copies ran while one was open for 6% -> 2% of each run, Pallas kernels for 0% -> 3%
where the time goes in v2:
time: 121 us; the launch traced here: 119 us
  starting transfers between devices  72.1 us (60%)
  blocking collectives  17.4 us (14%)
  waiting for transfers between devices  13.1 us (11%)
  local copies, waits for them, and re-layouts  8.68 us (7%)
  Pallas kernels  5.93 us (5%)
    ppermute x9, starting transfers between devices, per_device(): twin = lambda v: lax.ppermute(v, 'snode', TWIN)  21.4 us
    ppermute x4, starting transfers between devices, per_device(): z_on = lambda v: lax.ppermute(v, 'snode', Z_ROUND)  20.5 us
    ppermute x4, starting transfers between devices, per_device(): y_on = lambda v: lax.ppermute(v, ('snode', 'grp'), Y_ROUND)  18.7 us
    all_to_all x1, blocking collectives, per_device(): lax.all_to_all(update, 'grp', split_axis=0, concat_axis=0, tiled=True)  17.4 us
    ppermute x4, waiting for transfers between devices, per_device(): y_on = lambda v: lax.ppermute(v, ('snode', 'grp'), Y_ROUND)  7.81 us
    unnamed x20, local copies, waits for them, and re-layouts  6.26 us
    ppermute x1, starting transfers between devices, per_device(): lists = jnp.concatenate([pair, lax.ppermute(pair, 'snode', X_TWO)])  4.65 us
    all_to_all x1, starting transfers between devices, per_device(): lax.all_to_all(answers.reshape((NX, SLOTS) + block), 'snode', split_axis=...  3.74 us
  transfers between devices with their start and end apart: 20, of which 7 were waited for; matrix products, arithmetic and copies ran while one was open for 2% of the time, Pallas kernels for 3%

profile of v2, /device:TPU:1, one launch (start us, length us, event | category | flops | bytes accessed | tf_op | source)
XLA Modules:
  0.0 119.5 jit_solution(12984199153900387019)
XLA Ops:
  0.6 11.5 %collective-permute-start.3 = (f32[4,32,256]{2,1,0:T(8,128)}, f32[4,32,256]{2,1,0:T(8,128)S(1)}, u32[]{:S(2)}, u32[]{:S(2)}) collective-permute-start(f32[4,32,256]{2,1,0:T(8,128)} %refs_0_.1), channel_id=1, source_target_pairs={{0,16},{8,120},{16,32},{24,8},{32,48},{40,24},{48,64},{56,40},{64,... | collective-permute-start | bytes 393224 | tf_op jit(solution)/shard_map/ppermute | solution.py:88
  12.1 1.9 %collective-permute-start.2 = (f32[4,32,256]{2,1,0:T(8,128)}, f32[4,32,256]{2,1,0:T(8,128)S(1)}, u32[]{:S(2)}, u32[]{:S(2)}) collective-permute-start(f32[4,32,256]{2,1,0:T(8,128)} %refs_0_.1), channel_id=1, source_target_pairs={{0,8},{8,0},{16,24},{24,16},{32,40},{40,32},{48,56},{56,48},{64,72... | collective-permute-start | bytes 393224 | tf_op jit(solution)/shard_map/ppermute | solution.py:87
  14.4 1.2 %collective-permute-done.2.refs_1_ = f32[4,32,256]{2,1,0:T(8,128)S(1)} collective-permute-done((f32[4,32,256]{2,1,0:T(8,128)}, f32[4,32,256]{2,1,0:T(8,128)S(1)}, u32[]{:S(2)}, u32[]{:S(2)}) %collective-permute-start.2) | collective-permute-done | bytes 131104 | tf_op jit(solution)/shard_map/ppermute | solution.py:87
  15.6 3.7 %collective-permute-start.4 = (f32[8,32,256]{2,1,0:T(8,128)S(1)}, f32[8,32,256]{2,1,0:T(8,128)S(1)}, u32[]{:S(2)}, u32[]{:S(2)}) collective-permute-start(f32[8,32,256]{2,1,0:T(8,128)S(1)} %pad_maximum_fusion.1), channel_id=1, source_target_pairs={{0,16},{8,120},{16,32},{24,8},{32,48},{40,24},{48,64},{56,40},{64,... | collective-permute-start | bytes 786440 | tf_op jit(solution)/shard_map/ppermute | solution.py:88
  19.3 5.1 %collective-permute-start.11 = (f32[8,32,256]{2,1,0:T(8,128)}, f32[8,32,256]{2,1,0:T(8,128)S(1)}, u32[]{:S(2)}, u32[]{:S(2)}) collective-permute-start(f32[8,32,256]{2,1,0:T(8,128)} %bitcast.11), channel_id=1, source_target_pairs={{0,1},{1,2},{2,3},{3,4},{4,5},{5,6},{6,7},{7,0},{8,15},{9,8},{10,9... | collective-permute-start | bytes 786440 | tf_op jit(solution)/shard_map/ppermute | solution.py:89
  24.4 1.9 %collective-permute-start.12 = (f32[8,32,256]{2,1,0:T(8,128)}, f32[8,32,256]{2,1,0:T(8,128)S(1)}, u32[]{:S(2)}, u32[]{:S(2)}) collective-permute-start(f32[8,32,256]{2,1,0:T(8,128)} %bitcast.12), channel_id=1, source_target_pairs={{0,8},{8,0},{16,24},{24,16},{32,40},{40,32},{48,56},{56,48},{64,72... | collective-permute-start | bytes 786440 | tf_op jit(solution)/shard_map/ppermute | solution.py:87
  27.2 2.2 %collective-permute-start.5 = (f32[8,32,256]{2,1,0:T(8,128)S(1)}, f32[8,32,256]{2,1,0:T(8,128)S(1)}, u32[]{:S(2)}, u32[]{:S(2)}) collective-permute-start(f32[8,32,256]{2,1,0:T(8,128)S(1)} %collective-permute-done.4.refs_3_), channel_id=1, source_target_pairs={{0,16},{8,120},{16,32},{24,8},{32,48},{40,24},{48,64},{56,40},{64,... | collective-permute-start | bytes 786440 | tf_op jit(solution)/shard_map/ppermute | solution.py:88
  29.7 3.1 %collective-permute-start = (s32[16]{0:T(128)S(1)}, s32[16]{0:T(128)S(1)}, u32[]{:S(2)}, u32[]{:S(2)}) collective-permute-start(s32[16]{0:T(128)S(1)} %select_reduce_fusion), channel_id=1, source_target_pairs={{0,128},{8,136},{16,144},{24,152},{32,160},{40,168},{48,176},{56,1... | collective-permute-start | bytes 200 | tf_op jit(solution)/shard_map/ppermute | solution.py:113
  32.9 1.7 %collective-permute-done.5.refs_4_ = f32[8,32,256]{2,1,0:T(8,128)S(1)} collective-permute-done((f32[8,32,256]{2,1,0:T(8,128)S(1)}, f32[8,32,256]{2,1,0:T(8,128)S(1)}, u32[]{:S(2)}, u32[]{:S(2)}) %collective-permute-start.5) | collective-permute-done | bytes 262176 | tf_op jit(solution)/shard_map/ppermute | solution.py:88
  34.6 3.1 %collective-permute-start.6 = (f32[8,32,256]{2,1,0:T(8,128)S(1)}, f32[8,32,256]{2,1,0:T(8,128)S(1)}, u32[]{:S(2)}, u32[]{:S(2)}) collective-permute-start(f32[8,32,256]{2,1,0:T(8,128)S(1)} %collective-permute-done.5.refs_4_), channel_id=1, source_target_pairs={{0,16},{8,120},{16,32},{24,8},{32,48},{40,24},{48,64},{56,40},{64,... | collective-permute-start | bytes 786440 | tf_op jit(solution)/shard_map/ppermute | solution.py:88
  37.9 3.5 %collective-permute-start.13 = (f32[16,32,256]{2,1,0:T(8,128)S(1)}, f32[16,32,256]{2,1,0:T(8,128)S(1)}, u32[]{:S(2)}, u32[]{:S(2)}) collective-permute-start(f32[16,32,256]{2,1,0:T(8,128)S(1)} %pad_maximum_fusion), channel_id=1, source_target_pairs={{0,1},{1,2},{2,3},{3,4},{4,5},{5,6},{6,7},{7,0},{8,15},{9,8},{10,9... | collective-permute-start | bytes 1572872 | tf_op jit(solution)/shard_map/ppermute | solution.py:89
  41.4 4.7 %collective-permute-start.1 = (s32[2,16]{1,0:T(2,128)S(1)}, s32[2,16]{1,0:T(2,128)S(1)}, u32[]{:S(2)}, u32[]{:S(2)}) collective-permute-start(s32[2,16]{1,0:T(2,128)S(1)} %pad_add_fusion.1), channel_id=1, source_target_pairs={{0,256},{8,264},{16,272},{24,280},{32,288},{40,296},{48,304},{56,3... | collective-permute-start | bytes 392 | tf_op jit(solution)/shard_map/ppermute | solution.py:114
  46.0 2.0 %collective-permute-start.8 = (f32[8,32,256]{2,1,0:T(8,128)S(1)}, f32[8,32,256]{2,1,0:T(8,128)S(1)}, u32[]{:S(2)}, u32[]{:S(2)}) collective-permute-start(f32[8,32,256]{2,1,0:T(8,128)S(1)} %collective-permute-done.4.refs_3_), channel_id=1, source_target_pairs={{0,8},{8,0},{16,24},{24,16},{32,40},{40,32},{48,56},{56,48},{64,72... | collective-permute-start | bytes 786440 | tf_op jit(solution)/shard_map/ppermute | solution.py:87
  48.0 2.3 %collective-permute-start.9 = (f32[8,32,256]{2,1,0:T(8,128)S(1)}, f32[8,32,256]{2,1,0:T(8,128)S(1)}, u32[]{:S(2)}, u32[]{:S(2)}) collective-permute-start(f32[8,32,256]{2,1,0:T(8,128)S(1)} %collective-permute-done.5.refs_4_), channel_id=1, source_target_pairs={{0,8},{8,0},{16,24},{24,16},{32,40},{40,32},{48,56},{56,48},{64,72... | collective-permute-start | bytes 786440 | tf_op jit(solution)/shard_map/ppermute | solution.py:87
  50.4 2.0 %collective-permute-start.10 = (f32[8,32,256]{2,1,0:T(8,128)S(1)}, f32[8,32,256]{2,1,0:T(8,128)S(1)}, u32[]{:S(2)}, u32[]{:S(2)}) collective-permute-start(f32[8,32,256]{2,1,0:T(8,128)S(1)} %collective-permute-done.6.refs_5_), channel_id=1, source_target_pairs={{0,8},{8,0},{16,24},{24,16},{32,40},{40,32},{48,56},{56,48},{64,72... | collective-permute-start | bytes 786440 | tf_op jit(solution)/shard_map/ppermute | solution.py:87
  53.1 2.3 %collective-permute-start.7 = (f32[4,32,256]{2,1,0:T(8,128)S(1)}, f32[4,32,256]{2,1,0:T(8,128)S(1)}, u32[]{:S(2)}, u32[]{:S(2)}) collective-permute-start(f32[4,32,256]{2,1,0:T(8,128)S(1)} %collective-permute-done.3.refs_2_), channel_id=1, source_target_pairs={{0,8},{8,0},{16,24},{24,16},{32,40},{40,32},{48,56},{56,48},{64,72... | collective-permute-start | bytes 393224 | tf_op jit(solution)/shard_map/ppermute | solution.py:87
  57.3 2.2 %shard_map.68 = f32[64,32,256]{2,1,0:T(8,128)} custom-call(s32[64]{0:T(128)S(1)} %compare_select_fusion.12.place_ref, f32[4,32,256]{2,1,0:T(8,128)S(1)} %copy-done.7, f32[4,32,256]{2,1,0:T(8,128)S(1)} %collective-permute-done.2.refs_1_, f32[4,32,256]{2,1,0:T(8,128)S(1)} %collective-permute-done.3.refs_2_, f32[8,32,256]{2,1,0:T(8,128)S(1)} %collective-permute-done.4.refs_3_, ...), custom_call_target="tpu_custom_call" | custom-call | bytes 4000000 | tf_op jit(solution)/shard_map/pallas_call | solution.py:131
  59.5 3.7 %all-to-all-start = ((f32[4,16,32,256]{3,2,1,0:T(8,128)}), f32[4,16,32,256]{3,2,1,0:T(8,128)S(1)}, u32[]{:S(2)}, u32[]{:S(2)}) async-start(f32[4,16,32,256]{3,2,1,0:T(8,128)} %bitcast.3), calls=%async_computation | async-start | bytes 4194304 | tf_op jit(solution)/shard_map/all_to_all | solution.py:140
  63.2 4.8 %collective-permute-start.14 = (f32[16,32,256]{2,1,0:T(8,128)S(1)}, f32[16,32,256]{2,1,0:T(8,128)S(1)}, u32[]{:S(2)}, u32[]{:S(2)}) collective-permute-start(f32[16,32,256]{2,1,0:T(8,128)S(1)} %collective-permute-done.13.refs_0_), channel_id=1, source_target_pairs={{0,1},{1,2},{2,3},{3,4},{4,5},{5,6},{6,7},{7,0},{8,15},{9,8},{10,9... | collective-permute-start | bytes 1572872 | tf_op jit(solution)/shard_map/ppermute | solution.py:89
  68.1 6.1 %collective-permute-done.14.refs_1_ = f32[16,32,256]{2,1,0:T(8,128)S(1)} collective-permute-done((f32[16,32,256]{2,1,0:T(8,128)S(1)}, f32[16,32,256]{2,1,0:T(8,128)S(1)}, u32[]{:S(2)}, u32[]{:S(2)}) %collective-permute-start.14) | collective-permute-done | bytes 524320 | tf_op jit(solution)/shard_map/ppermute | solution.py:89
  74.2 5.3 %collective-permute-start.15 = (f32[16,32,256]{2,1,0:T(8,128)S(1)}, f32[16,32,256]{2,1,0:T(8,128)}, u32[]{:S(2)}, u32[]{:S(2)}) collective-permute-start(f32[16,32,256]{2,1,0:T(8,128)S(1)} %collective-permute-done.14.refs_1_), channel_id=1, source_target_pairs={{0,1},{1,2},{2,3},{3,4},{4,5},{5,6},{6,7},{7,0},{8,15},{9,8},{10,9... | collective-permute-start | bytes 1572872 | tf_op jit(solution)/shard_map/ppermute | solution.py:89
  79.5 1.9 %collective-permute-start.16 = (f32[8,32,256]{2,1,0:T(8,128)S(1)}, f32[8,32,256]{2,1,0:T(8,128)S(1)}, u32[]{:S(2)}, u32[]{:S(2)}) collective-permute-start(f32[8,32,256]{2,1,0:T(8,128)S(1)} %slice.14), channel_id=1, source_target_pairs={{0,8},{8,0},{16,24},{24,16},{32,40},{40,32},{48,56},{56,48},{64,72... | collective-permute-start | bytes 786440 | tf_op jit(solution)/shard_map/ppermute | solution.py:87
  81.5 2.4 %collective-permute-start.17 = (f32[8,32,256]{2,1,0:T(8,128)S(1)}, f32[8,32,256]{2,1,0:T(8,128)S(1)}, u32[]{:S(2)}, u32[]{:S(2)}) collective-permute-start(f32[8,32,256]{2,1,0:T(8,128)S(1)} %slice.15), channel_id=1, source_target_pairs={{0,8},{8,0},{16,24},{24,16},{32,40},{40,32},{48,56},{56,48},{64,72... | collective-permute-start | bytes 786440 | tf_op jit(solution)/shard_map/ppermute | solution.py:87
  83.9 1.7 %collective-permute-done.15.refs_2_ = f32[16,32,256]{2,1,0:T(8,128)} collective-permute-done((f32[16,32,256]{2,1,0:T(8,128)S(1)}, f32[16,32,256]{2,1,0:T(8,128)}, u32[]{:S(2)}, u32[]{:S(2)}) %collective-permute-start.15) | collective-permute-done | bytes 524320 | tf_op jit(solution)/shard_map/ppermute | solution.py:89
  86.6 4.6 %collective-permute-start.18 = (f32[8,32,256]{2,1,0:T(8,128)S(1)}, f32[8,32,256]{2,1,0:T(8,128)S(1)}, u32[]{:S(2)}, u32[]{:S(2)}) collective-permute-start(f32[8,32,256]{2,1,0:T(8,128)S(1)} %slice.16), channel_id=1, source_target_pairs={{0,8},{8,0},{16,24},{24,16},{32,40},{40,32},{48,56},{56,48},{64,72... | collective-permute-start | bytes 786440 | tf_op jit(solution)/shard_map/ppermute | solution.py:87
  91.2 1.1 collective-permute-done.18.refs_5_
  93.3 1.4 %shard_map.69 = (bf16[8,256,256]{2,1,0:T(8,128)(2,1)S(1)}, bf16[8,256,256]{2,1,0:T(8,128)(2,1)S(1)}) custom-call(s32[8]{0:T(128)S(1)} %fusion.7.rows_ref, f32[8,32,256]{2,1,0:T(8,128)S(1)} %bitcast.13, f32[8,32,256]{2,1,0:T(8,128)S(1)} %copy-done.6, f32[16,32,256]{2,1,0:T(8,128)S(1)} %collective-permute-done.13.refs_0_, ...), custom_call_target="tpu_custom_call" | custom-call | bytes 4000000 | tf_op jit(solution)/shard_map/pallas_call | solution.py:146
  95.6 1.0 copy-done.2
  96.6 1.2 %copy-done.1 = bf16[8,256,256]{2,1,0:T(8,128)(2,1)S(1)} copy-done((bf16[8,256,256]{2,1,0:T(8,128)(2,1)S(1)}, bf16[8,256,256]{2,1,0:T(8,128)(2,1)}, u32[]{:S(2)}) %copy-start.1) | copy-done | bytes 1048600
  97.8 1.2 %copy-done.3 = bf16[8,256,256]{2,1,0:T(8,128)(2,1)S(1)} copy-done((bf16[8,256,256]{2,1,0:T(8,128)(2,1)S(1)}, bf16[8,256,256]{2,1,0:T(8,128)(2,1)}, u32[]{:S(2)}) %copy-start.3) | copy-done | bytes 1048600
  99.0 2.3 %shard_map.70 = (f32[8,32,256]{2,1,0:T(8,128)}, f32[8,32,256]{2,1,0:T(8,128)S(1)}) custom-call(s32[64]{0:T(128)S(1)} %multiply_add_fusion.pick_ref, f32[64,32,256]{2,1,0:T(8,128)S(1)} %bitcast.10, bf16[8,256,256]{2,1,0:T(8,128)(2,1)S(1)} %copy-done.1, bf16[8,256,256]{2,1,0:T(8,128)(2,1)S(1)} %copy-done.3, f32[8,32,256]{2,1,0:T(8,128)S(1)} %bitcast.14), custom_call_target="tpu_custom_call" | custom-call | flops 1000000000 | bytes 5000000 | tf_op jit(solution)/shard_map/pallas_call | solution.py:156
  101.4 17.4 %all_to_all.10 = f32[8,32,256]{2,1,0:T(8,128)S(1)} all-to-all(f32[8,32,256]{2,1,0:T(8,128)S(1)} %get-tuple-element.9), channel_id=1, replica_groups=mesh['snode'=64,'grp'=8] {'grp'}, dimensions={0} | all-to-all | bytes 524288 | tf_op jit(solution)/shard_map/all_to_all | solution.py:167
  (52 shorter events, 7.7 us)
Async XLA Ops:
  0.6 13.7 %collective-permute-start.3 = (f32[4,32,256]{2,1,0:T(8,128)}, f32[4,32,256]{2,1,0:T(8,128)S(1)}, u32[]{:S(2)}, u32[]{:S(2)}) collective-permute-start(f32[4,32,256]{2,1,0:T(8,128)} %refs_0_.1), channel_id=1, source_target_pairs={{0,16},{8,120},{16,32},{24,8},{32,48},{40,24},{48,64},{56,40},{64,... | collective-permute-start | bytes 393224 | tf_op jit(solution)/shard_map/ppermute | solution.py:88
  12.1 3.5 %collective-permute-start.2 = (f32[4,32,256]{2,1,0:T(8,128)}, f32[4,32,256]{2,1,0:T(8,128)S(1)}, u32[]{:S(2)}, u32[]{:S(2)}) collective-permute-start(f32[4,32,256]{2,1,0:T(8,128)} %refs_0_.1), channel_id=1, source_target_pairs={{0,8},{8,0},{16,24},{24,16},{32,40},{40,32},{48,56},{56,48},{64,72... | collective-permute-start | bytes 393224 | tf_op jit(solution)/shard_map/ppermute | solution.py:87
  15.6 11.6 %collective-permute-start.4 = (f32[8,32,256]{2,1,0:T(8,128)S(1)}, f32[8,32,256]{2,1,0:T(8,128)S(1)}, u32[]{:S(2)}, u32[]{:S(2)}) collective-permute-start(f32[8,32,256]{2,1,0:T(8,128)S(1)} %pad_maximum_fusion.1), channel_id=1, source_target_pairs={{0,16},{8,120},{16,32},{24,8},{32,48},{40,24},{48,64},{56,40},{64,... | collective-permute-start | bytes 786440 | tf_op jit(solution)/shard_map/ppermute | solution.py:88
  19.3 18.5 %collective-permute-start.11 = (f32[8,32,256]{2,1,0:T(8,128)}, f32[8,32,256]{2,1,0:T(8,128)S(1)}, u32[]{:S(2)}, u32[]{:S(2)}) collective-permute-start(f32[8,32,256]{2,1,0:T(8,128)} %bitcast.11), channel_id=1, source_target_pairs={{0,1},{1,2},{2,3},{3,4},{4,5},{5,6},{6,7},{7,0},{8,15},{9,8},{10,9... | collective-permute-start | bytes 786440 | tf_op jit(solution)/shard_map/ppermute | solution.py:89
  24.4 13.4 %collective-permute-start.12 = (f32[8,32,256]{2,1,0:T(8,128)}, f32[8,32,256]{2,1,0:T(8,128)S(1)}, u32[]{:S(2)}, u32[]{:S(2)}) collective-permute-start(f32[8,32,256]{2,1,0:T(8,128)} %bitcast.12), channel_id=1, source_target_pairs={{0,8},{8,0},{16,24},{24,16},{32,40},{40,32},{48,56},{56,48},{64,72... | collective-permute-start | bytes 786440 | tf_op jit(solution)/shard_map/ppermute | solution.py:87
  27.2 7.4 %collective-permute-start.5 = (f32[8,32,256]{2,1,0:T(8,128)S(1)}, f32[8,32,256]{2,1,0:T(8,128)S(1)}, u32[]{:S(2)}, u32[]{:S(2)}) collective-permute-start(f32[8,32,256]{2,1,0:T(8,128)S(1)} %collective-permute-done.4.refs_3_), channel_id=1, source_target_pairs={{0,16},{8,120},{16,32},{24,8},{32,48},{40,24},{48,64},{56,40},{64,... | collective-permute-start | bytes 786440 | tf_op jit(solution)/shard_map/ppermute | solution.py:88
  29.7 11.6 %collective-permute-start = (s32[16]{0:T(128)S(1)}, s32[16]{0:T(128)S(1)}, u32[]{:S(2)}, u32[]{:S(2)}) collective-permute-start(s32[16]{0:T(128)S(1)} %select_reduce_fusion), channel_id=1, source_target_pairs={{0,128},{8,136},{16,144},{24,152},{32,160},{40,168},{48,176},{56,1... | collective-permute-start | bytes 200 | tf_op jit(solution)/shard_map/ppermute | solution.py:113
  34.6 15.7 %collective-permute-start.6 = (f32[8,32,256]{2,1,0:T(8,128)S(1)}, f32[8,32,256]{2,1,0:T(8,128)S(1)}, u32[]{:S(2)}, u32[]{:S(2)}) collective-permute-start(f32[8,32,256]{2,1,0:T(8,128)S(1)} %collective-permute-done.5.refs_4_), channel_id=1, source_target_pairs={{0,16},{8,120},{16,32},{24,8},{32,48},{40,24},{48,64},{56,40},{64,... | collective-permute-start | bytes 786440 | tf_op jit(solution)/shard_map/ppermute | solution.py:88
  37.8 21.7 %copy-start.5 = (f32[8,32,256]{2,1,0:T(8,128)}, f32[8,32,256]{2,1,0:T(8,128)S(1)}, u32[]{:S(2)}) copy-start(f32[8,32,256]{2,1,0:T(8,128)S(1)} %collective-permute-done.11.first_ref) | copy-start | bytes 786436
  37.9 25.4 %collective-permute-start.13 = (f32[16,32,256]{2,1,0:T(8,128)S(1)}, f32[16,32,256]{2,1,0:T(8,128)S(1)}, u32[]{:S(2)}, u32[]{:S(2)}) collective-permute-start(f32[16,32,256]{2,1,0:T(8,128)S(1)} %pad_maximum_fusion), channel_id=1, source_target_pairs={{0,1},{1,2},{2,3},{3,4},{4,5},{5,6},{6,7},{7,0},{8,15},{9,8},{10,9... | collective-permute-start | bytes 1572872 | tf_op jit(solution)/shard_map/ppermute | solution.py:89
  41.4 11.0 %collective-permute-start.1 = (s32[2,16]{1,0:T(2,128)S(1)}, s32[2,16]{1,0:T(2,128)S(1)}, u32[]{:S(2)}, u32[]{:S(2)}) collective-permute-start(s32[2,16]{1,0:T(2,128)S(1)} %pad_add_fusion.1), channel_id=1, source_target_pairs={{0,256},{8,264},{16,272},{24,280},{32,288},{40,296},{48,304},{56,3... | collective-permute-start | bytes 392 | tf_op jit(solution)/shard_map/ppermute | solution.py:114
  46.0 10.3 %collective-permute-start.8 = (f32[8,32,256]{2,1,0:T(8,128)S(1)}, f32[8,32,256]{2,1,0:T(8,128)S(1)}, u32[]{:S(2)}, u32[]{:S(2)}) collective-permute-start(f32[8,32,256]{2,1,0:T(8,128)S(1)} %collective-permute-done.4.refs_3_), channel_id=1, source_target_pairs={{0,8},{8,0},{16,24},{24,16},{32,40},{40,32},{48,56},{56,48},{64,72... | collective-permute-start | bytes 786440 | tf_op jit(solution)/shard_map/ppermute | solution.py:87
  48.0 8.3 %collective-permute-start.9 = (f32[8,32,256]{2,1,0:T(8,128)S(1)}, f32[8,32,256]{2,1,0:T(8,128)S(1)}, u32[]{:S(2)}, u32[]{:S(2)}) collective-permute-start(f32[8,32,256]{2,1,0:T(8,128)S(1)} %collective-permute-done.5.refs_4_), channel_id=1, source_target_pairs={{0,8},{8,0},{16,24},{24,16},{32,40},{40,32},{48,56},{56,48},{64,72... | collective-permute-start | bytes 786440 | tf_op jit(solution)/shard_map/ppermute | solution.py:87
  50.4 6.0 %collective-permute-start.10 = (f32[8,32,256]{2,1,0:T(8,128)S(1)}, f32[8,32,256]{2,1,0:T(8,128)S(1)}, u32[]{:S(2)}, u32[]{:S(2)}) collective-permute-start(f32[8,32,256]{2,1,0:T(8,128)S(1)} %collective-permute-done.6.refs_5_), channel_id=1, source_target_pairs={{0,8},{8,0},{16,24},{24,16},{32,40},{40,32},{48,56},{56,48},{64,72... | collective-permute-start | bytes 786440 | tf_op jit(solution)/shard_map/ppermute | solution.py:87
  53.1 3.3 %collective-permute-start.7 = (f32[4,32,256]{2,1,0:T(8,128)S(1)}, f32[4,32,256]{2,1,0:T(8,128)S(1)}, u32[]{:S(2)}, u32[]{:S(2)}) collective-permute-start(f32[4,32,256]{2,1,0:T(8,128)S(1)} %collective-permute-done.3.refs_2_), channel_id=1, source_target_pairs={{0,8},{8,0},{16,24},{24,16},{32,40},{40,32},{48,56},{56,48},{64,72... | collective-permute-start | bytes 393224 | tf_op jit(solution)/shard_map/ppermute | solution.py:87
  56.3 0.9 copy-start.7
  59.5 31.7 %copy-start.9 = (s32[8]{0:T(128)S(1)}, s32[8]{0:T(128)}, u32[]{:S(2)}) copy-start(s32[8]{0:T(128)} %constant.155.clone) | copy-start | bytes 100
  59.5 32.8 %copy-start.4 = (f32[1,8,32,256]{3,2,1,0:T(8,128)S(1)}, f32[1,8,32,256]{3,2,1,0:T(8,128)}, u32[]{:S(2)}) copy-start(f32[1,8,32,256]{3,2,1,0:T(8,128)} %param.6) | copy-start | bytes 786436
  59.5 37.1 %all-to-all-start = ((f32[4,16,32,256]{3,2,1,0:T(8,128)}), f32[4,16,32,256]{3,2,1,0:T(8,128)S(1)}, u32[]{:S(2)}, u32[]{:S(2)}) async-start(f32[4,16,32,256]{3,2,1,0:T(8,128)} %bitcast.3), calls=%async_computation | async-start | bytes 4194304 | tf_op jit(solution)/shard_map/all_to_all | solution.py:140
  63.2 10.9 %collective-permute-start.14 = (f32[16,32,256]{2,1,0:T(8,128)S(1)}, f32[16,32,256]{2,1,0:T(8,128)S(1)}, u32[]{:S(2)}, u32[]{:S(2)}) collective-permute-start(f32[16,32,256]{2,1,0:T(8,128)S(1)} %collective-permute-done.13.refs_0_), channel_id=1, source_target_pairs={{0,1},{1,2},{2,3},{3,4},{4,5},{5,6},{6,7},{7,0},{8,15},{9,8},{10,9... | collective-permute-start | bytes 1572872 | tf_op jit(solution)/shard_map/ppermute | solution.py:89
  74.2 11.4 %collective-permute-start.15 = (f32[16,32,256]{2,1,0:T(8,128)S(1)}, f32[16,32,256]{2,1,0:T(8,128)}, u32[]{:S(2)}, u32[]{:S(2)}) collective-permute-start(f32[16,32,256]{2,1,0:T(8,128)S(1)} %collective-permute-done.14.refs_1_), channel_id=1, source_target_pairs={{0,1},{1,2},{2,3},{3,4},{4,5},{5,6},{6,7},{7,0},{8,15},{9,8},{10,9... | collective-permute-start | bytes 1572872 | tf_op jit(solution)/shard_map/ppermute | solution.py:89
  79.5 11.7 %collective-permute-start.16 = (f32[8,32,256]{2,1,0:T(8,128)S(1)}, f32[8,32,256]{2,1,0:T(8,128)S(1)}, u32[]{:S(2)}, u32[]{:S(2)}) collective-permute-start(f32[8,32,256]{2,1,0:T(8,128)S(1)} %slice.14), channel_id=1, source_target_pairs={{0,8},{8,0},{16,24},{24,16},{32,40},{40,32},{48,56},{56,48},{64,72... | collective-permute-start | bytes 786440 | tf_op jit(solution)/shard_map/ppermute | solution.py:87
  81.5 9.7 %collective-permute-start.17 = (f32[8,32,256]{2,1,0:T(8,128)S(1)}, f32[8,32,256]{2,1,0:T(8,128)S(1)}, u32[]{:S(2)}, u32[]{:S(2)}) collective-permute-start(f32[8,32,256]{2,1,0:T(8,128)S(1)} %slice.15), channel_id=1, source_target_pairs={{0,8},{8,0},{16,24},{24,16},{32,40},{40,32},{48,56},{56,48},{64,72... | collective-permute-start | bytes 786440 | tf_op jit(solution)/shard_map/ppermute | solution.py:87
  86.6 5.7 %collective-permute-start.18 = (f32[8,32,256]{2,1,0:T(8,128)S(1)}, f32[8,32,256]{2,1,0:T(8,128)S(1)}, u32[]{:S(2)}, u32[]{:S(2)}) collective-permute-start(f32[8,32,256]{2,1,0:T(8,128)S(1)} %slice.16), channel_id=1, source_target_pairs={{0,8},{8,0},{16,24},{24,16},{32,40},{40,32},{48,56},{56,48},{64,72... | collective-permute-start | bytes 786440 | tf_op jit(solution)/shard_map/ppermute | solution.py:87
  92.3 1.0 copy-start.6
  94.6 1.0 copy-start
  95.6 1.0 copy-start.2
  96.6 1.2 %copy-start.1 = (bf16[8,256,256]{2,1,0:T(8,128)(2,1)S(1)}, bf16[8,256,256]{2,1,0:T(8,128)(2,1)}, u32[]{:S(2)}) copy-start(bf16[8,256,256]{2,1,0:T(8,128)(2,1)} %copy-done) | copy-start | bytes 3145732
  97.8 1.2 %copy-start.3 = (bf16[8,256,256]{2,1,0:T(8,128)(2,1)S(1)}, bf16[8,256,256]{2,1,0:T(8,128)(2,1)}, u32[]{:S(2)}) copy-start(bf16[8,256,256]{2,1,0:T(8,128)(2,1)} %copy-done.2) | copy-start | bytes 3145732
  99.0 19.8 %copy-start.8 = (f32[1,32,256]{2,1,0:T(8,128)S(1)}, f32[1,32,256]{2,1,0:T(8,128)}, u32[]{:S(2)}) copy-start(f32[1,32,256]{2,1,0:T(8,128)} %param.8) | copy-start | bytes 98308

commit v3 on v1

v3 whole, which is shorter than its diff:
```python
import jax
import jax.numpy as jnp
from jax import lax
from jax.experimental import pallas as pl
from jax.experimental.pallas import tpu as pltpu
from jax.sharding import PartitionSpec as P

NX, NZ, NC, NY = 4, 8, 2, 8
SLOTS = 16
HALF = NY // 2


def node(x, z, c):
    return ((x % NX) * NZ + z % NZ) * NC + c


EVERY = [(x, z, c) for x in range(NX) for z in range(NZ) for c in range(NC)]
TWIN = [(node(x, z, c), node(x, z, 1 - c)) for x, z, c in EVERY]
Y_UP = [(y, (y + 1) % NY) for y in range(NY)]
Y_DOWN = [(y, (y - 1) % NY) for y in range(NY)]
X_ONE = [(node(x, z, c), node(x ^ 1, z, c)) for x, z, c in EVERY]
X_TWO = [(node(x, z, c), node(x ^ 2, z, c)) for x, z, c in EVERY]
Z_LINES = [[node(x, z, c) for z in range(NZ)] for x in range(NX) for c in range(NC)]
X_LINES = [[node(x, z, c) for x in range(NX)] for z in range(NZ) for c in range(NC)]
VMEM = pl.BlockSpec(memory_space=pltpu.VMEM)
ANY = pl.BlockSpec(memory_space=pl.ANY)
SMEM = pl.BlockSpec(memory_space=pltpu.SMEM)
PARAMS = pltpu.CompilerParams(vmem_limit_bytes=12 * 1024 * 1024)


def split(v):
    high = v.astype(jnp.bfloat16)
    return high, (v - high.astype(jnp.float32)).astype(jnp.bfloat16)


def dot3(a, b, dims):
    (ah, al), (bh, bl) = a, b
    dot = lambda u, v: lax.dot_general(u, v, (dims, ((), ())), preferred_element_type=jnp.float32)
    return dot(ah, bh) + (dot(ah, bl) + dot(al, bh))


def collect(place_ref, mine_ref, twins_ref, answers_ref):
    count = mine_ref.shape[0]

    def one(s, carry):
        place = place_ref[s]
        inside = lax.rem(place, count)
        answers_ref[s] = jnp.where(place < count, mine_ref[inside], twins_ref[inside])
        return carry

    lax.fori_loop(0, answers_ref.shape[0], one, 0, unroll=8)


def products(slot_ref, from_ref, start_ref, fetched_ref, own_ref, *refs):
    *pieces, off_ref, update_ref, whole_ref, named_ref, sems = refs
    kcount, rows, width = own_ref.shape
    copies = []

    def fetch(source, target):
        copies.append(pltpu.make_async_copy(source, target, sems.at[len(copies)]))
        copies[-1].start()

    for number in range(SLOTS):
        fetch(fetched_ref.at[from_ref[number]], named_ref.at[number])
    ranges = [(0, kcount)] * (len(pieces) - 2) + [(0, kcount // 2), (kcount // 2, kcount)]
    for number, (piece, (begin, end)) in enumerate(zip(pieces, ranges)):
        start = pl.multiple_of(start_ref[min(number + 1, NY - 1)], rows)
        fetch(piece, whole_ref.at[pl.ds(begin, end - begin), pl.ds(start, rows), :])
    start = pl.multiple_of(start_ref[0], rows)
    whole_ref[:, pl.ds(start, rows), :] = own_ref[...]
    for copy in copies:
        copy.wait()

    total = jnp.zeros((kcount * rows, width), jnp.float32)
    for b in range(kcount):
        left = jnp.concatenate([named_ref[slot_ref[a * kcount + b]] for a in range(kcount)], axis=0)
        total += dot3(split(left), split(whole_ref[b]), ((1,), (0,)))
    off = -total
    off_ref[...] = off.reshape(off_ref.shape)
    own = own_ref[...].reshape(kcount * rows, width)
    update_ref[...] = dot3(split(own), split(off), ((0,), (0,))).reshape(update_ref.shape)


def per_device(ancestor_inverse, panel, need_list, diag_factor):
    _, kcount, rows, width = panel.shape
    held = ancestor_inverse.shape[0]
    here, y = lax.axis_index("snode"), lax.axis_index("grp")
    x, c = here // (NZ * NC), here % NC
    own = panel[0]
    block = (rows, width)

    wanted = need_list.reshape(-1)
    ids = jnp.arange(NX * NZ * NC * held, dtype=jnp.int32)
    present = jnp.any(wanted[:, None] == ids[None, :], axis=0)
    slot = jnp.sum((present[None, :] & (ids[None, :] < wanted[:, None])).astype(jnp.int32), axis=1)
    order = jnp.arange(SLOTS, dtype=jnp.int32)
    distinct = jnp.max(jnp.where(slot[None, :] == order[:, None], wanted[None, :], 0), axis=1)
    pair = jnp.stack([distinct, lax.ppermute(distinct, "snode", X_ONE)])
    lists = jnp.concatenate([pair, lax.ppermute(pair, "snode", X_TWO)])

    mine = lax.all_to_all(
        jnp.broadcast_to(ancestor_inverse[None], (NZ,) + ancestor_inverse.shape),
        "snode", split_axis=0, concat_axis=0, tiled=True, axis_index_groups=Z_LINES,
    ).reshape((NZ * held,) + block)
    up = down = own
    pieces = []
    for step in range(1, HALF + 1):
        last = step == HALF
        up = lax.ppermute(up[: kcount // 2] if last else up, "grp", Y_UP)
        down = lax.ppermute(down[kcount // 2 :] if last else down, "grp", Y_DOWN)
        pieces += [up, down]
        if step == 2:
            mine, lists, up, down = lax.optimization_barrier((mine, lists, up, down))
    twins = lax.ppermute(mine, "snode", TWIN)

    asked = lists[jnp.arange(NX) ^ x]
    owner, k = asked // held, asked % held
    place = owner // NC % NZ * held + k + jnp.where(owner % NC == c, 0, NZ * held)
    place = jnp.where(owner // (NC * NZ) == x, place, 0)

    answers = pl.pallas_call(
        collect,
        out_shape=jax.ShapeDtypeStruct((NX * SLOTS,) + block, jnp.float32),
        in_specs=[SMEM, VMEM, VMEM],
        out_specs=VMEM,
        compiler_params=PARAMS,
        cost_estimate=pl.CostEstimate(flops=0, bytes_accessed=4_000_000, transcendentals=0),
    )(place.reshape(-1), mine, twins)
    fetched = lax.all_to_all(
        answers.reshape((NX, SLOTS) + block), "snode", split_axis=0, concat_axis=0, tiled=True, axis_index_groups=X_LINES
    ).reshape((NX * SLOTS,) + block)

    starts = (y + jnp.array([0, -1, 1, -2, 2, -3, 3, HALF], jnp.int32)) % NY * rows
    off, update = pl.pallas_call(
        products,
        out_shape=(
            jax.ShapeDtypeStruct((kcount,) + block, jnp.float32),
            jax.ShapeDtypeStruct((NY,) + block, jnp.float32),
        ),
        in_specs=[SMEM] * 3 + [ANY, VMEM] + [ANY] * len(pieces),
        out_specs=(VMEM, VMEM),
        scratch_shapes=[
            pltpu.VMEM((kcount, NY * rows, width), jnp.float32),
            pltpu.VMEM((SLOTS,) + block, jnp.float32),
            pltpu.SemaphoreType.DMA((SLOTS + len(pieces),)),
        ],
        compiler_params=PARAMS,
        cost_estimate=pl.CostEstimate(flops=1_000_000_000, bytes_accessed=5_000_000, transcendentals=0),
    )(slot, distinct // (held * NC * NZ) * SLOTS + order, starts, fetched, own, *pieces)
    parts = lax.all_to_all(update, "grp", split_axis=0, concat_axis=0, tiled=True)
    return off[None], diag_factor - jnp.sum(parts, axis=0)[None]


def solution(mesh):
    return jax.shard_map(
        per_device,
        mesh=mesh,
        in_specs=(
            P("snode", "grp", None),
            P("snode", None, "grp", None),
            P("snode", None, None),
            P("snode", "grp", None),
        ),
        out_specs=(P("snode", None, "grp", None), P("snode", "grp", None)),
        check_vma=False,
    )
```

time: 124 us -> 106 us (0.85)
  between operations: 14.3 us -> 0.89 us
  waiting for transfers between devices: 35.1 us -> 22.7 us
  starting transfers between devices: 44.7 us -> 52.2 us
  Pallas kernels: 2.34 us -> 5.21 us
  local copies, waits for them, and re-layouts: 7.25 us -> 5.68 us
    all_to_all x1 -> x2, waiting for transfers between devices: 25.7 us -> 5.48 us  [the longest x1 4.55 us: per_device(): lax.all_to_all(answers.reshape((NX, SLOTS) + block), 'snode', split_axis=...]
    all_to_all x1 -> x2, starting transfers between devices: 4.14 us -> 15 us  [the longest x1 10.9 us: per_device(): lax.all_to_all(jnp.broadcast_to(ancestor_inverse[None], (NZ,) + ancestor_...]
    ppermute x6 -> x9, waiting for transfers between devices: 8.16 us -> 14.2 us  [the longest x4 8.64 us: per_device(): up = lax.ppermute(up[:kcount // 2] if last else up, 'grp', Y_UP)]
    ppermute x6 -> x9, starting transfers between devices: 32.8 us -> 29.4 us  [the longest x4 15.2 us: per_device(): down = lax.ppermute(down[kcount // 2:] if last else down, 'grp', Y_DOWN)]
    pallas_call x1 -> x2, Pallas kernels: 2.34 us -> 5.21 us  [the longest x1 4.38 us: per_device(): pl.pallas_call(products, out_shape=(jax.ShapeDtypeStruct((kcount,) + bloc...]
    broadcast_in_dim x0 -> x1, local copies, waits for them, and re-layouts: none -> 2.04 us  [per_device(): jnp.broadcast_to(ancestor_inverse[None], (NZ,) + ancestor_inverse.shape)]
    gather x1 -> x0, local copies, waits for them, and re-layouts: 1.98 us -> none  [per_device(): pool[place]]
    concatenate x2 -> x0, other arithmetic: 1.94 us -> none  [the longest x1 1.02 us: per_device(): ring = jnp.concatenate(ring)]
  transfers between devices with their start and end apart: 10 -> 13, of which waited for: 6 -> 8; matrix products, arithmetic and copies ran while one was open for 6% -> 1% of each run, Pallas kernels for 0% -> 0%
where the time goes in v3:
time: 106 us; the launch traced here: 104 us
  starting transfers between devices  52.2 us (49%)
  waiting for transfers between devices  22.7 us (21%)
  blocking collectives  15.6 us (15%)
  local copies, waits for them, and re-layouts  5.68 us (5%)
  Pallas kernels  5.21 us (5%)
  other arithmetic  1.88 us (2%)
    all_to_all x1, blocking collectives, per_device(): lax.all_to_all(update, 'grp', split_axis=0, concat_axis=0, tiled=True)  15.6 us
    ppermute x4, starting transfers between devices, per_device(): down = lax.ppermute(down[kcount // 2:] if last else down, 'grp', Y_DOWN)  15.2 us
    all_to_all x1, starting transfers between devices, per_device(): lax.all_to_all(jnp.broadcast_to(ancestor_inverse[None], (NZ,) + ancestor_...  10.9 us
    ppermute x4, starting transfers between devices, per_device(): up = lax.ppermute(up[:kcount // 2] if last else up, 'grp', Y_UP)  9.53 us
    ppermute x4, waiting for transfers between devices, per_device(): up = lax.ppermute(up[:kcount // 2] if last else up, 'grp', Y_UP)  8.64 us
    ppermute x1, starting transfers between devices, per_device(): twins = lax.ppermute(mine, 'snode', TWIN)  4.7 us
    ppermute x1, starting transfers between devices, per_device(): lists = jnp.concatenate([pair, lax.ppermute(pair, 'snode', X_TWO)])  4.65 us
    all_to_all x1, waiting for transfers between devices, per_device(): lax.all_to_all(answers.reshape((NX, SLOTS) + block), 'snode', split_axis=...  4.55 us
  transfers between devices with their start and end apart: 13, of which 8 were waited for; matrix products, arithmetic and copies ran while one was open for 1% of the time, Pallas kernels for 0%

profile of v3, /device:TPU:1, one launch (start us, length us, event | category | flops | bytes accessed | tf_op | source)
XLA Modules:
  0.0 104.1 jit_solution(16457551763025315164)
XLA Ops:
  0.6 2.0 %broadcast_in_dim.40 = f32[8,4,32,256]{3,2,1,0:T(8,128)} broadcast(f32[4,32,256]{2,1,0:T(8,128)} %param.5), dimensions={1,2,3} | broadcast | bytes 1179648 | tf_op jit(solution)/shard_map/broadcast_in_dim | solution.py:102
  2.7 10.9 %all-to-all-start = ((f32[8,4,32,256]{3,2,1,0:T(8,128)}), f32[8,4,32,256]{3,2,1,0:T(8,128)S(1)}, u32[]{:S(2)}, u32[]{:S(2)}) async-start(f32[8,4,32,256]{3,2,1,0:T(8,128)} %broadcast_in_dim.40), calls=%async_computation | async-start | bytes 2097152 | tf_op jit(solution)/shard_map/all_to_all | solution.py:101
  13.6 3.2 %collective-permute-start.2 = (f32[8,32,256]{2,1,0:T(8,128)S(1)}, f32[8,32,256]{2,1,0:T(8,128)S(1)}, u32[]{:S(2)}, u32[]{:S(2)}) collective-permute-start(f32[8,32,256]{2,1,0:T(8,128)S(1)} %bitcast.15), channel_id=1, source_target_pairs={{0,1},{1,2},{2,3},{3,4},{4,5},{5,6},{6,7},{7,0},{8,9},{9,10},{10,1... | collective-permute-start | bytes 786440 | tf_op jit(solution)/shard_map/ppermute | solution.py:109
  16.8 3.8 %collective-permute-start.4 = (f32[8,32,256]{2,1,0:T(8,128)S(1)}, f32[8,32,256]{2,1,0:T(8,128)S(1)}, u32[]{:S(2)}, u32[]{:S(2)}) collective-permute-start(f32[8,32,256]{2,1,0:T(8,128)S(1)} %bitcast.16), channel_id=1, source_target_pairs={{0,7},{1,0},{2,1},{3,2},{4,3},{5,4},{6,5},{7,6},{8,15},{9,8},{10,9... | collective-permute-start | bytes 786440 | tf_op jit(solution)/shard_map/ppermute | solution.py:110
  20.8 0.2 convert_reduce_fusion.slot_ref
  21.0 3.4 %collective-permute-done.2.refs_0_ = f32[8,32,256]{2,1,0:T(8,128)S(1)} collective-permute-done((f32[8,32,256]{2,1,0:T(8,128)S(1)}, f32[8,32,256]{2,1,0:T(8,128)S(1)}, u32[]{:S(2)}, u32[]{:S(2)}) %collective-permute-start.2) | collective-permute-done | bytes 262176 | tf_op jit(solution)/shard_map/ppermute | solution.py:109
  24.4 1.9 %collective-permute-start.3 = (f32[8,32,256]{2,1,0:T(8,128)S(1)}, f32[8,32,256]{2,1,0:T(8,128)}, u32[]{:S(2)}, u32[]{:S(2)}) collective-permute-start(f32[8,32,256]{2,1,0:T(8,128)S(1)} %collective-permute-done.2.refs_0_), channel_id=1, source_target_pairs={{0,1},{1,2},{2,3},{3,4},{4,5},{5,6},{6,7},{7,0},{8,9},{9,10},{10,1... | collective-permute-start | bytes 786440 | tf_op jit(solution)/shard_map/ppermute | solution.py:109
  26.3 4.6 %collective-permute-start.5 = (f32[8,32,256]{2,1,0:T(8,128)S(1)}, f32[8,32,256]{2,1,0:T(8,128)}, u32[]{:S(2)}, u32[]{:S(2)}) collective-permute-start(f32[8,32,256]{2,1,0:T(8,128)S(1)} %collective-permute-done.4.refs_1_), channel_id=1, source_target_pairs={{0,7},{1,0},{2,1},{3,2},{4,3},{5,4},{6,5},{7,6},{8,15},{9,8},{10,9... | collective-permute-start | bytes 786440 | tf_op jit(solution)/shard_map/ppermute | solution.py:110
  30.9 0.1 select_reduce_fusion
  31.0 3.1 %collective-permute-start = (s32[16]{0:T(128)S(1)}, s32[16]{0:T(128)S(1)}, u32[]{:S(2)}, u32[]{:S(2)}) collective-permute-start(s32[16]{0:T(128)S(1)} %select_reduce_fusion), channel_id=1, source_target_pairs={{0,128},{8,136},{16,144},{24,152},{32,160},{40,168},{48,176},{56,1... | collective-permute-start | bytes 200 | tf_op jit(solution)/shard_map/ppermute | solution.py:98
  34.1 1.6 %collective-permute-done = s32[16]{0:T(128)S(1)} collective-permute-done((s32[16]{0:T(128)S(1)}, s32[16]{0:T(128)S(1)}, u32[]{:S(2)}, u32[]{:S(2)}) %collective-permute-start) | collective-permute-done | bytes 96 | tf_op jit(solution)/shard_map/ppermute | solution.py:98
  35.7 4.6 %collective-permute-start.1 = (s32[2,16]{1,0:T(2,128)S(1)}, s32[2,16]{1,0:T(2,128)S(1)}, u32[]{:S(2)}, u32[]{:S(2)}) collective-permute-start(s32[2,16]{1,0:T(2,128)S(1)} %pad_add_fusion.1), channel_id=1, source_target_pairs={{0,256},{8,264},{16,272},{24,280},{32,288},{40,296},{48,304},{56,3... | collective-permute-start | bytes 392 | tf_op jit(solution)/shard_map/ppermute | solution.py:99
  40.3 1.5 %collective-permute-done.1 = s32[2,16]{1,0:T(2,128)S(1)} collective-permute-done((s32[2,16]{1,0:T(2,128)S(1)}, s32[2,16]{1,0:T(2,128)S(1)}, u32[]{:S(2)}, u32[]{:S(2)}) %collective-permute-start.1) | collective-permute-done | bytes 160 | tf_op jit(solution)/shard_map/ppermute | solution.py:99
  41.8 0.9 all-to-all-done
  42.7 4.7 %collective-permute-start.6 = (f32[32,32,256]{2,1,0:T(8,128)S(1)}, f32[32,32,256]{2,1,0:T(8,128)S(1)}, u32[]{:S(2)}, u32[]{:S(2)}) collective-permute-start(f32[32,32,256]{2,1,0:T(8,128)S(1)} %bitcast.13), channel_id=1, source_target_pairs={{0,8},{8,0},{16,24},{24,16},{32,40},{40,32},{48,56},{56,48},{64,72... | collective-permute-start | bytes 3145736 | tf_op jit(solution)/shard_map/ppermute | solution.py:114
  47.5 0.6 gather_fusion
  48.2 1.5 %collective-permute-done.6.twins_ref = f32[32,32,256]{2,1,0:T(8,128)S(1)} collective-permute-done((f32[32,32,256]{2,1,0:T(8,128)S(1)}, f32[32,32,256]{2,1,0:T(8,128)S(1)}, u32[]{:S(2)}, u32[]{:S(2)}) %collective-permute-start.6) | collective-permute-done | bytes 1048608 | tf_op jit(solution)/shard_map/ppermute | solution.py:114
  49.7 0.8 shard_map.68
  50.6 1.3 %copy-done = f32[64,32,256]{2,1,0:T(8,128)} copy-done((f32[64,32,256]{2,1,0:T(8,128)}, f32[64,32,256]{2,1,0:T(8,128)S(1)}, u32[]{:S(2)}) %copy-start) | copy-done | bytes 2097176
  51.9 4.1 %all-to-all-start.1 = ((f32[4,16,32,256]{3,2,1,0:T(8,128)}), f32[4,16,32,256]{3,2,1,0:T(8,128)S(1)}, u32[]{:S(2)}, u32[]{:S(2)}) async-start(f32[4,16,32,256]{3,2,1,0:T(8,128)} %bitcast.12), calls=%async_computation.1 | async-start | bytes 4194304 | tf_op jit(solution)/shard_map/all_to_all | solution.py:129
  56.1 2.8 %collective-permute-start.8 = (f32[8,32,256]{2,1,0:T(8,128)}, f32[8,32,256]{2,1,0:T(8,128)S(1)}, u32[]{:S(2)}, u32[]{:S(2)}) collective-permute-start(f32[8,32,256]{2,1,0:T(8,128)} %collective-permute-done.5.refs_3_), channel_id=1, source_target_pairs={{0,7},{1,0},{2,1},{3,2},{4,3},{5,4},{6,5},{7,6},{8,15},{9,8},{10,9... | collective-permute-start | bytes 786440 | tf_op jit(solution)/shard_map/ppermute | solution.py:110
  58.8 2.5 %collective-permute-start.7 = (f32[8,32,256]{2,1,0:T(8,128)}, f32[8,32,256]{2,1,0:T(8,128)S(1)}, u32[]{:S(2)}, u32[]{:S(2)}) collective-permute-start(f32[8,32,256]{2,1,0:T(8,128)} %collective-permute-done.3.refs_2_), channel_id=1, source_target_pairs={{0,1},{1,2},{2,3},{3,4},{4,5},{5,6},{6,7},{7,0},{8,9},{9,10},{10,1... | collective-permute-start | bytes 786440 | tf_op jit(solution)/shard_map/ppermute | solution.py:109
  61.4 4.0 %collective-permute-done.8.refs_5_ = f32[8,32,256]{2,1,0:T(8,128)S(1)} collective-permute-done((f32[8,32,256]{2,1,0:T(8,128)}, f32[8,32,256]{2,1,0:T(8,128)S(1)}, u32[]{:S(2)}, u32[]{:S(2)}) %collective-permute-start.8) | collective-permute-done | bytes 262176 | tf_op jit(solution)/shard_map/ppermute | solution.py:110
  65.4 4.0 %collective-permute-start.10 = (f32[4,32,256]{2,1,0:T(8,128)S(1)}, f32[4,32,256]{2,1,0:T(8,128)S(1)}, u32[]{:S(2)}, u32[]{:S(2)}) collective-permute-start(f32[4,32,256]{2,1,0:T(8,128)S(1)} %slice.11), channel_id=1, source_target_pairs={{0,7},{1,0},{2,1},{3,2},{4,3},{5,4},{6,5},{7,6},{8,15},{9,8},{10,9... | collective-permute-start | bytes 393224 | tf_op jit(solution)/shard_map/ppermute | solution.py:110
  69.4 1.9 %collective-permute-start.9 = (f32[4,32,256]{2,1,0:T(8,128)S(1)}, f32[4,32,256]{2,1,0:T(8,128)S(1)}, u32[]{:S(2)}, u32[]{:S(2)}) collective-permute-start(f32[4,32,256]{2,1,0:T(8,128)S(1)} %slice.10), channel_id=1, source_target_pairs={{0,1},{1,2},{2,3},{3,4},{4,5},{5,6},{6,7},{7,0},{8,9},{9,10},{10,1... | collective-permute-start | bytes 393224 | tf_op jit(solution)/shard_map/ppermute | solution.py:109
  71.4 5.2 %collective-permute-done.9.refs_6_ = f32[4,32,256]{2,1,0:T(8,128)S(1)} collective-permute-done((f32[4,32,256]{2,1,0:T(8,128)S(1)}, f32[4,32,256]{2,1,0:T(8,128)S(1)}, u32[]{:S(2)}, u32[]{:S(2)}) %collective-permute-start.9) | collective-permute-done | bytes 131104 | tf_op jit(solution)/shard_map/ppermute | solution.py:109
  76.6 0.7 copy-done.2
  77.3 4.6 %all-to-all-done.1 = f32[4,16,32,256]{3,2,1,0:T(8,128)S(1)} async-done(((f32[4,16,32,256]{3,2,1,0:T(8,128)}), f32[4,16,32,256]{3,2,1,0:T(8,128)S(1)}, u32[]{:S(2)}, u32[]{:S(2)}) %all-to-all-start.1) | async-done | bytes 2097184 | tf_op jit(solution)/shard_map/all_to_all | solution.py:129
  81.8 0.9 copy-done.3
  82.7 4.4 %shard_map.69 = (f32[8,32,256]{2,1,0:T(8,128)}, f32[8,32,256]{2,1,0:T(8,128)S(1)}) custom-call(s32[64]{0:T(128)S(1)} %convert_reduce_fusion.slot_ref, s32[16]{0:T(128)S(1)} %iota_add_fusion.from_ref, s32[8]{0:T(128)S(1)} %fusion.4.start_ref, f32[64,32,256]{2,1,0:T(8,128)S(1)} %bitcast.11, f32[8,32,256]{2,1,0:T(8,128)S(1)} %bitcast.17, ...), custom_call_target="tpu_custom_call" | custom-call | flops 1000000000 | bytes 5000000 | tf_op jit(solution)/shard_map/pallas_call | solution.py:134
  87.1 15.6 %all_to_all.15 = f32[8,32,256]{2,1,0:T(8,128)S(1)} all-to-all(f32[8,32,256]{2,1,0:T(8,128)S(1)} %get-tuple-element.13), channel_id=1, replica_groups=mesh['snode'=64,'grp'=8] {'grp'}, dimensions={0} | all-to-all | bytes 524288 | tf_op jit(solution)/shard_map/all_to_all | solution.py:150
  102.7 1.4 %bitcast_subtract_fusion = f32[1,32,256]{2,1,0:T(8,128)} fusion(f32[1,32,256]{2,1,0:T(8,128)} %param.8, f32[32,256]{1,0:T(8,128)S(1)} %reduce_sum.19), kind=kLoop, calls=%fused_computation.6 | loop fusion | flops 8192 | bytes 98304 | tf_op jit(solution)/shard_map/sub | solution.py:151
  (27 shorter events, 0.4 us)
Async XLA Ops:
  0.6 12.9 %copy-start.1 = (f32[1,8,32,256]{3,2,1,0:T(8,128)S(1)}, f32[1,8,32,256]{3,2,1,0:T(8,128)}, u32[]{:S(2)}) copy-start(f32[1,8,32,256]{3,2,1,0:T(8,128)} %param.6) | copy-start | bytes 786436
  0.6 20.0 %copy-start.4 = (s32[1,8,8]{2,1,0:T(8,128)S(1)}, s32[1,8,8]{2,1,0:T(8,128)}, u32[]{:S(2)}) copy-start(s32[1,8,8]{2,1,0:T(8,128)} %param.7) | copy-start | bytes 772
  2.7 40.1 %all-to-all-start = ((f32[8,4,32,256]{3,2,1,0:T(8,128)}), f32[8,4,32,256]{3,2,1,0:T(8,128)S(1)}, u32[]{:S(2)}, u32[]{:S(2)}) async-start(f32[8,4,32,256]{3,2,1,0:T(8,128)} %broadcast_in_dim.40), calls=%async_computation | async-start | bytes 2097152 | tf_op jit(solution)/shard_map/all_to_all | solution.py:101
  13.6 10.8 %collective-permute-start.2 = (f32[8,32,256]{2,1,0:T(8,128)S(1)}, f32[8,32,256]{2,1,0:T(8,128)S(1)}, u32[]{:S(2)}, u32[]{:S(2)}) collective-permute-start(f32[8,32,256]{2,1,0:T(8,128)S(1)} %bitcast.15), channel_id=1, source_target_pairs={{0,1},{1,2},{2,3},{3,4},{4,5},{5,6},{6,7},{7,0},{8,9},{9,10},{10,1... | collective-permute-start | bytes 786440 | tf_op jit(solution)/shard_map/ppermute | solution.py:109
  16.8 9.5 %collective-permute-start.4 = (f32[8,32,256]{2,1,0:T(8,128)S(1)}, f32[8,32,256]{2,1,0:T(8,128)S(1)}, u32[]{:S(2)}, u32[]{:S(2)}) collective-permute-start(f32[8,32,256]{2,1,0:T(8,128)S(1)} %bitcast.16), channel_id=1, source_target_pairs={{0,7},{1,0},{2,1},{3,2},{4,3},{5,4},{6,5},{7,6},{8,15},{9,8},{10,9... | collective-permute-start | bytes 786440 | tf_op jit(solution)/shard_map/ppermute | solution.py:110
  24.4 17.4 %collective-permute-start.3 = (f32[8,32,256]{2,1,0:T(8,128)S(1)}, f32[8,32,256]{2,1,0:T(8,128)}, u32[]{:S(2)}, u32[]{:S(2)}) collective-permute-start(f32[8,32,256]{2,1,0:T(8,128)S(1)} %collective-permute-done.2.refs_0_), channel_id=1, source_target_pairs={{0,1},{1,2},{2,3},{3,4},{4,5},{5,6},{6,7},{7,0},{8,9},{9,10},{10,1... | collective-permute-start | bytes 786440 | tf_op jit(solution)/shard_map/ppermute | solution.py:109
  26.3 15.5 %collective-permute-start.5 = (f32[8,32,256]{2,1,0:T(8,128)S(1)}, f32[8,32,256]{2,1,0:T(8,128)}, u32[]{:S(2)}, u32[]{:S(2)}) collective-permute-start(f32[8,32,256]{2,1,0:T(8,128)S(1)} %collective-permute-done.4.refs_1_), channel_id=1, source_target_pairs={{0,7},{1,0},{2,1},{3,2},{4,3},{5,4},{6,5},{7,6},{8,15},{9,8},{10,9... | collective-permute-start | bytes 786440 | tf_op jit(solution)/shard_map/ppermute | solution.py:110
  31.0 4.7 %collective-permute-start = (s32[16]{0:T(128)S(1)}, s32[16]{0:T(128)S(1)}, u32[]{:S(2)}, u32[]{:S(2)}) collective-permute-start(s32[16]{0:T(128)S(1)} %select_reduce_fusion), channel_id=1, source_target_pairs={{0,128},{8,136},{16,144},{24,152},{32,160},{40,168},{48,176},{56,1... | collective-permute-start | bytes 200 | tf_op jit(solution)/shard_map/ppermute | solution.py:98
  35.7 6.1 %collective-permute-start.1 = (s32[2,16]{1,0:T(2,128)S(1)}, s32[2,16]{1,0:T(2,128)S(1)}, u32[]{:S(2)}, u32[]{:S(2)}) collective-permute-start(s32[2,16]{1,0:T(2,128)S(1)} %pad_add_fusion.1), channel_id=1, source_target_pairs={{0,256},{8,264},{16,272},{24,280},{32,288},{40,296},{48,304},{56,3... | collective-permute-start | bytes 392 | tf_op jit(solution)/shard_map/ppermute | solution.py:99
  42.7 7.0 %collective-permute-start.6 = (f32[32,32,256]{2,1,0:T(8,128)S(1)}, f32[32,32,256]{2,1,0:T(8,128)S(1)}, u32[]{:S(2)}, u32[]{:S(2)}) collective-permute-start(f32[32,32,256]{2,1,0:T(8,128)S(1)} %bitcast.13), channel_id=1, source_target_pairs={{0,8},{8,0},{16,24},{24,16},{32,40},{40,32},{48,56},{56,48},{64,72... | collective-permute-start | bytes 3145736 | tf_op jit(solution)/shard_map/ppermute | solution.py:114
  50.6 1.3 %copy-start = (f32[64,32,256]{2,1,0:T(8,128)}, f32[64,32,256]{2,1,0:T(8,128)S(1)}, u32[]{:S(2)}) copy-start(f32[64,32,256]{2,1,0:T(8,128)S(1)} %shard_map.68) | copy-start | bytes 6291460
  51.9 19.4 %copy-start.5 = (s32[8]{0:T(128)S(1)}, s32[8]{0:T(128)}, u32[]{:S(2)}) copy-start(s32[8]{0:T(128)} %constant.128.clone) | copy-start | bytes 100
  51.9 29.9 %all-to-all-start.1 = ((f32[4,16,32,256]{3,2,1,0:T(8,128)}), f32[4,16,32,256]{3,2,1,0:T(8,128)S(1)}, u32[]{:S(2)}, u32[]{:S(2)}) async-start(f32[4,16,32,256]{3,2,1,0:T(8,128)} %bitcast.12), calls=%async_computation.1 | async-start | bytes 4194304 | tf_op jit(solution)/shard_map/all_to_all | solution.py:129
  56.1 9.3 %collective-permute-start.8 = (f32[8,32,256]{2,1,0:T(8,128)}, f32[8,32,256]{2,1,0:T(8,128)S(1)}, u32[]{:S(2)}, u32[]{:S(2)}) collective-permute-start(f32[8,32,256]{2,1,0:T(8,128)} %collective-permute-done.5.refs_3_), channel_id=1, source_target_pairs={{0,7},{1,0},{2,1},{3,2},{4,3},{5,4},{6,5},{7,6},{8,15},{9,8},{10,9... | collective-permute-start | bytes 786440 | tf_op jit(solution)/shard_map/ppermute | solution.py:110
  58.8 10.5 %collective-permute-start.7 = (f32[8,32,256]{2,1,0:T(8,128)}, f32[8,32,256]{2,1,0:T(8,128)S(1)}, u32[]{:S(2)}, u32[]{:S(2)}) collective-permute-start(f32[8,32,256]{2,1,0:T(8,128)} %collective-permute-done.3.refs_2_), channel_id=1, source_target_pairs={{0,1},{1,2},{2,3},{3,4},{4,5},{5,6},{6,7},{7,0},{8,9},{9,10},{10,1... | collective-permute-start | bytes 786440 | tf_op jit(solution)/shard_map/ppermute | solution.py:109
  65.4 6.0 %collective-permute-start.10 = (f32[4,32,256]{2,1,0:T(8,128)S(1)}, f32[4,32,256]{2,1,0:T(8,128)S(1)}, u32[]{:S(2)}, u32[]{:S(2)}) collective-permute-start(f32[4,32,256]{2,1,0:T(8,128)S(1)} %slice.11), channel_id=1, source_target_pairs={{0,7},{1,0},{2,1},{3,2},{4,3},{5,4},{6,5},{7,6},{8,15},{9,8},{10,9... | collective-permute-start | bytes 393224 | tf_op jit(solution)/shard_map/ppermute | solution.py:110
  69.4 7.2 %collective-permute-start.9 = (f32[4,32,256]{2,1,0:T(8,128)S(1)}, f32[4,32,256]{2,1,0:T(8,128)S(1)}, u32[]{:S(2)}, u32[]{:S(2)}) collective-permute-start(f32[4,32,256]{2,1,0:T(8,128)S(1)} %slice.10), channel_id=1, source_target_pairs={{0,1},{1,2},{2,3},{3,4},{4,5},{5,6},{6,7},{7,0},{8,9},{9,10},{10,1... | collective-permute-start | bytes 393224 | tf_op jit(solution)/shard_map/ppermute | solution.py:109
  76.6 0.7 copy-start.2
  81.8 0.9 copy-start.3

commit v4 on v3

v4 whole, which is shorter than its diff:
```python
import jax
import jax.numpy as jnp
from jax import lax
from jax.experimental import pallas as pl
from jax.experimental.pallas import tpu as pltpu
from jax.sharding import PartitionSpec as P

NX, NZ, NC, NY = 4, 8, 2, 8
SLOTS = 16
HALF = NY // 2


def node(x, z, c):
    return ((x % NX) * NZ + z % NZ) * NC + c


EVERY = [(x, z, c) for x in range(NX) for z in range(NZ) for c in range(NC)]
TWIN = [(node(x, z, c), node(x, z, 1 - c)) for x, z, c in EVERY]
Y_ROUND = [
    (node(x, z, c) * NY + y, node(x, z, c) * NY + (y + 1 - 2 * c) % NY) for x, z, c in EVERY for y in range(NY)
]
X_ONE = [(node(x, z, c), node(x ^ 1, z, c)) for x, z, c in EVERY]
X_TWO = [(node(x, z, c), node(x ^ 2, z, c)) for x, z, c in EVERY]
Z_LINES = [[node(x, z, c) for z in range(NZ)] for x in range(NX) for c in range(NC)]
X_LINES = [[node(x, z, c) for x in range(NX)] for z in range(NZ) for c in range(NC)]
VMEM = pl.BlockSpec(memory_space=pltpu.VMEM)
HBM = pl.BlockSpec(memory_space=pltpu.HBM)
SMEM = pl.BlockSpec(memory_space=pltpu.SMEM)
PARAMS = pltpu.CompilerParams(vmem_limit_bytes=12 * 1024 * 1024)


def split(v):
    high = v.astype(jnp.bfloat16)
    return high, (v - high.astype(jnp.float32)).astype(jnp.bfloat16)


def dot3(a, b, dims):
    (ah, al), (bh, bl) = a, b
    dot = lambda u, v: lax.dot_general(u, v, (dims, ((), ())), preferred_element_type=jnp.float32)
    return dot(ah, bh) + (dot(ah, bl) + dot(al, bh))


def repeat(block_ref, all_ref, sem):
    copies = [pltpu.make_async_copy(block_ref, all_ref.at[n], sem.at[n]) for n in range(all_ref.shape[0])]
    for copy in copies:
        copy.start()
    for copy in copies:
        copy.wait()


def collect(place_ref, mine_ref, twins_ref, answers_ref, picked_ref, sem):
    count = mine_ref.shape[0]
    readers, slots = answers_ref.shape[:2]
    for reader in range(readers):

        def one(s, carry):
            place = place_ref[reader * slots + s]
            inside = lax.rem(place, count)
            picked_ref[reader, s] = jnp.where(place < count, mine_ref[inside], twins_ref[inside])
            return carry

        lax.fori_loop(0, slots, one, 0, unroll=8)
        pltpu.make_async_copy(picked_ref.at[reader], answers_ref.at[reader], sem.at[reader]).start()
    for reader in range(readers):
        pltpu.make_async_copy(picked_ref.at[reader], answers_ref.at[reader], sem.at[reader]).wait()


def stage(own_ref, diag_ref, staged_ref):
    staged_ref[: own_ref.shape[0]] = own_ref[...]
    staged_ref[own_ref.shape[0]] = diag_ref[...]


def products(pick_ref, start_ref, fetched_ref, staged_ref, *refs):
    *pieces, off_ref, update_ref, whole_ref, sems = refs
    kcount, rows, _ = off_ref.shape
    copies = []

    starts = [pl.multiple_of(start_ref[number], rows) for number in range(NY)]
    messages = (len(pieces) - 1) // 2
    parts = [staged_ref.at[pl.ds(0, kcount)], pieces[0]] + [piece.at[pl.ds(0, kcount)] for piece in pieces[1 : 1 + messages]]
    parts += [piece.at[pl.ds(kcount, kcount)] for piece in pieces[1 + messages :]]
    for number, (part, start) in enumerate(zip(parts, starts)):
        copies.append(pltpu.make_async_copy(part, whole_ref.at[:, pl.ds(start, rows), :], sems.at[number]))
        copies[-1].start()
    for copy in copies:
        copy.wait()

    total = jnp.zeros((kcount * rows, whole_ref.shape[2]), jnp.float32)
    for b in range(kcount):
        left = jnp.concatenate([fetched_ref[pick_ref[a * kcount + b]] for a in range(kcount)], axis=0)
        total += dot3(split(left), split(whole_ref[b]), ((1,), (0,)))
    off_ref[...] = -total.reshape(off_ref.shape)
    own = staged_ref[:kcount].reshape(total.shape)
    update_ref[...] = dot3(split(own), split(total), ((0,), (0,))).reshape(update_ref.shape)
    update_ref[lax.div(starts[0], rows)] += staged_ref[kcount]


def per_device(ancestor_inverse, panel, need_list, diag_factor):
    _, kcount, rows, width = panel.shape
    held = ancestor_inverse.shape[0]
    here, y = lax.axis_index("snode"), lax.axis_index("grp")
    x, c = here // (NZ * NC), here % NC
    own = panel[0]
    block = (rows, width)

    wanted = need_list.reshape(-1)
    ids = jnp.arange(NX * NZ * NC * held, dtype=jnp.int32)
    present = jnp.any(wanted[:, None] == ids[None, :], axis=0)
    slot = jnp.sum((present[None, :] & (ids[None, :] < wanted[:, None])).astype(jnp.int32), axis=1)
    order = jnp.arange(SLOTS, dtype=jnp.int32)
    distinct = jnp.max(jnp.where(slot[None, :] == order[:, None], wanted[None, :], 0), axis=1)
    neighbour = lax.ppermute(distinct, "snode", X_ONE)
    pair = jnp.stack([distinct, neighbour])
    lists = jnp.concatenate([pair, lax.ppermute(pair, "snode", X_TWO)])

    copies = pl.pallas_call(
        repeat,
        out_shape=jax.ShapeDtypeStruct((NZ,) + ancestor_inverse.shape, jnp.float32),
        in_specs=[HBM],
        out_specs=HBM,
        scratch_shapes=[pltpu.SemaphoreType.DMA((NZ,))],
        compiler_params=PARAMS,
    )(ancestor_inverse)
    mine = lax.all_to_all(
        copies,
        "snode", split_axis=0, concat_axis=0, tiled=True, axis_index_groups=Z_LINES,
    ).reshape((NZ * held,) + block)
    on = lambda v: lax.ppermute(v, ("snode", "grp"), Y_ROUND)
    twin = lambda v: lax.ppermute(v, "snode", TWIN)
    lead = on(own)
    later, _ = lax.optimization_barrier((own, neighbour))
    passed = on(jnp.concatenate([lead, twin(later)]))
    mine, lists, passed = lax.optimization_barrier((mine, lists, passed))
    twins = twin(mine)
    staged = pl.pallas_call(
        stage,
        out_shape=jax.ShapeDtypeStruct((kcount + 1,) + block, jnp.float32),
        in_specs=[VMEM, VMEM],
        out_specs=VMEM,
        compiler_params=PARAMS,
    )(own, diag_factor[0])
    messages, swapped = [passed], []
    for step in range(HALF - 2):
        if step == 1:
            staged, messages[-1] = lax.optimization_barrier((staged, messages[-1]))
        following = on(messages[-1])
        before, following = lax.optimization_barrier((messages[-1], following))
        swapped.append(twin(before))
        messages.append(following)
    pieces = [lead] + messages + swapped + [twin(messages[-1])]

    asked = lists[jnp.arange(NX) ^ x]
    owner, k = asked // held, asked % held
    place = owner // NC % NZ * held + k + jnp.where(owner % NC == c, 0, NZ * held)
    place = jnp.where(owner // (NC * NZ) == x, place, 0)

    answers = pl.pallas_call(
        collect,
        out_shape=jax.ShapeDtypeStruct((NX, SLOTS) + block, jnp.float32),
        in_specs=[SMEM, VMEM, VMEM],
        out_specs=HBM,
        scratch_shapes=[pltpu.VMEM((NX, SLOTS) + block, jnp.float32), pltpu.SemaphoreType.DMA((NX,))],
        compiler_params=PARAMS,
        cost_estimate=pl.CostEstimate(flops=0, bytes_accessed=4_000_000, transcendentals=0),
    )(place.reshape(-1), mine, twins)
    fetched = lax.all_to_all(
        answers, "snode", split_axis=0, concat_axis=0, tiled=True, axis_index_groups=X_LINES
    ).reshape((NX * SLOTS,) + block)

    starts = (y + (2 * c - 1) * jnp.array([0, 1, 2, 3, 4, -1, -2, -3], jnp.int32)) % NY * rows
    off, update = pl.pallas_call(
        products,
        out_shape=(
            jax.ShapeDtypeStruct((kcount,) + block, jnp.float32),
            jax.ShapeDtypeStruct((NY,) + block, jnp.float32),
        ),
        in_specs=[SMEM] * 2 + [VMEM] * 2 + [HBM] * len(pieces),
        out_specs=(VMEM, VMEM),
        scratch_shapes=[pltpu.VMEM((kcount, NY * rows, width), jnp.float32), pltpu.SemaphoreType.DMA((NY,))],
        compiler_params=PARAMS,
        cost_estimate=pl.CostEstimate(flops=1_000_000_000, bytes_accessed=5_000_000, transcendentals=0),
    )(wanted // (held * NC * NZ) * SLOTS + slot, starts, fetched, staged, *pieces)
    parts = lax.all_to_all(update, "grp", split_axis=0, concat_axis=0, tiled=True)
    return off[None], jnp.sum(parts, axis=0)[None]


def solution(mesh):
    return jax.shard_map(
        per_device,
        mesh=mesh,
        in_specs=(
            P("snode", "grp", None),
            P("snode", None, "grp", None),
            P("snode", None, None),
            P("snode", "grp", None),
        ),
        out_specs=(P("snode", None, "grp", None), P("snode", "grp", None)),
        check_vma=False,
    )
```

time: 106 us -> 103 us (0.972); the launches traced: 104 us -> 103 us
  starting transfers between devices: 52.2 us -> 55 us
  local copies, waits for them, and re-layouts: 5.68 us -> 3 us
    ppermute x10, waiting for transfers between devices: 15.7 us -> 8.39 us  [the longest x4 6.09 us: per_device(): on = lambda v: lax.ppermute(v, ('snode', 'grp'), Y_ROUND)]
    all_to_all x2, waiting for transfers between devices: 5.48 us -> 11.8 us  [the longest x1 6.15 us: per_device(): lax.all_to_all(answers, 'snode', split_axis=0, concat_axis=0, tiled=True,...]
    ppermute x10, starting transfers between devices: 32.5 us -> 35.6 us  [the longest x4 20 us: per_device(): on = lambda v: lax.ppermute(v, ('snode', 'grp'), Y_ROUND)]
    broadcast_in_dim x1 -> x0, local copies, waits for them, and re-layouts: 2.04 us -> none  [per_device(): jnp.broadcast_to(ancestor_inverse[None], (NZ,) + ancestor_inverse.shape)]
    sub x1 -> x0, other arithmetic: 1.38 us -> none  [per_device(): return (off[None], diag_factor - jnp.sum(parts, axis=0)[None])]
    pallas_call x1 -> x3, Pallas kernels: 0.84 us -> 2.13 us  [the longest x1 1.06 us: per_device(): pl.pallas_call(collect, out_shape=jax.ShapeDtypeStruct((NX, SLOTS) + bloc...]
  transfers between devices with their start and end apart: 13 -> 13, of which waited for: 8 -> 8; matrix products, arithmetic and copies ran while one was open for 1% -> 1% of each run, Pallas kernels for 0% -> 1%
where the time goes in v4:
time: 103 us
  starting transfers between devices  55 us (53%)
  waiting for transfers between devices  21.7 us (21%)
  blocking collectives  15 us (15%)
  Pallas kernels  5.87 us (6%)
  local copies, waits for them, and re-layouts  3 us (3%)
  other arithmetic  1.16 us (1%)
    ppermute x4, starting transfers between devices, per_device(): on = lambda v: lax.ppermute(v, ('snode', 'grp'), Y_ROUND)  20 us
    all_to_all x1, blocking collectives, per_device(): lax.all_to_all(update, 'grp', split_axis=0, concat_axis=0, tiled=True)  15 us
    ppermute x5, starting transfers between devices, per_device(): twin = lambda v: lax.ppermute(v, 'snode', TWIN)  12.5 us
    all_to_all x1, starting transfers between devices, per_device(): lax.all_to_all(copies, 'snode', split_axis=0, concat_axis=0, tiled=True,...  10.9 us
    all_to_all x1, waiting for transfers between devices, per_device(): lax.all_to_all(answers, 'snode', split_axis=0, concat_axis=0, tiled=True,...  6.15 us
    ppermute x4, waiting for transfers between devices, per_device(): on = lambda v: lax.ppermute(v, ('snode', 'grp'), Y_ROUND)  6.09 us
    all_to_all x1, waiting for transfers between devices, per_device(): lax.all_to_all(copies, 'snode', split_axis=0, concat_axis=0, tiled=True,...  5.68 us
    ppermute x1, starting transfers between devices, per_device(): lists = jnp.concatenate([pair, lax.ppermute(pair, 'snode', X_TWO)])  4.36 us
  transfers between devices with their start and end apart: 13, of which 8 were waited for; matrix products, arithmetic and copies ran while one was open for 1% of the time, Pallas kernels for 1%

profile of v4, /device:TPU:1, one launch (start us, length us, event | category | flops | bytes accessed | tf_op | source)
XLA Modules:
  0.0 102.6 jit_solution(2210254350075063000)
XLA Ops:
  0.6 0.9 copy-done.2
  1.6 1.0 %shard_map.68 = f32[8,4,32,256]{3,2,1,0:T(8,128)} custom-call(f32[4,32,256]{2,1,0:T(8,128)S(1)} %copy-done.2), custom_call_target="tpu_custom_call" | custom-call | tf_op jit(solution)/shard_map/pallas_call | solution.py:116
  2.6 10.9 %all-to-all-start = ((f32[8,4,32,256]{3,2,1,0:T(8,128)}), f32[8,4,32,256]{3,2,1,0:T(8,128)S(1)}, u32[]{:S(2)}, u32[]{:S(2)}) async-start(f32[8,4,32,256]{3,2,1,0:T(8,128)} %shard_map.68), calls=%async_computation | async-start | bytes 2097152 | tf_op jit(solution)/shard_map/all_to_all | solution.py:124
  13.6 0.1 fusion
  13.7 0.2 convert_reduce_fusion
  13.9 0.1 select_reduce_fusion
  14.0 3.1 %collective-permute-start = (s32[16]{0:T(128)S(1)}, s32[16]{0:T(128)S(1)}, u32[]{:S(2)}, u32[]{:S(2)}) collective-permute-start(s32[16]{0:T(128)S(1)} %select_reduce_fusion), channel_id=1, source_target_pairs={{0,128},{8,136},{16,144},{24,152},{32,160},{40,168},{48,176},{56,1... | collective-permute-start | bytes 200 | tf_op jit(solution)/shard_map/ppermute | solution.py:112
  17.2 5.1 %collective-permute-start.2 = (f32[8,32,256]{2,1,0:T(8,128)S(1)}, f32[8,32,256]{2,1,0:T(8,128)S(1)}, u32[]{:S(2)}, u32[]{:S(2)}) collective-permute-start(f32[8,32,256]{2,1,0:T(8,128)S(1)} %bitcast.13), channel_id=1, source_target_pairs={{0,1},{1,2},{2,3},{3,4},{4,5},{5,6},{6,7},{7,0},{8,15},{9,8},{10,9... | collective-permute-start | bytes 786440 | tf_op jit(solution)/shard_map/ppermute | solution.py:128
  22.3 1.9 %collective-permute-start.3 = (f32[8,32,256]{2,1,0:T(8,128)S(1)}, f32[8,32,256]{2,1,0:T(8,128)S(1)}, u32[]{:S(2)}, u32[]{:S(2)}) collective-permute-start(f32[8,32,256]{2,1,0:T(8,128)S(1)} %bitcast.14), channel_id=1, source_target_pairs={{0,8},{8,0},{16,24},{24,16},{32,40},{40,32},{48,56},{56,48},{64,72... | collective-permute-start | bytes 786440 | tf_op jit(solution)/shard_map/ppermute | solution.py:129
  24.2 1.4 %collective-permute-done.2.refs_0_ = f32[8,32,256]{2,1,0:T(8,128)S(1)} collective-permute-done((f32[8,32,256]{2,1,0:T(8,128)S(1)}, f32[8,32,256]{2,1,0:T(8,128)S(1)}, u32[]{:S(2)}, u32[]{:S(2)}) %collective-permute-start.2) | collective-permute-done | bytes 262176 | tf_op jit(solution)/shard_map/ppermute | solution.py:128
  25.6 0.1 collective-permute-done.3
  25.7 5.2 %collective-permute-start.4 = (f32[16,32,256]{2,1,0:T(8,128)S(1)}, f32[16,32,256]{2,1,0:T(8,128)S(1)}, u32[]{:S(2)}, u32[]{:S(2)}) collective-permute-start(f32[16,32,256]{2,1,0:T(8,128)S(1)} %pad_maximum_fusion), channel_id=1, source_target_pairs={{0,1},{1,2},{2,3},{3,4},{4,5},{5,6},{6,7},{7,0},{8,15},{9,8},{10,9... | collective-permute-start | bytes 1572872 | tf_op jit(solution)/shard_map/ppermute | solution.py:128
  30.9 4.4 %collective-permute-start.1 = (s32[2,16]{1,0:T(2,128)S(1)}, s32[2,16]{1,0:T(2,128)S(1)}, u32[]{:S(2)}, u32[]{:S(2)}) collective-permute-start(s32[2,16]{1,0:T(2,128)S(1)} %pad_add_fusion.1), channel_id=1, source_target_pairs={{0,256},{8,264},{16,272},{24,280},{32,288},{40,296},{48,304},{56,3... | collective-permute-start | bytes 392 | tf_op jit(solution)/shard_map/ppermute | solution.py:114
  35.3 1.5 %collective-permute-done.1 = s32[2,16]{1,0:T(2,128)S(1)} collective-permute-done((s32[2,16]{1,0:T(2,128)S(1)}, s32[2,16]{1,0:T(2,128)S(1)}, u32[]{:S(2)}, u32[]{:S(2)}) %collective-permute-start.1) | collective-permute-done | bytes 160 | tf_op jit(solution)/shard_map/ppermute | solution.py:114
  36.8 0.2 collective-permute-done.4.refs_1_
  37.0 5.7 %all-to-all-done = f32[8,4,32,256]{3,2,1,0:T(8,128)S(1)} async-done(((f32[8,4,32,256]{3,2,1,0:T(8,128)}), f32[8,4,32,256]{3,2,1,0:T(8,128)S(1)}, u32[]{:S(2)}, u32[]{:S(2)}) %all-to-all-start) | async-done | bytes 1048608 | tf_op jit(solution)/shard_map/all_to_all | solution.py:124
  42.7 2.4 %collective-permute-start.5 = (f32[32,32,256]{2,1,0:T(8,128)S(1)}, f32[32,32,256]{2,1,0:T(8,128)S(1)}, u32[]{:S(2)}, u32[]{:S(2)}) collective-permute-start(f32[32,32,256]{2,1,0:T(8,128)S(1)} %bitcast.11), channel_id=1, source_target_pairs={{0,8},{8,0},{16,24},{24,16},{32,40},{40,32},{48,56},{56,48},{64,72... | collective-permute-start | bytes 3145736 | tf_op jit(solution)/shard_map/ppermute | solution.py:129
  45.2 0.6 gather_fusion
  45.8 5.1 %collective-permute-start.6 = (f32[16,32,256]{2,1,0:T(8,128)S(1)}, f32[16,32,256]{2,1,0:T(8,128)}, u32[]{:S(2)}, u32[]{:S(2)}) collective-permute-start(f32[16,32,256]{2,1,0:T(8,128)S(1)} %collective-permute-done.4.refs_1_), channel_id=1, source_target_pairs={{0,1},{1,2},{2,3},{3,4},{4,5},{5,6},{6,7},{7,0},{8,15},{9,8},{10,9... | collective-permute-start | bytes 1572872 | tf_op jit(solution)/shard_map/ppermute | solution.py:128
  50.9 1.1 %shard_map.69 = f32[4,16,32,256]{3,2,1,0:T(8,128)S(1)} custom-call(s32[64]{0:T(128)S(1)} %compare_select_fusion.6.place_ref, f32[32,32,256]{2,1,0:T(8,128)S(1)} %bitcast.12, f32[32,32,256]{2,1,0:T(8,128)S(1)} %collective-permute-done.5.twins_ref), custom_call_target="tpu_custom_call" | custom-call | bytes 4000000 | tf_op jit(solution)/shard_map/pallas_call | solution.py:157
  52.0 1.3 %copy-done = f32[4,16,32,256]{3,2,1,0:T(8,128)} copy-done((f32[4,16,32,256]{3,2,1,0:T(8,128)}, f32[4,16,32,256]{3,2,1,0:T(8,128)S(1)}, u32[]{:S(2)}) %copy-start) | copy-done | bytes 2097176
  53.4 4.1 %all-to-all-start.1 = ((f32[4,16,32,256]{3,2,1,0:T(8,128)}), f32[4,16,32,256]{3,2,1,0:T(8,128)S(1)}, u32[]{:S(2)}, u32[]{:S(2)}) async-start(f32[4,16,32,256]{3,2,1,0:T(8,128)} %copy-done), calls=%async_computation.1 | async-start | bytes 4194304 | tf_op jit(solution)/shard_map/all_to_all | solution.py:166
  57.5 4.6 %collective-permute-start.7 = (f32[16,32,256]{2,1,0:T(8,128)}, f32[16,32,256]{2,1,0:T(8,128)}, u32[]{:S(2)}, u32[]{:S(2)}) collective-permute-start(f32[16,32,256]{2,1,0:T(8,128)} %collective-permute-done.6.refs_2_), channel_id=1, source_target_pairs={{0,1},{1,2},{2,3},{3,4},{4,5},{5,6},{6,7},{7,0},{8,15},{9,8},{10,9... | collective-permute-start | bytes 1572872 | tf_op jit(solution)/shard_map/ppermute | solution.py:128
  62.1 1.9 %collective-permute-start.8 = (f32[16,32,256]{2,1,0:T(8,128)S(1)}, f32[16,32,256]{2,1,0:T(8,128)}, u32[]{:S(2)}, u32[]{:S(2)}) collective-permute-start(f32[16,32,256]{2,1,0:T(8,128)S(1)} %collective-permute-done.4.refs_1_), channel_id=1, source_target_pairs={{0,8},{8,0},{16,24},{24,16},{32,40},{40,32},{48,56},{56,48},{64,72... | collective-permute-start | bytes 1572872 | tf_op jit(solution)/shard_map/ppermute | solution.py:129
  64.1 4.5 %collective-permute-done.7.refs_3_ = f32[16,32,256]{2,1,0:T(8,128)} collective-permute-done((f32[16,32,256]{2,1,0:T(8,128)}, f32[16,32,256]{2,1,0:T(8,128)}, u32[]{:S(2)}, u32[]{:S(2)}) %collective-permute-start.7) | collective-permute-done | bytes 524320 | tf_op jit(solution)/shard_map/ppermute | solution.py:128
  68.6 4.4 %collective-permute-start.9 = (f32[16,32,256]{2,1,0:T(8,128)}, f32[16,32,256]{2,1,0:T(8,128)}, u32[]{:S(2)}, u32[]{:S(2)}) collective-permute-start(f32[16,32,256]{2,1,0:T(8,128)} %collective-permute-done.6.refs_2_), channel_id=1, source_target_pairs={{0,8},{8,0},{16,24},{24,16},{32,40},{40,32},{48,56},{56,48},{64,72... | collective-permute-start | bytes 1572872 | tf_op jit(solution)/shard_map/ppermute | solution.py:129
  72.9 1.9 %collective-permute-start.10 = (f32[16,32,256]{2,1,0:T(8,128)}, f32[16,32,256]{2,1,0:T(8,128)}, u32[]{:S(2)}, u32[]{:S(2)}) collective-permute-start(f32[16,32,256]{2,1,0:T(8,128)} %collective-permute-done.7.refs_3_), channel_id=1, source_target_pairs={{0,8},{8,0},{16,24},{24,16},{32,40},{40,32},{48,56},{56,48},{64,72... | collective-permute-start | bytes 1572872 | tf_op jit(solution)/shard_map/ppermute | solution.py:129
  74.9 2.1 %collective-permute-done.10.refs_6_ = f32[16,32,256]{2,1,0:T(8,128)} collective-permute-done((f32[16,32,256]{2,1,0:T(8,128)}, f32[16,32,256]{2,1,0:T(8,128)}, u32[]{:S(2)}, u32[]{:S(2)}) %collective-permute-start.10) | collective-permute-done | bytes 524320 | tf_op jit(solution)/shard_map/ppermute | solution.py:129
  77.1 6.1 %all-to-all-done.1 = f32[4,16,32,256]{3,2,1,0:T(8,128)S(1)} async-done(((f32[4,16,32,256]{3,2,1,0:T(8,128)}), f32[4,16,32,256]{3,2,1,0:T(8,128)S(1)}, u32[]{:S(2)}, u32[]{:S(2)}) %all-to-all-start.1) | async-done | bytes 2097184 | tf_op jit(solution)/shard_map/all_to_all | solution.py:166
  83.2 3.7 %shard_map.71 = (f32[8,32,256]{2,1,0:T(8,128)}, f32[8,32,256]{2,1,0:T(8,128)S(1)}) custom-call(s32[64]{0:T(128)S(1)} %multiply_add_fusion.pick_ref, s32[8]{0:T(128)S(1)} %fusion.4.start_ref, f32[64,32,256]{2,1,0:T(8,128)S(1)} %bitcast.10, f32[9,32,256]{2,1,0:T(8,128)S(1)} %shard_map.70.staged_ref, f32[8,32,256]{2,1,0:T(8,128)S(1)} %collective-permute-done.2.refs_0_, ...), custom_call_target="tpu_custom_call" | custom-call | flops 1000000000 | bytes 5000000 | tf_op jit(solution)/shard_map/pallas_call | solution.py:171
  87.0 15.0 %all_to_all.15 = f32[8,32,256]{2,1,0:T(8,128)S(1)} all-to-all(f32[8,32,256]{2,1,0:T(8,128)S(1)} %get-tuple-element.25), channel_id=1, replica_groups=mesh['snode'=64,'grp'=8] {'grp'}, dimensions={0} | all-to-all | bytes 524288 | tf_op jit(solution)/shard_map/all_to_all | solution.py:183
  102.0 0.6 reduce_sum.19
  (26 shorter events, 0.3 us)
Async XLA Ops:
  0.6 16.5 %copy-start.1 = (f32[1,8,32,256]{3,2,1,0:T(8,128)S(1)}, f32[1,8,32,256]{3,2,1,0:T(8,128)}, u32[]{:S(2)}) copy-start(f32[1,8,32,256]{3,2,1,0:T(8,128)} %param.6) | copy-start | bytes 786436
  0.6 0.9 copy-start.2
  1.6 11.9 %copy-start.4 = (s32[1,8,8]{2,1,0:T(8,128)S(1)}, s32[1,8,8]{2,1,0:T(8,128)}, u32[]{:S(2)}) copy-start(s32[1,8,8]{2,1,0:T(8,128)} %param.7) | copy-start | bytes 772
  2.6 40.1 %all-to-all-start = ((f32[8,4,32,256]{3,2,1,0:T(8,128)}), f32[8,4,32,256]{3,2,1,0:T(8,128)S(1)}, u32[]{:S(2)}, u32[]{:S(2)}) async-start(f32[8,4,32,256]{3,2,1,0:T(8,128)} %shard_map.68), calls=%async_computation | async-start | bytes 2097152 | tf_op jit(solution)/shard_map/all_to_all | solution.py:124
  14.0 8.2 %collective-permute-start = (s32[16]{0:T(128)S(1)}, s32[16]{0:T(128)S(1)}, u32[]{:S(2)}, u32[]{:S(2)}) collective-permute-start(s32[16]{0:T(128)S(1)} %select_reduce_fusion), channel_id=1, source_target_pairs={{0,128},{8,136},{16,144},{24,152},{32,160},{40,168},{48,176},{56,1... | collective-permute-start | bytes 200 | tf_op jit(solution)/shard_map/ppermute | solution.py:112
  17.2 8.4 %collective-permute-start.2 = (f32[8,32,256]{2,1,0:T(8,128)S(1)}, f32[8,32,256]{2,1,0:T(8,128)S(1)}, u32[]{:S(2)}, u32[]{:S(2)}) collective-permute-start(f32[8,32,256]{2,1,0:T(8,128)S(1)} %bitcast.13), channel_id=1, source_target_pairs={{0,1},{1,2},{2,3},{3,4},{4,5},{5,6},{6,7},{7,0},{8,15},{9,8},{10,9... | collective-permute-start | bytes 786440 | tf_op jit(solution)/shard_map/ppermute | solution.py:128
  22.3 3.4 %collective-permute-start.3 = (f32[8,32,256]{2,1,0:T(8,128)S(1)}, f32[8,32,256]{2,1,0:T(8,128)S(1)}, u32[]{:S(2)}, u32[]{:S(2)}) collective-permute-start(f32[8,32,256]{2,1,0:T(8,128)S(1)} %bitcast.14), channel_id=1, source_target_pairs={{0,8},{8,0},{16,24},{24,16},{32,40},{40,32},{48,56},{56,48},{64,72... | collective-permute-start | bytes 786440 | tf_op jit(solution)/shard_map/ppermute | solution.py:129
  25.7 11.3 %collective-permute-start.4 = (f32[16,32,256]{2,1,0:T(8,128)S(1)}, f32[16,32,256]{2,1,0:T(8,128)S(1)}, u32[]{:S(2)}, u32[]{:S(2)}) collective-permute-start(f32[16,32,256]{2,1,0:T(8,128)S(1)} %pad_maximum_fusion), channel_id=1, source_target_pairs={{0,1},{1,2},{2,3},{3,4},{4,5},{5,6},{6,7},{7,0},{8,15},{9,8},{10,9... | collective-permute-start | bytes 1572872 | tf_op jit(solution)/shard_map/ppermute | solution.py:128
  30.9 5.8 %collective-permute-start.1 = (s32[2,16]{1,0:T(2,128)S(1)}, s32[2,16]{1,0:T(2,128)S(1)}, u32[]{:S(2)}, u32[]{:S(2)}) collective-permute-start(s32[2,16]{1,0:T(2,128)S(1)} %pad_add_fusion.1), channel_id=1, source_target_pairs={{0,256},{8,264},{16,272},{24,280},{32,288},{40,296},{48,304},{56,3... | collective-permute-start | bytes 392 | tf_op jit(solution)/shard_map/ppermute | solution.py:114
  42.7 8.2 %collective-permute-start.5 = (f32[32,32,256]{2,1,0:T(8,128)S(1)}, f32[32,32,256]{2,1,0:T(8,128)S(1)}, u32[]{:S(2)}, u32[]{:S(2)}) collective-permute-start(f32[32,32,256]{2,1,0:T(8,128)S(1)} %bitcast.11), channel_id=1, source_target_pairs={{0,8},{8,0},{16,24},{24,16},{32,40},{40,32},{48,56},{56,48},{64,72... | collective-permute-start | bytes 3145736 | tf_op jit(solution)/shard_map/ppermute | solution.py:129
  45.8 11.7 %collective-permute-start.6 = (f32[16,32,256]{2,1,0:T(8,128)S(1)}, f32[16,32,256]{2,1,0:T(8,128)}, u32[]{:S(2)}, u32[]{:S(2)}) collective-permute-start(f32[16,32,256]{2,1,0:T(8,128)S(1)} %collective-permute-done.4.refs_1_), channel_id=1, source_target_pairs={{0,1},{1,2},{2,3},{3,4},{4,5},{5,6},{6,7},{7,0},{8,15},{9,8},{10,9... | collective-permute-start | bytes 1572872 | tf_op jit(solution)/shard_map/ppermute | solution.py:128
  52.0 1.3 %copy-start = (f32[4,16,32,256]{3,2,1,0:T(8,128)}, f32[4,16,32,256]{3,2,1,0:T(8,128)S(1)}, u32[]{:S(2)}) copy-start(f32[4,16,32,256]{3,2,1,0:T(8,128)S(1)} %shard_map.69) | copy-start | bytes 6291460
  53.3 4.2 %copy-start.3 = (f32[1,32,256]{2,1,0:T(8,128)S(1)}, f32[1,32,256]{2,1,0:T(8,128)}, u32[]{:S(2)}) copy-start(f32[1,32,256]{2,1,0:T(8,128)} %param.8) | copy-start | bytes 98308
  53.4 21.5 %copy-start.5 = (s32[8]{0:T(128)S(1)}, s32[8]{0:T(128)}, u32[]{:S(2)}) copy-start(s32[8]{0:T(128)} %constant.130.clone) | copy-start | bytes 100
  53.4 29.9 %all-to-all-start.1 = ((f32[4,16,32,256]{3,2,1,0:T(8,128)}), f32[4,16,32,256]{3,2,1,0:T(8,128)S(1)}, u32[]{:S(2)}, u32[]{:S(2)}) async-start(f32[4,16,32,256]{3,2,1,0:T(8,128)} %copy-done), calls=%async_computation.1 | async-start | bytes 4194304 | tf_op jit(solution)/shard_map/all_to_all | solution.py:166
  57.5 11.0 %collective-permute-start.7 = (f32[16,32,256]{2,1,0:T(8,128)}, f32[16,32,256]{2,1,0:T(8,128)}, u32[]{:S(2)}, u32[]{:S(2)}) collective-permute-start(f32[16,32,256]{2,1,0:T(8,128)} %collective-permute-done.6.refs_2_), channel_id=1, source_target_pairs={{0,1},{1,2},{2,3},{3,4},{4,5},{5,6},{6,7},{7,0},{8,15},{9,8},{10,9... | collective-permute-start | bytes 1572872 | tf_op jit(solution)/shard_map/ppermute | solution.py:128
  62.1 12.8 %collective-permute-start.8 = (f32[16,32,256]{2,1,0:T(8,128)S(1)}, f32[16,32,256]{2,1,0:T(8,128)}, u32[]{:S(2)}, u32[]{:S(2)}) collective-permute-start(f32[16,32,256]{2,1,0:T(8,128)S(1)} %collective-permute-done.4.refs_1_), channel_id=1, source_target_pairs={{0,8},{8,0},{16,24},{24,16},{32,40},{40,32},{48,56},{56,48},{64,72... | collective-permute-start | bytes 1572872 | tf_op jit(solution)/shard_map/ppermute | solution.py:129
  68.6 6.4 %collective-permute-start.9 = (f32[16,32,256]{2,1,0:T(8,128)}, f32[16,32,256]{2,1,0:T(8,128)}, u32[]{:S(2)}, u32[]{:S(2)}) collective-permute-start(f32[16,32,256]{2,1,0:T(8,128)} %collective-permute-done.6.refs_2_), channel_id=1, source_target_pairs={{0,8},{8,0},{16,24},{24,16},{32,40},{40,32},{48,56},{56,48},{64,72... | collective-permute-start | bytes 1572872 | tf_op jit(solution)/shard_map/ppermute | solution.py:129
  72.9 4.1 %collective-permute-start.10 = (f32[16,32,256]{2,1,0:T(8,128)}, f32[16,32,256]{2,1,0:T(8,128)}, u32[]{:S(2)}, u32[]{:S(2)}) collective-permute-start(f32[16,32,256]{2,1,0:T(8,128)} %collective-permute-done.7.refs_3_), channel_id=1, source_target_pairs={{0,8},{8,0},{16,24},{24,16},{32,40},{40,32},{48,56},{56,48},{64,72... | collective-permute-start | bytes 1572872 | tf_op jit(solution)/shard_map/ppermute | solution.py:129

commit v5 on v4

v5 whole, which is shorter than its diff:
```python
import jax
import jax.numpy as jnp
from jax import lax
from jax.experimental import pallas as pl
from jax.experimental.pallas import tpu as pltpu
from jax.sharding import PartitionSpec as P

NX, NZ, NC, NY = 4, 8, 2, 8
SLOTS = 16
FEW = 12
HALF = NY // 2


def node(x, z, c):
    return ((x % NX) * NZ + z % NZ) * NC + c


EVERY = [(x, z, c) for x in range(NX) for z in range(NZ) for c in range(NC)]
TWIN = [(node(x, z, c), node(x, z, 1 - c)) for x, z, c in EVERY]
Y_ROUND = [
    (node(x, z, c) * NY + y, node(x, z, c) * NY + (y + 1 - 2 * c) % NY) for x, z, c in EVERY for y in range(NY)
]
X_ONE = [(node(x, z, c), node(x ^ 1, z, c)) for x, z, c in EVERY]
X_TWO = [(node(x, z, c), node(x ^ 2, z, c)) for x, z, c in EVERY]
Z_LINES = [[node(x, z, c) for z in range(NZ)] for x in range(NX) for c in range(NC)]
X_LINES = [[node(x, z, c) for x in range(NX)] for z in range(NZ) for c in range(NC)]
VMEM = pl.BlockSpec(memory_space=pltpu.VMEM)
HBM = pl.BlockSpec(memory_space=pltpu.HBM)
SMEM = pl.BlockSpec(memory_space=pltpu.SMEM)
in_hbm = lambda v: pltpu.with_memory_space_constraint(v, pltpu.HBM)
in_vmem = lambda v: pltpu.with_memory_space_constraint(v, pltpu.VMEM)
PARAMS = pltpu.CompilerParams(vmem_limit_bytes=12 * 1024 * 1024)


def split(v):
    high = v.astype(jnp.bfloat16)
    return high, (v - high.astype(jnp.float32)).astype(jnp.bfloat16)


def dot3(a, b, dims):
    (ah, al), (bh, bl) = a, b
    dot = lambda u, v: lax.dot_general(u, v, (dims, ((), ())), preferred_element_type=jnp.float32)
    return dot(ah, bh) + (dot(ah, bl) + dot(al, bh))


def repeat(block_ref, all_ref, held_ref, sem, sems):
    copy = pltpu.make_async_copy(block_ref, held_ref, sem)
    copy.start()
    copy.wait()
    copies = [pltpu.make_async_copy(held_ref, all_ref.at[n], sems.at[n]) for n in range(all_ref.shape[0])]
    for copy in copies:
        copy.start()
    for copy in copies:
        copy.wait()


def collect(place_ref, mine_ref, twins_ref, few_ref, rest_ref, picked_ref, sem):
    count = mine_ref.shape[0]
    readers, few = few_ref.shape[:2]
    slots = few + rest_ref.shape[1]
    copies = []
    for target_ref, begin, end in ((few_ref, 0, few), (rest_ref, few, slots)):
        for reader in range(readers):

            def one(s, carry):
                place = place_ref[reader * slots + s]
                inside = lax.rem(place, count)
                picked_ref[reader, s] = jnp.where(place < count, mine_ref[inside], twins_ref[inside])
                return carry

            lax.fori_loop(begin, end, one, 0, unroll=4)
            source = picked_ref.at[reader, pl.ds(begin, end - begin)]
            copies.append(pltpu.make_async_copy(source, target_ref.at[reader], sem.at[len(copies)]))
            copies[-1].start()
    for copy in copies:
        copy.wait()


def stage(own_ref, diag_ref, staged_ref):
    staged_ref[: own_ref.shape[0]] = own_ref[...]
    staged_ref[own_ref.shape[0]] = diag_ref[...]


def assemble(start_ref, staged_ref, *refs):
    *pieces, whole_ref, raw_ref, sems = refs
    _, kcount, width, _ = whole_ref.shape
    rows = width // NY
    messages = (len(pieces) - 1) // 2
    parts = [piece.at[pl.ds(0, kcount)] for piece in pieces[: 1 + messages]]
    parts += [piece.at[pl.ds(kcount, kcount)] for piece in pieces[1 + messages :]]
    copies = [pltpu.make_async_copy(part, raw_ref.at[n], sems.at[n]) for n, part in enumerate(parts)]
    for copy in copies:
        copy.start()
    for number in range(NY):
        if number:
            copies[number - 1].wait()
        start = pl.multiple_of(start_ref[number], rows)
        high, low = split(raw_ref[number - 1] if number else staged_ref[:kcount])
        whole_ref[0, :, pl.ds(start, rows), :] = high
        whole_ref[1, :, pl.ds(start, rows), :] = low


def products(pick_ref, mine_ref, fetched_ref, extra_ref, staged_ref, whole_ref, off_ref, update_ref, held_ref, sem):
    kcount, rows, width = off_ref.shape
    count = fetched_ref.shape[0]

    def named(at):
        usual = fetched_ref[lax.min(at, count - 1)]
        return jnp.where(at < count, usual, extra_ref[lax.max(at - count, 0)])

    total = jnp.zeros((kcount * rows, width), jnp.float32)
    for b in range(kcount):
        left = jnp.concatenate([named(pick_ref[a * kcount + b]) for a in range(kcount)], axis=0)
        total += dot3(split(left), (whole_ref[0, b], whole_ref[1, b]), ((1,), (0,)))
    held_ref[...] = -total.reshape(off_ref.shape)
    copy = pltpu.make_async_copy(held_ref, off_ref, sem)
    copy.start()
    own = staged_ref[:kcount].reshape(total.shape)
    update_ref[...] = dot3(split(own), split(total), ((0,), (0,))).reshape(update_ref.shape)
    update_ref[mine_ref[0]] += staged_ref[kcount]
    copy.wait()


def per_device(ancestor_inverse, panel, need_list, diag_factor):
    _, kcount, rows, width = panel.shape
    held = ancestor_inverse.shape[0]
    here, y = lax.axis_index("snode"), lax.axis_index("grp")
    x, c = here // (NZ * NC), here % NC
    own = panel[0]
    block = (rows, width)

    wanted = need_list.reshape(-1)
    ids = jnp.arange(NX * NZ * NC * held, dtype=jnp.int32)
    present = jnp.any(wanted[:, None] == ids[None, :], axis=0)
    slot = jnp.sum((present[None, :] & (ids[None, :] < wanted[:, None])).astype(jnp.int32), axis=1)
    order = jnp.arange(SLOTS, dtype=jnp.int32)
    distinct = jnp.max(jnp.where(slot[None, :] == order[:, None], wanted[None, :], 0), axis=1)
    neighbour = lax.ppermute(distinct, "snode", X_ONE)
    twin = lambda v: lax.ppermute(v, "snode", TWIN)
    later, _ = lax.optimization_barrier((own, neighbour))
    twins_own = twin(later)
    pair, twins_own = lax.optimization_barrier((jnp.stack([distinct, neighbour]), twins_own))
    lists = jnp.concatenate([pair, lax.ppermute(pair, "snode", X_TWO)])

    span = held * NC * NZ
    lists = lists[jnp.arange(NX) ^ x]
    begins = jnp.sum((lists[:, None, :] < order[None, : NX + 1, None] * span).astype(jnp.int32), axis=2)
    first = jnp.sum((lists < x * span).astype(jnp.int32), axis=1)
    at = first[:, None] + order[None, :]
    asked = jnp.sum(jnp.where(at[:, :, None] == order, lists[:, None, :], 0), axis=2)
    many = jnp.max(begins[:, 1:] - begins[:, :-1]) > FEW
    owner, k = asked // held, asked % held
    place = owner // NC % NZ * held + k + jnp.where(owner % NC == c, 0, NZ * held)
    place = jnp.where((owner // (NC * NZ) == x) & (at < SLOTS), place, 0)

    copies = pl.pallas_call(
        repeat,
        out_shape=pltpu.HBM((NZ,) + ancestor_inverse.shape, jnp.float32),
        in_specs=[HBM],
        out_specs=HBM,
        scratch_shapes=[
            pltpu.VMEM(ancestor_inverse.shape, jnp.float32),
            pltpu.SemaphoreType.DMA,
            pltpu.SemaphoreType.DMA((NZ,)),
        ],
        compiler_params=PARAMS,
    )(in_hbm(ancestor_inverse))
    mine = lax.all_to_all(
        copies,
        "snode", split_axis=0, concat_axis=0, tiled=True, axis_index_groups=Z_LINES,
    ).reshape((NZ * held,) + block)
    on = lambda v: lax.ppermute(v, ("snode", "grp"), Y_ROUND)
    lead = on(own)
    passed = on(jnp.concatenate([lead, twins_own]))
    mine, place, many, passed = lax.optimization_barrier((mine, place, many, passed))
    twins = twin(mine)
    counts = jnp.sum((distinct[None, :] // span == order[:NX, None]).astype(jnp.int32), axis=1)
    fullest = jnp.argmax(counts).astype(jnp.int32)
    home = wanted // span
    place_there = slot - jnp.sum((distinct[None, :] < home[:, None] * span).astype(jnp.int32), axis=1)
    pick = jnp.where(place_there < FEW, home * FEW, NX * FEW - FEW) + place_there
    staged = pl.pallas_call(
        stage,
        out_shape=pltpu.VMEM((kcount + 1,) + block, jnp.float32),
        in_specs=[VMEM, VMEM],
        out_specs=VMEM,
        compiler_params=PARAMS,
    )(own, diag_factor[0])
    messages = [passed, on(passed)]
    staged, pick, fullest, following = lax.optimization_barrier((staged, pick, fullest, messages[1]))
    messages.append(on(following))
    before, last, _ = lax.optimization_barrier((messages[0], messages[1], following))
    swapped = [twin(before), twin(last), twin(messages[2])]
    pieces = [lead] + messages + swapped
    pieces = [in_vmem(piece) if number in (3, 4) else in_hbm(piece) for number, piece in enumerate(pieces)]

    few, rest = pl.pallas_call(
        collect,
        out_shape=(pltpu.HBM((NX, FEW) + block, jnp.float32), pltpu.HBM((NX, SLOTS - FEW) + block, jnp.float32)),
        in_specs=[SMEM, VMEM, VMEM],
        out_specs=(HBM, HBM),
        scratch_shapes=[pltpu.VMEM((NX, SLOTS) + block, jnp.float32), pltpu.SemaphoreType.DMA((2 * NX,))],
        compiler_params=PARAMS,
        cost_estimate=pl.CostEstimate(flops=0, bytes_accessed=4_000_000, transcendentals=0),
    )(place.reshape(-1), in_vmem(mine), in_vmem(twins))
    over_x = lambda v: lax.all_to_all(
        v, "snode", split_axis=0, concat_axis=0, tiled=True, axis_index_groups=X_LINES
    )
    fetched = over_x(few).reshape((NX * FEW,) + block)
    starts = (y + (2 * c - 1) * jnp.array([0, 1, 2, 3, 4, -1, -2, -3], jnp.int32)) % NY * rows
    whole = pl.pallas_call(
        assemble,
        out_shape=pltpu.VMEM((2, kcount, NY * rows, width), jnp.bfloat16),
        in_specs=[SMEM, VMEM] + [VMEM if number in (3, 4) else HBM for number in range(len(pieces))],
        out_specs=VMEM,
        scratch_shapes=[pltpu.VMEM((NY - 1, kcount) + block, jnp.float32), pltpu.SemaphoreType.DMA((NY - 1,))],
        compiler_params=PARAMS,
        cost_estimate=pl.CostEstimate(flops=0, bytes_accessed=4_000_000, transcendentals=0),
    )(starts, in_vmem(staged), *pieces)
    fetched, rest = lax.optimization_barrier((fetched, rest))
    extra = lax.cond(
        many,
        lambda v: lax.dynamic_index_in_dim(over_x(v), fullest, 0, keepdims=False),
        lambda v: jnp.zeros(v.shape[1:], v.dtype),
        rest,
    )

    off, update = pl.pallas_call(
        products,
        out_shape=(
            pltpu.HBM((kcount,) + block, jnp.float32),
            jax.ShapeDtypeStruct((NY,) + block, jnp.float32),
        ),
        in_specs=[SMEM] * 2 + [VMEM] * 4,
        out_specs=(HBM, VMEM),
        scratch_shapes=[pltpu.VMEM((kcount,) + block, jnp.float32), pltpu.SemaphoreType.DMA],
        compiler_params=PARAMS,
        cost_estimate=pl.CostEstimate(flops=1_000_000_000, bytes_accessed=5_000_000, transcendentals=0),
    )(pick, y.reshape(1), *map(in_vmem, (fetched, extra, staged, whole)))
    parts = lax.all_to_all(update, "grp", split_axis=0, concat_axis=0, tiled=True)
    return off[None], jnp.sum(parts, axis=0)[None]


def solution(mesh):
    return jax.shard_map(
        per_device,
        mesh=mesh,
        in_specs=(
            P("snode", "grp", None),
            P("snode", None, "grp", None),
            P("snode", None, None),
            P("snode", "grp", None),
        ),
        out_specs=(P("snode", None, "grp", None), P("snode", "grp", None)),
        check_vma=False,
    )
```

time: 103 us -> 98.3 us (0.954)
  waiting for transfers between devices: 21.7 us -> 12.4 us
  Pallas kernels: 5.87 us -> 9.17 us
  starting transfers between devices: 55 us -> 52.5 us
  other arithmetic: 1.16 us -> 3.52 us
  blocking collectives: 15 us -> 16.5 us
  local copies, waits for them, and re-layouts: 3 us -> 1.57 us
    all_to_all x1, waiting for transfers between devices: 6.15 us -> 1.03 us  [per_device(): lax.all_to_all(v, 'snode', split_axis=0, concat_axis=0, tiled=True, axis_...]
    all_to_all x1, waiting for transfers between devices: 5.68 us -> 2.32 us  [per_device(): lax.all_to_all(copies, 'snode', split_axis=0, concat_axis=0, tiled=True,...]
    pallas_call x4 -> x5, Pallas kernels: 5.87 us -> 9.17 us  [the longest x1 3.22 us: per_device(): pl.pallas_call(products, out_shape=(pltpu.HBM((kcount,) + block, jnp.floa...]
    ppermute x4, starting transfers between devices: 20 us -> 17.1 us  [per_device(): on = lambda v: lax.ppermute(v, ('snode', 'grp'), Y_ROUND)]
    all_to_all x1, blocking collectives: 15 us -> 16.5 us  [per_device(): lax.all_to_all(update, 'grp', split_axis=0, concat_axis=0, tiled=True)]
    ppermute x1, waiting for transfers between devices: 1.47 us -> 0.01 us  [per_device(): lists = jnp.concatenate([pair, lax.ppermute(pair, 'snode', X_TWO)])]
    unnamed x12 -> x14, local copies, waits for them, and re-layouts: 2.28 us -> 0.83 us
  transfers between devices with their start and end apart: 13 -> 13, of which waited for: 8 -> 6; matrix products, arithmetic and copies ran while one was open for 1% -> 4% of each run, Pallas kernels for 1% -> 4%
where the time goes in v5:
time: 98.3 us; the launch traced here: 97.3 us
  starting transfers between devices  52.5 us (53%)
  blocking collectives  16.5 us (17%)
  waiting for transfers between devices  12.4 us (13%)
  Pallas kernels  9.17 us (9%)
  other arithmetic  3.52 us (4%)
  between operations  1.67 us (2%)
  local copies, waits for them, and re-layouts  1.57 us (2%)
    ppermute x4, starting transfers between devices, per_device(): on = lambda v: lax.ppermute(v, ('snode', 'grp'), Y_ROUND)  17.1 us
    all_to_all x1, blocking collectives, per_device(): lax.all_to_all(update, 'grp', split_axis=0, concat_axis=0, tiled=True)  16.5 us
    ppermute x5, starting transfers between devices, per_device(): twin = lambda v: lax.ppermute(v, 'snode', TWIN)  12.7 us
    all_to_all x1, starting transfers between devices, per_device(): lax.all_to_all(copies, 'snode', split_axis=0, concat_axis=0, tiled=True,...  10.9 us
    ppermute x4, waiting for transfers between devices, per_device(): on = lambda v: lax.ppermute(v, ('snode', 'grp'), Y_ROUND)  6.84 us
    ppermute x1, starting transfers between devices, per_device(): lists = jnp.concatenate([pair, lax.ppermute(pair, 'snode', X_TWO)])  4.35 us
    all_to_all x1, starting transfers between devices, per_device(): lax.all_to_all(v, 'snode', split_axis=0, concat_axis=0, tiled=True, axis_...  4.35 us
    pallas_call x1, Pallas kernels, per_device(): pl.pallas_call(products, out_shape=(pltpu.HBM((kcount,) + block, jnp.floa...  3.22 us
  transfers between devices with their start and end apart: 13, of which 6 were waited for; matrix products, arithmetic and copies ran while one was open for 4% of the time, Pallas kernels for 4%

profile of v5, /device:TPU:1, one launch (start us, length us, event | category | flops | bytes accessed | tf_op | source)
XLA Modules:
  0.0 97.3 jit_solution(7326620614389370473)
XLA Ops:
  0.6 2.0 %shard_map.69 = f32[8,4,32,256]{3,2,1,0:T(8,128)} custom-call(f32[4,32,256]{2,1,0:T(8,128)} %block_ref.1), custom_call_target="tpu_custom_call" | custom-call | tf_op jit(solution)/shard_map/pallas_call | solution.py:156
  2.7 10.9 %all-to-all-start.1 = ((f32[8,4,32,256]{3,2,1,0:T(8,128)}), f32[8,4,32,256]{3,2,1,0:T(8,128)S(1)}, u32[]{:S(2)}, u32[]{:S(2)}) async-start(f32[8,4,32,256]{3,2,1,0:T(8,128)} %shard_map.69), calls=%async_computation.1 | async-start | bytes 2097152 | tf_op jit(solution)/shard_map/all_to_all | solution.py:168
  14.1 3.1 %collective-permute-start = (s32[16]{0:T(128)S(1)}, s32[16]{0:T(128)S(1)}, u32[]{:S(2)}, u32[]{:S(2)}) collective-permute-start(s32[16]{0:T(128)S(1)} %select_reduce_fusion.1), channel_id=1, source_target_pairs={{0,128},{8,136},{16,144},{24,152},{32,160},{40,168},{48,176},{56,1... | collective-permute-start | bytes 200 | tf_op jit(solution)/shard_map/ppermute | solution.py:138
  17.2 5.1 %collective-permute-start.3 = (f32[8,32,256]{2,1,0:T(8,128)S(1)}, f32[8,32,256]{2,1,0:T(8,128)S(1)}, u32[]{:S(2)}, u32[]{:S(2)}) collective-permute-start(f32[8,32,256]{2,1,0:T(8,128)S(1)} %bitcast.16), channel_id=1, source_target_pairs={{0,1},{1,2},{2,3},{3,4},{4,5},{5,6},{6,7},{7,0},{8,15},{9,8},{10,9... | collective-permute-start | bytes 786440 | tf_op jit(solution)/shard_map/ppermute | solution.py:172
  22.4 1.9 %collective-permute-start.1 = (f32[8,32,256]{2,1,0:T(8,128)S(1)}, f32[8,32,256]{2,1,0:T(8,128)S(1)}, u32[]{:S(2)}, u32[]{:S(2)}) collective-permute-start(f32[8,32,256]{2,1,0:T(8,128)S(1)} %bitcast.17), channel_id=1, source_target_pairs={{0,8},{8,0},{16,24},{24,16},{32,40},{40,32},{48,56},{56,48},{64,72... | collective-permute-start | bytes 786440 | tf_op jit(solution)/shard_map/ppermute | solution.py:139
  24.3 1.4 %collective-permute-done.1 = f32[8,32,256]{2,1,0:T(8,128)S(1)} collective-permute-done((f32[8,32,256]{2,1,0:T(8,128)S(1)}, f32[8,32,256]{2,1,0:T(8,128)S(1)}, u32[]{:S(2)}, u32[]{:S(2)}) %collective-permute-start.1) | collective-permute-done | bytes 262176 | tf_op jit(solution)/shard_map/ppermute | solution.py:139
  25.8 4.3 %collective-permute-start.2 = (s32[2,16]{1,0:T(2,128)S(1)}, s32[2,16]{1,0:T(2,128)S(1)}, u32[]{:S(2)}, u32[]{:S(2)}) collective-permute-start(s32[2,16]{1,0:T(2,128)S(1)} %pad_add_fusion.1), channel_id=1, source_target_pairs={{0,256},{8,264},{16,272},{24,280},{32,288},{40,296},{48,304},{56,3... | collective-permute-start | bytes 392 | tf_op jit(solution)/shard_map/ppermute | solution.py:143
  30.2 3.1 %collective-permute-start.4 = (f32[16,32,256]{2,1,0:T(8,128)S(1)}, f32[16,32,256]{2,1,0:T(8,128)S(1)}, u32[]{:S(2)}, u32[]{:S(2)}) collective-permute-start(f32[16,32,256]{2,1,0:T(8,128)S(1)} %pad_maximum_fusion), channel_id=1, source_target_pairs={{0,1},{1,2},{2,3},{3,4},{4,5},{5,6},{6,7},{7,0},{8,15},{9,8},{10,9... | collective-permute-start | bytes 1572872 | tf_op jit(solution)/shard_map/ppermute | solution.py:172
  33.3 0.6 gather_fusion
  33.9 0.2 convert_reduce_fusion.1
  34.2 0.6 subtract_reduce_fusion
  35.6 0.2 select_reduce_fusion
  35.9 4.5 %collective-permute-done.4.refs_1_ = f32[16,32,256]{2,1,0:T(8,128)S(1)} collective-permute-done((f32[16,32,256]{2,1,0:T(8,128)S(1)}, f32[16,32,256]{2,1,0:T(8,128)S(1)}, u32[]{:S(2)}, u32[]{:S(2)}) %collective-permute-start.4) | collective-permute-done | bytes 524320 | tf_op jit(solution)/shard_map/ppermute | solution.py:172
  40.4 2.3 %all-to-all-done.1 = f32[8,4,32,256]{3,2,1,0:T(8,128)S(1)} async-done(((f32[8,4,32,256]{3,2,1,0:T(8,128)}), f32[8,4,32,256]{3,2,1,0:T(8,128)S(1)}, u32[]{:S(2)}, u32[]{:S(2)}) %all-to-all-start.1) | async-done | bytes 1048608 | tf_op jit(solution)/shard_map/all_to_all | solution.py:168
  42.8 2.4 %collective-permute-start.6 = (f32[32,32,256]{2,1,0:T(8,128)S(1)}, f32[32,32,256]{2,1,0:T(8,128)S(1)}, u32[]{:S(2)}, u32[]{:S(2)}) collective-permute-start(f32[32,32,256]{2,1,0:T(8,128)S(1)} %bitcast.14), channel_id=1, source_target_pairs={{0,8},{8,0},{16,24},{24,16},{32,40},{40,32},{48,56},{56,48},{64,72... | collective-permute-start | bytes 3145736 | tf_op jit(solution)/shard_map/ppermute | solution.py:139
  45.3 5.1 %collective-permute-start.5 = (f32[16,32,256]{2,1,0:T(8,128)S(1)}, f32[16,32,256]{2,1,0:T(8,128)}, u32[]{:S(2)}, u32[]{:S(2)}) collective-permute-start(f32[16,32,256]{2,1,0:T(8,128)S(1)} %collective-permute-done.4.refs_1_), channel_id=1, source_target_pairs={{0,1},{1,2},{2,3},{3,4},{4,5},{5,6},{6,7},{7,0},{8,15},{9,8},{10,9... | collective-permute-start | bytes 1572872 | tf_op jit(solution)/shard_map/ppermute | solution.py:172
  50.4 0.2 convert_reduce_fusion.4
  50.7 2.0 %shard_map.70 = (f32[4,12,32,256]{3,2,1,0:T(8,128)}, f32[4,4,32,256]{3,2,1,0:T(8,128)}) custom-call(s32[64]{0:T(128)S(1)} %reshape.130.place_ref, f32[32,32,256]{2,1,0:T(8,128)S(1)} %bitcast.15, f32[32,32,256]{2,1,0:T(8,128)S(1)} %collective-permute-done.6.twins_ref), custom_call_target="tpu_custom_call" | custom-call | bytes 4000000 | tf_op jit(solution)/shard_map/pallas_call | solution.py:197
  52.7 4.3 %all-to-all-start.2 = ((f32[4,12,32,256]{3,2,1,0:T(8,128)}), f32[4,12,32,256]{3,2,1,0:T(8,128)}, u32[]{:S(2)}, u32[]{:S(2)}) async-start(f32[4,12,32,256]{3,2,1,0:T(8,128)} %get-tuple-element.39), calls=%async_computation.2 | async-start | bytes 3145728 | tf_op jit(solution)/shard_map/all_to_all | solution.py:206
  57.1 0.7 iota_reduce_fusion
  57.8 3.8 %collective-permute-start.7 = (f32[16,32,256]{2,1,0:T(8,128)}, f32[16,32,256]{2,1,0:T(8,128)S(1)}, u32[]{:S(2)}, u32[]{:S(2)}) collective-permute-start(f32[16,32,256]{2,1,0:T(8,128)} %collective-permute-done.5.refs_2_), channel_id=1, source_target_pairs={{0,1},{1,2},{2,3},{3,4},{4,5},{5,6},{6,7},{7,0},{8,15},{9,8},{10,9... | collective-permute-start | bytes 1572872 | tf_op jit(solution)/shard_map/ppermute | solution.py:172
  61.7 1.9 %collective-permute-start.8 = (f32[16,32,256]{2,1,0:T(8,128)}, f32[16,32,256]{2,1,0:T(8,128)S(1)}, u32[]{:S(2)}, u32[]{:S(2)}) collective-permute-start(f32[16,32,256]{2,1,0:T(8,128)} %copy-done.3), channel_id=1, source_target_pairs={{0,8},{8,0},{16,24},{24,16},{32,40},{40,32},{48,56},{56,48},{64,72... | collective-permute-start | bytes 1572872 | tf_op jit(solution)/shard_map/ppermute | solution.py:139
  63.6 2.4 %collective-permute-start.9 = (f32[16,32,256]{2,1,0:T(8,128)}, f32[16,32,256]{2,1,0:T(8,128)S(1)}, u32[]{:S(2)}, u32[]{:S(2)}) collective-permute-start(f32[16,32,256]{2,1,0:T(8,128)} %collective-permute-done.5.refs_2_), channel_id=1, source_target_pairs={{0,8},{8,0},{16,24},{24,16},{32,40},{40,32},{48,56},{56,48},{64,72... | collective-permute-start | bytes 1572872 | tf_op jit(solution)/shard_map/ppermute | solution.py:139
  66.0 2.3 %collective-permute-done.7.refs_3_ = f32[16,32,256]{2,1,0:T(8,128)S(1)} collective-permute-done((f32[16,32,256]{2,1,0:T(8,128)}, f32[16,32,256]{2,1,0:T(8,128)S(1)}, u32[]{:S(2)}, u32[]{:S(2)}) %collective-permute-start.7) | collective-permute-done | bytes 524320 | tf_op jit(solution)/shard_map/ppermute | solution.py:172
  68.3 4.0 %collective-permute-start.10 = (f32[16,32,256]{2,1,0:T(8,128)S(1)}, f32[16,32,256]{2,1,0:T(8,128)}, u32[]{:S(2)}, u32[]{:S(2)}) collective-permute-start(f32[16,32,256]{2,1,0:T(8,128)S(1)} %collective-permute-done.7.refs_3_), channel_id=1, source_target_pairs={{0,8},{8,0},{16,24},{24,16},{32,40},{40,32},{48,56},{56,48},{64,72... | collective-permute-start | bytes 1572872 | tf_op jit(solution)/shard_map/ppermute | solution.py:139
  72.4 0.8 copy-done.4
  73.2 0.8 collective-permute-done.10.refs_6_
  74.0 1.9 %shard_map.71.whole_ref = bf16[2,8,256,256]{3,2,1,0:T(8,128)(2,1)S(1)} custom-call(s32[8]{0:T(128)S(1)} %fusion.12.start_ref, f32[9,32,256]{2,1,0:T(8,128)S(1)} %shard_map.68.staged_ref, f32[8,32,256]{2,1,0:T(8,128)} %copy-done.2, f32[16,32,256]{2,1,0:T(8,128)} %copy-done.3, f32[16,32,256]{2,1,0:T(8,128)} %collective-permute-done.5.refs_2_, ...), custom_call_target="tpu_custom_call" | custom-call | bytes 4000000 | tf_op jit(solution)/shard_map/pallas_call | solution.py:211
  75.9 1.0 %all-to-all-done.2 = f32[4,12,32,256]{3,2,1,0:T(8,128)} async-done(((f32[4,12,32,256]{3,2,1,0:T(8,128)}), f32[4,12,32,256]{3,2,1,0:T(8,128)}, u32[]{:S(2)}, u32[]{:S(2)}) %all-to-all-start.2) | async-done | bytes 1572896 | tf_op jit(solution)/shard_map/all_to_all | solution.py:206
  77.0 3.2 %shard_map.72 = (f32[8,32,256]{2,1,0:T(8,128)}, f32[8,32,256]{2,1,0:T(8,128)S(1)}) custom-call(s32[64]{0:T(128)S(1)} %fusion.11.pick_ref, s32[1]{0:T(128)} %bitcast.7.mine_ref, f32[48,32,256]{2,1,0:T(8,128)} %bitcast.8.fetched_ref, f32[4,32,256]{2,1,0:T(8,128)S(1)} %get-tuple-element.53.extra_ref, f32[9,32,256]{2,1,0:T(8,128)S(1)} %shard_map.68.staged_ref, ...), custom_call_target="tpu_custom_call" | custom-call | flops 1000000000 | bytes 5000000 | tf_op jit(solution)/shard_map/pallas_call | solution.py:228
  80.2 16.5 %all_to_all.19 = f32[8,32,256]{2,1,0:T(8,128)S(1)} all-to-all(f32[8,32,256]{2,1,0:T(8,128)S(1)} %get-tuple-element.50), channel_id=1, replica_groups=mesh['snode'=64,'grp'=8] {'grp'}, dimensions={0} | all-to-all | bytes 524288 | tf_op jit(solution)/shard_map/all_to_all | solution.py:240
  96.7 0.6 reduce_sum.69
  (44 shorter events, 1.1 us)
Async XLA Ops:
  0.6 12.9 %copy-start.5 = (s32[1,8,8]{2,1,0:T(8,128)S(1)}, s32[1,8,8]{2,1,0:T(8,128)}, u32[]{:S(2)}) copy-start(s32[1,8,8]{2,1,0:T(8,128)} %param.9) | copy-start | bytes 772
  0.6 16.5 %copy-start = (f32[1,8,32,256]{3,2,1,0:T(8,128)S(1)}, f32[1,8,32,256]{3,2,1,0:T(8,128)}, u32[]{:S(2)}) copy-start(f32[1,8,32,256]{3,2,1,0:T(8,128)} %param.8) | copy-start | bytes 786436
  2.7 42.5 %copy-start.1 = (f32[1,32,256]{2,1,0:T(8,128)S(1)}, f32[1,32,256]{2,1,0:T(8,128)}, u32[]{:S(2)}) copy-start(f32[1,32,256]{2,1,0:T(8,128)} %param.10) | copy-start | bytes 98308
  2.7 40.1 %all-to-all-start.1 = ((f32[8,4,32,256]{3,2,1,0:T(8,128)}), f32[8,4,32,256]{3,2,1,0:T(8,128)S(1)}, u32[]{:S(2)}, u32[]{:S(2)}) async-start(f32[8,4,32,256]{3,2,1,0:T(8,128)} %shard_map.69), calls=%async_computation.1 | async-start | bytes 2097152 | tf_op jit(solution)/shard_map/all_to_all | solution.py:168
  14.1 8.3 %collective-permute-start = (s32[16]{0:T(128)S(1)}, s32[16]{0:T(128)S(1)}, u32[]{:S(2)}, u32[]{:S(2)}) collective-permute-start(s32[16]{0:T(128)S(1)} %select_reduce_fusion.1), channel_id=1, source_target_pairs={{0,128},{8,136},{16,144},{24,152},{32,160},{40,168},{48,176},{56,1... | collective-permute-start | bytes 200 | tf_op jit(solution)/shard_map/ppermute | solution.py:138
  17.2 12.9 %collective-permute-start.3 = (f32[8,32,256]{2,1,0:T(8,128)S(1)}, f32[8,32,256]{2,1,0:T(8,128)S(1)}, u32[]{:S(2)}, u32[]{:S(2)}) collective-permute-start(f32[8,32,256]{2,1,0:T(8,128)S(1)} %bitcast.16), channel_id=1, source_target_pairs={{0,1},{1,2},{2,3},{3,4},{4,5},{5,6},{6,7},{7,0},{8,15},{9,8},{10,9... | collective-permute-start | bytes 786440 | tf_op jit(solution)/shard_map/ppermute | solution.py:172
  22.4 3.4 %collective-permute-start.1 = (f32[8,32,256]{2,1,0:T(8,128)S(1)}, f32[8,32,256]{2,1,0:T(8,128)S(1)}, u32[]{:S(2)}, u32[]{:S(2)}) collective-permute-start(f32[8,32,256]{2,1,0:T(8,128)S(1)} %bitcast.17), channel_id=1, source_target_pairs={{0,8},{8,0},{16,24},{24,16},{32,40},{40,32},{48,56},{56,48},{64,72... | collective-permute-start | bytes 786440 | tf_op jit(solution)/shard_map/ppermute | solution.py:139
  25.8 7.5 %collective-permute-start.2 = (s32[2,16]{1,0:T(2,128)S(1)}, s32[2,16]{1,0:T(2,128)S(1)}, u32[]{:S(2)}, u32[]{:S(2)}) collective-permute-start(s32[2,16]{1,0:T(2,128)S(1)} %pad_add_fusion.1), channel_id=1, source_target_pairs={{0,256},{8,264},{16,272},{24,280},{32,288},{40,296},{48,304},{56,3... | collective-permute-start | bytes 392 | tf_op jit(solution)/shard_map/ppermute | solution.py:143
  30.1 12.6 %copy-start.2 = (f32[8,32,256]{2,1,0:T(8,128)}, f32[8,32,256]{2,1,0:T(8,128)S(1)}, u32[]{:S(2)}) copy-start(f32[8,32,256]{2,1,0:T(8,128)S(1)} %collective-permute-done.3.refs_0_) | copy-start | bytes 786436
  30.2 10.2 %collective-permute-start.4 = (f32[16,32,256]{2,1,0:T(8,128)S(1)}, f32[16,32,256]{2,1,0:T(8,128)S(1)}, u32[]{:S(2)}, u32[]{:S(2)}) collective-permute-start(f32[16,32,256]{2,1,0:T(8,128)S(1)} %pad_maximum_fusion), channel_id=1, source_target_pairs={{0,1},{1,2},{2,3},{3,4},{4,5},{5,6},{6,7},{7,0},{8,15},{9,8},{10,9... | collective-permute-start | bytes 1572872 | tf_op jit(solution)/shard_map/ppermute | solution.py:172
  40.4 17.4 %copy-start.3 = (f32[16,32,256]{2,1,0:T(8,128)}, f32[16,32,256]{2,1,0:T(8,128)S(1)}, u32[]{:S(2)}) copy-start(f32[16,32,256]{2,1,0:T(8,128)S(1)} %collective-permute-done.4.refs_1_) | copy-start | bytes 1572868
  42.8 7.9 %collective-permute-start.6 = (f32[32,32,256]{2,1,0:T(8,128)S(1)}, f32[32,32,256]{2,1,0:T(8,128)S(1)}, u32[]{:S(2)}, u32[]{:S(2)}) collective-permute-start(f32[32,32,256]{2,1,0:T(8,128)S(1)} %bitcast.14), channel_id=1, source_target_pairs={{0,8},{8,0},{16,24},{24,16},{32,40},{40,32},{48,56},{56,48},{64,72... | collective-permute-start | bytes 3145736 | tf_op jit(solution)/shard_map/ppermute | solution.py:139
  45.3 12.5 %collective-permute-start.5 = (f32[16,32,256]{2,1,0:T(8,128)S(1)}, f32[16,32,256]{2,1,0:T(8,128)}, u32[]{:S(2)}, u32[]{:S(2)}) collective-permute-start(f32[16,32,256]{2,1,0:T(8,128)S(1)} %collective-permute-done.4.refs_1_), channel_id=1, source_target_pairs={{0,1},{1,2},{2,3},{3,4},{4,5},{5,6},{6,7},{7,0},{8,15},{9,8},{10,9... | collective-permute-start | bytes 1572872 | tf_op jit(solution)/shard_map/ppermute | solution.py:172
  52.7 19.7 %copy-start.6 = (s32[8]{0:T(128)S(1)}, s32[8]{0:T(128)}, u32[]{:S(2)}) copy-start(s32[8]{0:T(128)} %constant.159.clone) | copy-start | bytes 100
  52.7 24.3 %all-to-all-start.2 = ((f32[4,12,32,256]{3,2,1,0:T(8,128)}), f32[4,12,32,256]{3,2,1,0:T(8,128)}, u32[]{:S(2)}, u32[]{:S(2)}) async-start(f32[4,12,32,256]{3,2,1,0:T(8,128)} %get-tuple-element.39), calls=%async_computation.2 | async-start | bytes 3145728 | tf_op jit(solution)/shard_map/all_to_all | solution.py:206
  57.8 10.5 %collective-permute-start.7 = (f32[16,32,256]{2,1,0:T(8,128)}, f32[16,32,256]{2,1,0:T(8,128)S(1)}, u32[]{:S(2)}, u32[]{:S(2)}) collective-permute-start(f32[16,32,256]{2,1,0:T(8,128)} %collective-permute-done.5.refs_2_), channel_id=1, source_target_pairs={{0,1},{1,2},{2,3},{3,4},{4,5},{5,6},{6,7},{7,0},{8,15},{9,8},{10,9... | collective-permute-start | bytes 1572872 | tf_op jit(solution)/shard_map/ppermute | solution.py:172
  61.7 10.7 %collective-permute-start.8 = (f32[16,32,256]{2,1,0:T(8,128)}, f32[16,32,256]{2,1,0:T(8,128)S(1)}, u32[]{:S(2)}, u32[]{:S(2)}) collective-permute-start(f32[16,32,256]{2,1,0:T(8,128)} %copy-done.3), channel_id=1, source_target_pairs={{0,8},{8,0},{16,24},{24,16},{32,40},{40,32},{48,56},{56,48},{64,72... | collective-permute-start | bytes 1572872 | tf_op jit(solution)/shard_map/ppermute | solution.py:139
  63.6 8.8 %collective-permute-start.9 = (f32[16,32,256]{2,1,0:T(8,128)}, f32[16,32,256]{2,1,0:T(8,128)S(1)}, u32[]{:S(2)}, u32[]{:S(2)}) collective-permute-start(f32[16,32,256]{2,1,0:T(8,128)} %collective-permute-done.5.refs_2_), channel_id=1, source_target_pairs={{0,8},{8,0},{16,24},{24,16},{32,40},{40,32},{48,56},{56,48},{64,72... | collective-permute-start | bytes 1572872 | tf_op jit(solution)/shard_map/ppermute | solution.py:139
  68.3 5.7 %collective-permute-start.10 = (f32[16,32,256]{2,1,0:T(8,128)S(1)}, f32[16,32,256]{2,1,0:T(8,128)}, u32[]{:S(2)}, u32[]{:S(2)}) collective-permute-start(f32[16,32,256]{2,1,0:T(8,128)S(1)} %collective-permute-done.7.refs_3_), channel_id=1, source_target_pairs={{0,8},{8,0},{16,24},{24,16},{32,40},{40,32},{48,56},{56,48},{64,72... | collective-permute-start | bytes 1572872 | tf_op jit(solution)/shard_map/ppermute | solution.py:139
  72.4 0.8 copy-start.4

commit v6 on v5

--- a/solution.py
+++ b/solution.py
@@ -22,7 +22,7 @@
 ]
 X_ONE = [(node(x, z, c), node(x ^ 1, z, c)) for x, z, c in EVERY]
 X_TWO = [(node(x, z, c), node(x ^ 2, z, c)) for x, z, c in EVERY]
-Z_LINES = [[node(x, z, c) for z in range(NZ)] for x in range(NX) for c in range(NC)]
+Z_LINES = [[node(x, z, c) for z in reversed(range(NZ))] for x in range(NX) for c in range(NC)]
 X_LINES = [[node(x, z, c) for x in range(NX)] for z in range(NZ) for c in range(NC)]
 VMEM = pl.BlockSpec(memory_space=pltpu.VMEM)
 HBM = pl.BlockSpec(memory_space=pltpu.HBM)
@@ -150,7 +150,7 @@
     asked = jnp.sum(jnp.where(at[:, :, None] == order, lists[:, None, :], 0), axis=2)
     many = jnp.max(begins[:, 1:] - begins[:, :-1]) > FEW
     owner, k = asked // held, asked % held
-    place = owner // NC % NZ * held + k + jnp.where(owner % NC == c, 0, NZ * held)
+    place = (NZ - 1 - owner // NC % NZ) * held + k + jnp.where(owner % NC == c, 0, NZ * held)
     place = jnp.where((owner // (NC * NZ) == x) & (at < SLOTS), place, 0)
 
     copies = pl.pallas_call(

time: 98.3 us -> 98.5 us (level)
  starting transfers between devices: 52.5 us -> 55.3 us
  waiting for transfers between devices: 12.4 us -> 10.3 us
    ppermute x5, starting transfers between devices: 12.7 us -> 17.1 us  [per_device(): twin = lambda v: lax.ppermute(v, 'snode', TWIN)]
    ppermute x4, starting transfers between devices: 17.1 us -> 13.3 us  [per_device(): on = lambda v: lax.ppermute(v, ('snode', 'grp'), Y_ROUND)]
    all_to_all x1, waiting for transfers between devices: 2.32 us -> 0.01 us  [per_device(): lax.all_to_all(copies, 'snode', split_axis=0, concat_axis=0, tiled=True,...]
    all_to_all x1, starting transfers between devices: 10.9 us -> 13.1 us  [per_device(): lax.all_to_all(copies, 'snode', split_axis=0, concat_axis=0, tiled=True,...]
    ppermute x4, waiting for transfers between devices: 6.84 us -> 8.01 us  [per_device(): on = lambda v: lax.ppermute(v, ('snode', 'grp'), Y_ROUND)]
    all_to_all x1, waiting for transfers between devices: 1.03 us -> 0.01 us  [per_device(): lax.all_to_all(v, 'snode', split_axis=0, concat_axis=0, tiled=True, axis_...]
  transfers between devices with their start and end apart: 13 -> 13, of which waited for: 6 -> 5; matrix products, arithmetic and copies ran while one was open for 4% -> 4% of each run, Pallas kernels for 4% -> 4%
where the time goes in v6:
time: 98.5 us; the launch traced here: 97.8 us
  starting transfers between devices  55.3 us (56%)
  blocking collectives  16.2 us (16%)
  waiting for transfers between devices  10.3 us (10%)
  Pallas kernels  9.16 us (9%)
  other arithmetic  3.52 us (4%)
  between operations  1.68 us (2%)
  local copies, waits for them, and re-layouts  1.57 us (2%)
    ppermute x5, starting transfers between devices, per_device(): twin = lambda v: lax.ppermute(v, 'snode', TWIN)  17.1 us
    all_to_all x1, blocking collectives, per_device(): lax.all_to_all(update, 'grp', split_axis=0, concat_axis=0, tiled=True)  16.2 us
    ppermute x4, starting transfers between devices, per_device(): on = lambda v: lax.ppermute(v, ('snode', 'grp'), Y_ROUND)  13.3 us
    all_to_all x1, starting transfers between devices, per_device(): lax.all_to_all(copies, 'snode', split_axis=0, concat_axis=0, tiled=True,...  13.1 us
    ppermute x4, waiting for transfers between devices, per_device(): on = lambda v: lax.ppermute(v, ('snode', 'grp'), Y_ROUND)  8.01 us
    ppermute x1, starting transfers between devices, per_device(): lists = jnp.concatenate([pair, lax.ppermute(pair, 'snode', X_TWO)])  4.35 us
    all_to_all x1, starting transfers between devices, per_device(): lax.all_to_all(v, 'snode', split_axis=0, concat_axis=0, tiled=True, axis_...  4.35 us
    pallas_call x1, Pallas kernels, per_device(): pl.pallas_call(products, out_shape=(pltpu.HBM((kcount,) + block, jnp.floa...  3.22 us
  transfers between devices with their start and end apart: 13, of which 5 were waited for; matrix products, arithmetic and copies ran while one was open for 4% of the time, Pallas kernels for 4%

profile of v6, /device:TPU:1, one launch (start us, length us, event | category | flops | bytes accessed | tf_op | source)
XLA Modules:
  0.0 97.8 jit_solution(10614870566386761685)
XLA Ops:
  0.6 2.0 %shard_map.69 = f32[8,4,32,256]{3,2,1,0:T(8,128)} custom-call(f32[4,32,256]{2,1,0:T(8,128)} %block_ref.1), custom_call_target="tpu_custom_call" | custom-call | tf_op jit(solution)/shard_map/pallas_call | solution.py:156
  2.7 13.1 %all-to-all-start.1 = ((f32[8,4,32,256]{3,2,1,0:T(8,128)}), f32[8,4,32,256]{3,2,1,0:T(8,128)S(1)}, u32[]{:S(2)}, u32[]{:S(2)}) async-start(f32[8,4,32,256]{3,2,1,0:T(8,128)} %shard_map.69), calls=%async_computation.1 | async-start | bytes 2097152 | tf_op jit(solution)/shard_map/all_to_all | solution.py:168
  16.0 0.2 convert_reduce_fusion
  16.3 3.1 %collective-permute-start = (s32[16]{0:T(128)S(1)}, s32[16]{0:T(128)S(1)}, u32[]{:S(2)}, u32[]{:S(2)}) collective-permute-start(s32[16]{0:T(128)S(1)} %select_reduce_fusion.1), channel_id=1, source_target_pairs={{0,128},{8,136},{16,144},{24,152},{32,160},{40,168},{48,176},{56,1... | collective-permute-start | bytes 200 | tf_op jit(solution)/shard_map/ppermute | solution.py:138
  19.4 5.1 %collective-permute-start.3 = (f32[8,32,256]{2,1,0:T(8,128)S(1)}, f32[8,32,256]{2,1,0:T(8,128)S(1)}, u32[]{:S(2)}, u32[]{:S(2)}) collective-permute-start(f32[8,32,256]{2,1,0:T(8,128)S(1)} %bitcast.16), channel_id=1, source_target_pairs={{0,1},{1,2},{2,3},{3,4},{4,5},{5,6},{6,7},{7,0},{8,15},{9,8},{10,9... | collective-permute-start | bytes 786440 | tf_op jit(solution)/shard_map/ppermute | solution.py:172
  24.6 1.9 %collective-permute-start.1 = (f32[8,32,256]{2,1,0:T(8,128)S(1)}, f32[8,32,256]{2,1,0:T(8,128)S(1)}, u32[]{:S(2)}, u32[]{:S(2)}) collective-permute-start(f32[8,32,256]{2,1,0:T(8,128)S(1)} %bitcast.17), channel_id=1, source_target_pairs={{0,8},{8,0},{16,24},{24,16},{32,40},{40,32},{48,56},{56,48},{64,72... | collective-permute-start | bytes 786440 | tf_op jit(solution)/shard_map/ppermute | solution.py:139
  26.6 1.4 %collective-permute-done.1 = f32[8,32,256]{2,1,0:T(8,128)S(1)} collective-permute-done((f32[8,32,256]{2,1,0:T(8,128)S(1)}, f32[8,32,256]{2,1,0:T(8,128)S(1)}, u32[]{:S(2)}, u32[]{:S(2)}) %collective-permute-start.1) | collective-permute-done | bytes 262176 | tf_op jit(solution)/shard_map/ppermute | solution.py:139
  28.0 4.3 %collective-permute-start.2 = (s32[2,16]{1,0:T(2,128)S(1)}, s32[2,16]{1,0:T(2,128)S(1)}, u32[]{:S(2)}, u32[]{:S(2)}) collective-permute-start(s32[2,16]{1,0:T(2,128)S(1)} %pad_add_fusion.1), channel_id=1, source_target_pairs={{0,256},{8,264},{16,272},{24,280},{32,288},{40,296},{48,304},{56,3... | collective-permute-start | bytes 392 | tf_op jit(solution)/shard_map/ppermute | solution.py:143
  32.4 3.1 %collective-permute-start.4 = (f32[16,32,256]{2,1,0:T(8,128)S(1)}, f32[16,32,256]{2,1,0:T(8,128)S(1)}, u32[]{:S(2)}, u32[]{:S(2)}) collective-permute-start(f32[16,32,256]{2,1,0:T(8,128)S(1)} %pad_maximum_fusion), channel_id=1, source_target_pairs={{0,1},{1,2},{2,3},{3,4},{4,5},{5,6},{6,7},{7,0},{8,15},{9,8},{10,9... | collective-permute-start | bytes 1572872 | tf_op jit(solution)/shard_map/ppermute | solution.py:172
  35.6 0.6 gather_fusion
  36.1 0.2 convert_reduce_fusion.1
  36.4 0.6 subtract_reduce_fusion
  37.9 0.2 select_reduce_fusion
  38.2 4.5 %collective-permute-done.4.refs_1_ = f32[16,32,256]{2,1,0:T(8,128)S(1)} collective-permute-done((f32[16,32,256]{2,1,0:T(8,128)S(1)}, f32[16,32,256]{2,1,0:T(8,128)S(1)}, u32[]{:S(2)}, u32[]{:S(2)}) %collective-permute-start.4) | collective-permute-done | bytes 524320 | tf_op jit(solution)/shard_map/ppermute | solution.py:172
  42.7 4.4 %collective-permute-start.6 = (f32[32,32,256]{2,1,0:T(8,128)S(1)}, f32[32,32,256]{2,1,0:T(8,128)S(1)}, u32[]{:S(2)}, u32[]{:S(2)}) collective-permute-start(f32[32,32,256]{2,1,0:T(8,128)S(1)} %bitcast.14), channel_id=1, source_target_pairs={{0,8},{8,0},{16,24},{24,16},{32,40},{40,32},{48,56},{56,48},{64,72... | collective-permute-start | bytes 3145736 | tf_op jit(solution)/shard_map/ppermute | solution.py:139
  47.2 2.1 %collective-permute-start.5 = (f32[16,32,256]{2,1,0:T(8,128)S(1)}, f32[16,32,256]{2,1,0:T(8,128)}, u32[]{:S(2)}, u32[]{:S(2)}) collective-permute-start(f32[16,32,256]{2,1,0:T(8,128)S(1)} %collective-permute-done.4.refs_1_), channel_id=1, source_target_pairs={{0,1},{1,2},{2,3},{3,4},{4,5},{5,6},{6,7},{7,0},{8,15},{9,8},{10,9... | collective-permute-start | bytes 1572872 | tf_op jit(solution)/shard_map/ppermute | solution.py:172
  49.4 0.2 convert_reduce_fusion.4
  49.6 2.0 %shard_map.70 = (f32[4,12,32,256]{3,2,1,0:T(8,128)}, f32[4,4,32,256]{3,2,1,0:T(8,128)}) custom-call(s32[64]{0:T(128)S(1)} %reshape.130.place_ref, f32[32,32,256]{2,1,0:T(8,128)S(1)} %bitcast.15, f32[32,32,256]{2,1,0:T(8,128)S(1)} %collective-permute-done.6.twins_ref), custom_call_target="tpu_custom_call" | custom-call | bytes 4000000 | tf_op jit(solution)/shard_map/pallas_call | solution.py:197
  51.6 4.3 %all-to-all-start.2 = ((f32[4,12,32,256]{3,2,1,0:T(8,128)}), f32[4,12,32,256]{3,2,1,0:T(8,128)}, u32[]{:S(2)}, u32[]{:S(2)}) async-start(f32[4,12,32,256]{3,2,1,0:T(8,128)} %get-tuple-element.39), calls=%async_computation.2 | async-start | bytes 3145728 | tf_op jit(solution)/shard_map/all_to_all | solution.py:206
  56.0 0.7 iota_reduce_fusion
  56.7 0.8 collective-permute-done.5.refs_2_
  57.6 3.0 %collective-permute-start.7 = (f32[16,32,256]{2,1,0:T(8,128)}, f32[16,32,256]{2,1,0:T(8,128)S(1)}, u32[]{:S(2)}, u32[]{:S(2)}) collective-permute-start(f32[16,32,256]{2,1,0:T(8,128)} %collective-permute-done.5.refs_2_), channel_id=1, source_target_pairs={{0,1},{1,2},{2,3},{3,4},{4,5},{5,6},{6,7},{7,0},{8,15},{9,8},{10,9... | collective-permute-start | bytes 1572872 | tf_op jit(solution)/shard_map/ppermute | solution.py:172
  60.6 2.9 %collective-permute-start.8 = (f32[16,32,256]{2,1,0:T(8,128)}, f32[16,32,256]{2,1,0:T(8,128)S(1)}, u32[]{:S(2)}, u32[]{:S(2)}) collective-permute-start(f32[16,32,256]{2,1,0:T(8,128)} %copy-done.3), channel_id=1, source_target_pairs={{0,8},{8,0},{16,24},{24,16},{32,40},{40,32},{48,56},{56,48},{64,72... | collective-permute-start | bytes 1572872 | tf_op jit(solution)/shard_map/ppermute | solution.py:139
  63.5 1.9 %collective-permute-start.9 = (f32[16,32,256]{2,1,0:T(8,128)}, f32[16,32,256]{2,1,0:T(8,128)S(1)}, u32[]{:S(2)}, u32[]{:S(2)}) collective-permute-start(f32[16,32,256]{2,1,0:T(8,128)} %collective-permute-done.5.refs_2_), channel_id=1, source_target_pairs={{0,8},{8,0},{16,24},{24,16},{32,40},{40,32},{48,56},{56,48},{64,72... | collective-permute-start | bytes 1572872 | tf_op jit(solution)/shard_map/ppermute | solution.py:139
  65.4 2.7 %collective-permute-done.7.refs_3_ = f32[16,32,256]{2,1,0:T(8,128)S(1)} collective-permute-done((f32[16,32,256]{2,1,0:T(8,128)}, f32[16,32,256]{2,1,0:T(8,128)S(1)}, u32[]{:S(2)}, u32[]{:S(2)}) %collective-permute-start.7) | collective-permute-done | bytes 524320 | tf_op jit(solution)/shard_map/ppermute | solution.py:172
  68.1 5.9 %collective-permute-start.10 = (f32[16,32,256]{2,1,0:T(8,128)S(1)}, f32[16,32,256]{2,1,0:T(8,128)}, u32[]{:S(2)}, u32[]{:S(2)}) collective-permute-start(f32[16,32,256]{2,1,0:T(8,128)S(1)} %collective-permute-done.7.refs_3_), channel_id=1, source_target_pairs={{0,8},{8,0},{16,24},{24,16},{32,40},{40,32},{48,56},{56,48},{64,72... | collective-permute-start | bytes 1572872 | tf_op jit(solution)/shard_map/ppermute | solution.py:139
  74.1 0.8 copy-done.4
  74.9 0.8 collective-permute-done.10.refs_6_
  75.7 1.9 %shard_map.71.whole_ref = bf16[2,8,256,256]{3,2,1,0:T(8,128)(2,1)S(1)} custom-call(s32[8]{0:T(128)S(1)} %fusion.13.start_ref, f32[9,32,256]{2,1,0:T(8,128)S(1)} %shard_map.68.staged_ref, f32[8,32,256]{2,1,0:T(8,128)} %copy-done.2, f32[16,32,256]{2,1,0:T(8,128)} %copy-done.3, f32[16,32,256]{2,1,0:T(8,128)} %collective-permute-done.5.refs_2_, ...), custom_call_target="tpu_custom_call" | custom-call | bytes 4000000 | tf_op jit(solution)/shard_map/pallas_call | solution.py:211
  77.7 3.2 %shard_map.72 = (f32[8,32,256]{2,1,0:T(8,128)}, f32[8,32,256]{2,1,0:T(8,128)S(1)}) custom-call(s32[64]{0:T(128)S(1)} %fusion.12.pick_ref, s32[1]{0:T(128)} %bitcast.7.mine_ref, f32[48,32,256]{2,1,0:T(8,128)} %bitcast.8.fetched_ref, f32[4,32,256]{2,1,0:T(8,128)S(1)} %get-tuple-element.53.extra_ref, f32[9,32,256]{2,1,0:T(8,128)S(1)} %shard_map.68.staged_ref, ...), custom_call_target="tpu_custom_call" | custom-call | flops 1000000000 | bytes 5000000 | tf_op jit(solution)/shard_map/pallas_call | solution.py:228
  80.9 16.2 %all_to_all.19 = f32[8,32,256]{2,1,0:T(8,128)S(1)} all-to-all(f32[8,32,256]{2,1,0:T(8,128)S(1)} %get-tuple-element.50), channel_id=1, replica_groups=mesh['snode'=64,'grp'=8] {'grp'}, dimensions={0} | all-to-all | bytes 524288 | tf_op jit(solution)/shard_map/all_to_all | solution.py:240
  97.1 0.6 reduce_sum.69
  (44 shorter events, 1.0 us)
Async XLA Ops:
  0.6 15.2 %copy-start.5 = (s32[1,8,8]{2,1,0:T(8,128)S(1)}, s32[1,8,8]{2,1,0:T(8,128)}, u32[]{:S(2)}) copy-start(s32[1,8,8]{2,1,0:T(8,128)} %param.9) | copy-start | bytes 772
  0.6 18.8 %copy-start = (f32[1,8,32,256]{3,2,1,0:T(8,128)S(1)}, f32[1,8,32,256]{3,2,1,0:T(8,128)}, u32[]{:S(2)}) copy-start(f32[1,8,32,256]{3,2,1,0:T(8,128)} %param.8) | copy-start | bytes 786436
  2.7 44.4 %copy-start.1 = (f32[1,32,256]{2,1,0:T(8,128)S(1)}, f32[1,32,256]{2,1,0:T(8,128)}, u32[]{:S(2)}) copy-start(f32[1,32,256]{2,1,0:T(8,128)} %param.10) | copy-start | bytes 98308
  2.7 40.0 %all-to-all-start.1 = ((f32[8,4,32,256]{3,2,1,0:T(8,128)}), f32[8,4,32,256]{3,2,1,0:T(8,128)S(1)}, u32[]{:S(2)}, u32[]{:S(2)}) async-start(f32[8,4,32,256]{3,2,1,0:T(8,128)} %shard_map.69), calls=%async_computation.1 | async-start | bytes 2097152 | tf_op jit(solution)/shard_map/all_to_all | solution.py:168
  16.3 8.3 %collective-permute-start = (s32[16]{0:T(128)S(1)}, s32[16]{0:T(128)S(1)}, u32[]{:S(2)}, u32[]{:S(2)}) collective-permute-start(s32[16]{0:T(128)S(1)} %select_reduce_fusion.1), channel_id=1, source_target_pairs={{0,128},{8,136},{16,144},{24,152},{32,160},{40,168},{48,176},{56,1... | collective-permute-start | bytes 200 | tf_op jit(solution)/shard_map/ppermute | solution.py:138
  19.4 12.9 %collective-permute-start.3 = (f32[8,32,256]{2,1,0:T(8,128)S(1)}, f32[8,32,256]{2,1,0:T(8,128)S(1)}, u32[]{:S(2)}, u32[]{:S(2)}) collective-permute-start(f32[8,32,256]{2,1,0:T(8,128)S(1)} %bitcast.16), channel_id=1, source_target_pairs={{0,1},{1,2},{2,3},{3,4},{4,5},{5,6},{6,7},{7,0},{8,15},{9,8},{10,9... | collective-permute-start | bytes 786440 | tf_op jit(solution)/shard_map/ppermute | solution.py:172
  24.6 3.4 %collective-permute-start.1 = (f32[8,32,256]{2,1,0:T(8,128)S(1)}, f32[8,32,256]{2,1,0:T(8,128)S(1)}, u32[]{:S(2)}, u32[]{:S(2)}) collective-permute-start(f32[8,32,256]{2,1,0:T(8,128)S(1)} %bitcast.17), channel_id=1, source_target_pairs={{0,8},{8,0},{16,24},{24,16},{32,40},{40,32},{48,56},{56,48},{64,72... | collective-permute-start | bytes 786440 | tf_op jit(solution)/shard_map/ppermute | solution.py:139
  28.0 7.5 %collective-permute-start.2 = (s32[2,16]{1,0:T(2,128)S(1)}, s32[2,16]{1,0:T(2,128)S(1)}, u32[]{:S(2)}, u32[]{:S(2)}) collective-permute-start(s32[2,16]{1,0:T(2,128)S(1)} %pad_add_fusion.1), channel_id=1, source_target_pairs={{0,256},{8,264},{16,272},{24,280},{32,288},{40,296},{48,304},{56,3... | collective-permute-start | bytes 392 | tf_op jit(solution)/shard_map/ppermute | solution.py:143
  32.4 10.3 %copy-start.2 = (f32[8,32,256]{2,1,0:T(8,128)}, f32[8,32,256]{2,1,0:T(8,128)S(1)}, u32[]{:S(2)}) copy-start(f32[8,32,256]{2,1,0:T(8,128)S(1)} %collective-permute-done.3.refs_0_) | copy-start | bytes 786436
  32.4 10.2 %collective-permute-start.4 = (f32[16,32,256]{2,1,0:T(8,128)S(1)}, f32[16,32,256]{2,1,0:T(8,128)S(1)}, u32[]{:S(2)}, u32[]{:S(2)}) collective-permute-start(f32[16,32,256]{2,1,0:T(8,128)S(1)} %pad_maximum_fusion), channel_id=1, source_target_pairs={{0,1},{1,2},{2,3},{3,4},{4,5},{5,6},{6,7},{7,0},{8,15},{9,8},{10,9... | collective-permute-start | bytes 1572872 | tf_op jit(solution)/shard_map/ppermute | solution.py:172
  42.6 14.9 %copy-start.3 = (f32[16,32,256]{2,1,0:T(8,128)}, f32[16,32,256]{2,1,0:T(8,128)S(1)}, u32[]{:S(2)}) copy-start(f32[16,32,256]{2,1,0:T(8,128)S(1)} %collective-permute-done.4.refs_1_) | copy-start | bytes 1572868
  42.7 7.0 %collective-permute-start.6 = (f32[32,32,256]{2,1,0:T(8,128)S(1)}, f32[32,32,256]{2,1,0:T(8,128)S(1)}, u32[]{:S(2)}, u32[]{:S(2)}) collective-permute-start(f32[32,32,256]{2,1,0:T(8,128)S(1)} %bitcast.14), channel_id=1, source_target_pairs={{0,8},{8,0},{16,24},{24,16},{32,40},{40,32},{48,56},{56,48},{64,72... | collective-permute-start | bytes 3145736 | tf_op jit(solution)/shard_map/ppermute | solution.py:139
  47.2 10.3 %collective-permute-start.5 = (f32[16,32,256]{2,1,0:T(8,128)S(1)}, f32[16,32,256]{2,1,0:T(8,128)}, u32[]{:S(2)}, u32[]{:S(2)}) collective-permute-start(f32[16,32,256]{2,1,0:T(8,128)S(1)} %collective-permute-done.4.refs_1_), channel_id=1, source_target_pairs={{0,1},{1,2},{2,3},{3,4},{4,5},{5,6},{6,7},{7,0},{8,15},{9,8},{10,9... | collective-permute-start | bytes 1572872 | tf_op jit(solution)/shard_map/ppermute | solution.py:172
  51.6 22.4 %copy-start.6 = (s32[8]{0:T(128)S(1)}, s32[8]{0:T(128)}, u32[]{:S(2)}) copy-start(s32[8]{0:T(128)} %constant.160.clone) | copy-start | bytes 100
  51.6 26.0 %all-to-all-start.2 = ((f32[4,12,32,256]{3,2,1,0:T(8,128)}), f32[4,12,32,256]{3,2,1,0:T(8,128)}, u32[]{:S(2)}, u32[]{:S(2)}) async-start(f32[4,12,32,256]{3,2,1,0:T(8,128)} %get-tuple-element.39), calls=%async_computation.2 | async-start | bytes 3145728 | tf_op jit(solution)/shard_map/all_to_all | solution.py:206
  57.6 10.5 %collective-permute-start.7 = (f32[16,32,256]{2,1,0:T(8,128)}, f32[16,32,256]{2,1,0:T(8,128)S(1)}, u32[]{:S(2)}, u32[]{:S(2)}) collective-permute-start(f32[16,32,256]{2,1,0:T(8,128)} %collective-permute-done.5.refs_2_), channel_id=1, source_target_pairs={{0,1},{1,2},{2,3},{3,4},{4,5},{5,6},{6,7},{7,0},{8,15},{9,8},{10,9... | collective-permute-start | bytes 1572872 | tf_op jit(solution)/shard_map/ppermute | solution.py:172
  60.6 13.5 %collective-permute-start.8 = (f32[16,32,256]{2,1,0:T(8,128)}, f32[16,32,256]{2,1,0:T(8,128)S(1)}, u32[]{:S(2)}, u32[]{:S(2)}) collective-permute-start(f32[16,32,256]{2,1,0:T(8,128)} %copy-done.3), channel_id=1, source_target_pairs={{0,8},{8,0},{16,24},{24,16},{32,40},{40,32},{48,56},{56,48},{64,72... | collective-permute-start | bytes 1572872 | tf_op jit(solution)/shard_map/ppermute | solution.py:139
  63.5 10.6 %collective-permute-start.9 = (f32[16,32,256]{2,1,0:T(8,128)}, f32[16,32,256]{2,1,0:T(8,128)S(1)}, u32[]{:S(2)}, u32[]{:S(2)}) collective-permute-start(f32[16,32,256]{2,1,0:T(8,128)} %collective-permute-done.5.refs_2_), channel_id=1, source_target_pairs={{0,8},{8,0},{16,24},{24,16},{32,40},{40,32},{48,56},{56,48},{64,72... | collective-permute-start | bytes 1572872 | tf_op jit(solution)/shard_map/ppermute | solution.py:139
  68.1 7.6 %collective-permute-start.10 = (f32[16,32,256]{2,1,0:T(8,128)S(1)}, f32[16,32,256]{2,1,0:T(8,128)}, u32[]{:S(2)}, u32[]{:S(2)}) collective-permute-start(f32[16,32,256]{2,1,0:T(8,128)S(1)} %collective-permute-done.7.refs_3_), channel_id=1, source_target_pairs={{0,8},{8,0},{16,24},{24,16},{32,40},{40,32},{48,56},{56,48},{64,72... | collective-permute-start | bytes 1572872 | tf_op jit(solution)/shard_map/ppermute | solution.py:139
  74.1 0.8 copy-start.4

commit v7 on v5

--- a/solution.py
+++ b/solution.py
@@ -174,8 +174,6 @@
     passed = on(jnp.concatenate([lead, twins_own]))
     mine, place, many, passed = lax.optimization_barrier((mine, place, many, passed))
     twins = twin(mine)
-    counts = jnp.sum((distinct[None, :] // span == order[:NX, None]).astype(jnp.int32), axis=1)
-    fullest = jnp.argmax(counts).astype(jnp.int32)
     home = wanted // span
     place_there = slot - jnp.sum((distinct[None, :] < home[:, None] * span).astype(jnp.int32), axis=1)
     pick = jnp.where(place_there < FEW, home * FEW, NX * FEW - FEW) + place_there
@@ -187,7 +185,7 @@
         compiler_params=PARAMS,
     )(own, diag_factor[0])
     messages = [passed, on(passed)]
-    staged, pick, fullest, following = lax.optimization_barrier((staged, pick, fullest, messages[1]))
+    staged, pick, following = lax.optimization_barrier((staged, pick, messages[1]))
     messages.append(on(following))
     before, last, _ = lax.optimization_barrier((messages[0], messages[1], following))
     swapped = [twin(before), twin(last), twin(messages[2])]
@@ -217,13 +215,13 @@
         compiler_params=PARAMS,
         cost_estimate=pl.CostEstimate(flops=0, bytes_accessed=4_000_000, transcendentals=0),
     )(starts, in_vmem(staged), *pieces)
-    fetched, rest = lax.optimization_barrier((fetched, rest))
-    extra = lax.cond(
-        many,
-        lambda v: lax.dynamic_index_in_dim(over_x(v), fullest, 0, keepdims=False),
-        lambda v: jnp.zeros(v.shape[1:], v.dtype),
-        rest,
-    )
+    _, rest = lax.optimization_barrier((fetched, rest))
+
+    def more(rest, distinct):
+        counts = jnp.sum((distinct[None, :] // span == order[:NX, None]).astype(jnp.int32), axis=1)
+        return lax.dynamic_index_in_dim(over_x(rest), jnp.argmax(counts), 0, keepdims=False)
+
+    extra = lax.cond(many, more, lambda rest, _: jnp.zeros(rest.shape[1:], rest.dtype), rest, distinct)
 
     off, update = pl.pallas_call(
         products,

time: 98.3 us -> 98.1 us (level)
  starting transfers between devices: 52.5 us -> 53.5 us
  transfers between devices with their start and end apart: 13 -> 13, of which waited for: 6 -> 6; matrix products, arithmetic and copies ran while one was open for 4% -> 3% of each run, Pallas kernels for 4% -> 4%
where the time goes in v7:
time: 98.1 us; the launch traced here: 97.2 us
  starting transfers between devices  53.5 us (55%)
  blocking collectives  16.6 us (17%)
  waiting for transfers between devices  12.1 us (12%)
  Pallas kernels  9.17 us (9%)
  other arithmetic  2.6 us (3%)
  between operations  1.68 us (2%)
  local copies, waits for them, and re-layouts  1.57 us (2%)
    ppermute x4, starting transfers between devices, per_device(): on = lambda v: lax.ppermute(v, ('snode', 'grp'), Y_ROUND)  17.9 us
    all_to_all x1, blocking collectives, per_device(): lax.all_to_all(update, 'grp', split_axis=0, concat_axis=0, tiled=True)  16.6 us
    ppermute x5, starting transfers between devices, per_device(): twin = lambda v: lax.ppermute(v, 'snode', TWIN)  12.9 us
    all_to_all x1, starting transfers between devices, per_device(): lax.all_to_all(copies, 'snode', split_axis=0, concat_axis=0, tiled=True,...  10.9 us
    ppermute x4, waiting for transfers between devices, per_device(): on = lambda v: lax.ppermute(v, ('snode', 'grp'), Y_ROUND)  6.58 us
    ppermute x1, starting transfers between devices, per_device(): lists = jnp.concatenate([pair, lax.ppermute(pair, 'snode', X_TWO)])  4.35 us
    all_to_all x1, starting transfers between devices, per_device(): lax.all_to_all(v, 'snode', split_axis=0, concat_axis=0, tiled=True, axis_...  4.35 us
    pallas_call x1, Pallas kernels, per_device(): pl.pallas_call(products, out_shape=(pltpu.HBM((kcount,) + block, jnp.floa...  3.22 us
  transfers between devices with their start and end apart: 13, of which 6 were waited for; matrix products, arithmetic and copies ran while one was open for 3% of the time, Pallas kernels for 4%

profile of v7, /device:TPU:1, one launch (start us, length us, event | category | flops | bytes accessed | tf_op | source)
XLA Modules:
  0.0 97.2 jit_solution(12428168234584845769)
XLA Ops:
  0.6 2.0 %shard_map.69 = f32[8,4,32,256]{3,2,1,0:T(8,128)} custom-call(f32[4,32,256]{2,1,0:T(8,128)} %block_ref.1), custom_call_target="tpu_custom_call" | custom-call | tf_op jit(solution)/shard_map/pallas_call | solution.py:156
  2.7 10.9 %all-to-all-start.1 = ((f32[8,4,32,256]{3,2,1,0:T(8,128)}), f32[8,4,32,256]{3,2,1,0:T(8,128)S(1)}, u32[]{:S(2)}, u32[]{:S(2)}) async-start(f32[8,4,32,256]{3,2,1,0:T(8,128)} %shard_map.69), calls=%async_computation.1 | async-start | bytes 2097152 | tf_op jit(solution)/shard_map/all_to_all | solution.py:168
  13.7 0.2 convert_reduce_fusion.1
  13.9 0.1 select_reduce_fusion.1
  14.1 3.1 %collective-permute-start = (s32[16]{0:T(128)S(1)}, s32[16]{0:T(128)S(1)}, u32[]{:S(2)}, u32[]{:S(2)}) collective-permute-start(s32[16]{0:T(128)S(1)} %select_reduce_fusion.1), channel_id=1, source_target_pairs={{0,128},{8,136},{16,144},{24,152},{32,160},{40,168},{48,176},{56,1... | collective-permute-start | bytes 200 | tf_op jit(solution)/shard_map/ppermute | solution.py:138
  17.2 5.1 %collective-permute-start.3 = (f32[8,32,256]{2,1,0:T(8,128)S(1)}, f32[8,32,256]{2,1,0:T(8,128)S(1)}, u32[]{:S(2)}, u32[]{:S(2)}) collective-permute-start(f32[8,32,256]{2,1,0:T(8,128)S(1)} %bitcast.16), channel_id=1, source_target_pairs={{0,1},{1,2},{2,3},{3,4},{4,5},{5,6},{6,7},{7,0},{8,15},{9,8},{10,9... | collective-permute-start | bytes 786440 | tf_op jit(solution)/shard_map/ppermute | solution.py:172
  22.4 1.9 %collective-permute-start.1 = (f32[8,32,256]{2,1,0:T(8,128)S(1)}, f32[8,32,256]{2,1,0:T(8,128)S(1)}, u32[]{:S(2)}, u32[]{:S(2)}) collective-permute-start(f32[8,32,256]{2,1,0:T(8,128)S(1)} %bitcast.17), channel_id=1, source_target_pairs={{0,8},{8,0},{16,24},{24,16},{32,40},{40,32},{48,56},{56,48},{64,72... | collective-permute-start | bytes 786440 | tf_op jit(solution)/shard_map/ppermute | solution.py:139
  24.3 1.4 %collective-permute-done.1 = f32[8,32,256]{2,1,0:T(8,128)S(1)} collective-permute-done((f32[8,32,256]{2,1,0:T(8,128)S(1)}, f32[8,32,256]{2,1,0:T(8,128)S(1)}, u32[]{:S(2)}, u32[]{:S(2)}) %collective-permute-start.1) | collective-permute-done | bytes 262176 | tf_op jit(solution)/shard_map/ppermute | solution.py:139
  25.8 4.3 %collective-permute-start.2 = (s32[2,16]{1,0:T(2,128)S(1)}, s32[2,16]{1,0:T(2,128)S(1)}, u32[]{:S(2)}, u32[]{:S(2)}) collective-permute-start(s32[2,16]{1,0:T(2,128)S(1)} %pad_add_fusion.1), channel_id=1, source_target_pairs={{0,256},{8,264},{16,272},{24,280},{32,288},{40,296},{48,304},{56,3... | collective-permute-start | bytes 392 | tf_op jit(solution)/shard_map/ppermute | solution.py:143
  30.2 3.1 %collective-permute-start.4 = (f32[16,32,256]{2,1,0:T(8,128)S(1)}, f32[16,32,256]{2,1,0:T(8,128)S(1)}, u32[]{:S(2)}, u32[]{:S(2)}) collective-permute-start(f32[16,32,256]{2,1,0:T(8,128)S(1)} %pad_maximum_fusion), channel_id=1, source_target_pairs={{0,1},{1,2},{2,3},{3,4},{4,5},{5,6},{6,7},{7,0},{8,15},{9,8},{10,9... | collective-permute-start | bytes 1572872 | tf_op jit(solution)/shard_map/ppermute | solution.py:172
  33.3 0.6 gather_fusion
  33.9 0.2 convert_reduce_fusion.2
  34.2 0.6 subtract_reduce_fusion
  35.6 0.2 select_reduce_fusion
  35.9 4.5 %collective-permute-done.4.refs_1_ = f32[16,32,256]{2,1,0:T(8,128)S(1)} collective-permute-done((f32[16,32,256]{2,1,0:T(8,128)S(1)}, f32[16,32,256]{2,1,0:T(8,128)S(1)}, u32[]{:S(2)}, u32[]{:S(2)}) %collective-permute-start.4) | collective-permute-done | bytes 524320 | tf_op jit(solution)/shard_map/ppermute | solution.py:172
  40.4 2.3 %all-to-all-done.1 = f32[8,4,32,256]{3,2,1,0:T(8,128)S(1)} async-done(((f32[8,4,32,256]{3,2,1,0:T(8,128)}), f32[8,4,32,256]{3,2,1,0:T(8,128)S(1)}, u32[]{:S(2)}, u32[]{:S(2)}) %all-to-all-start.1) | async-done | bytes 1048608 | tf_op jit(solution)/shard_map/all_to_all | solution.py:168
  42.8 2.4 %collective-permute-start.6 = (f32[32,32,256]{2,1,0:T(8,128)S(1)}, f32[32,32,256]{2,1,0:T(8,128)S(1)}, u32[]{:S(2)}, u32[]{:S(2)}) collective-permute-start(f32[32,32,256]{2,1,0:T(8,128)S(1)} %bitcast.14), channel_id=1, source_target_pairs={{0,8},{8,0},{16,24},{24,16},{32,40},{40,32},{48,56},{56,48},{64,72... | collective-permute-start | bytes 3145736 | tf_op jit(solution)/shard_map/ppermute | solution.py:139
  45.2 5.1 %collective-permute-start.5 = (f32[16,32,256]{2,1,0:T(8,128)S(1)}, f32[16,32,256]{2,1,0:T(8,128)}, u32[]{:S(2)}, u32[]{:S(2)}) collective-permute-start(f32[16,32,256]{2,1,0:T(8,128)S(1)} %collective-permute-done.4.refs_1_), channel_id=1, source_target_pairs={{0,1},{1,2},{2,3},{3,4},{4,5},{5,6},{6,7},{7,0},{8,15},{9,8},{10,9... | collective-permute-start | bytes 1572872 | tf_op jit(solution)/shard_map/ppermute | solution.py:172
  50.5 2.0 %shard_map.70 = (f32[4,12,32,256]{3,2,1,0:T(8,128)}, f32[4,4,32,256]{3,2,1,0:T(8,128)}) custom-call(s32[64]{0:T(128)S(1)} %reshape.114.place_ref, f32[32,32,256]{2,1,0:T(8,128)S(1)} %bitcast.15, f32[32,32,256]{2,1,0:T(8,128)S(1)} %collective-permute-done.6.twins_ref), custom_call_target="tpu_custom_call" | custom-call | bytes 4000000 | tf_op jit(solution)/shard_map/pallas_call | solution.py:195
  52.5 4.3 %all-to-all-start.2 = ((f32[4,12,32,256]{3,2,1,0:T(8,128)}), f32[4,12,32,256]{3,2,1,0:T(8,128)}, u32[]{:S(2)}, u32[]{:S(2)}) async-start(f32[4,12,32,256]{3,2,1,0:T(8,128)} %get-tuple-element.39), calls=%async_computation.2 | async-start | bytes 3145728 | tf_op jit(solution)/shard_map/all_to_all | solution.py:204
  56.9 4.6 %collective-permute-start.7 = (f32[16,32,256]{2,1,0:T(8,128)}, f32[16,32,256]{2,1,0:T(8,128)S(1)}, u32[]{:S(2)}, u32[]{:S(2)}) collective-permute-start(f32[16,32,256]{2,1,0:T(8,128)} %collective-permute-done.5.refs_2_), channel_id=1, source_target_pairs={{0,1},{1,2},{2,3},{3,4},{4,5},{5,6},{6,7},{7,0},{8,15},{9,8},{10,9... | collective-permute-start | bytes 1572872 | tf_op jit(solution)/shard_map/ppermute | solution.py:172
  61.5 1.9 %collective-permute-start.8 = (f32[16,32,256]{2,1,0:T(8,128)}, f32[16,32,256]{2,1,0:T(8,128)S(1)}, u32[]{:S(2)}, u32[]{:S(2)}) collective-permute-start(f32[16,32,256]{2,1,0:T(8,128)} %copy-done.3), channel_id=1, source_target_pairs={{0,8},{8,0},{16,24},{24,16},{32,40},{40,32},{48,56},{56,48},{64,72... | collective-permute-start | bytes 1572872 | tf_op jit(solution)/shard_map/ppermute | solution.py:139
  63.5 2.4 %collective-permute-start.9 = (f32[16,32,256]{2,1,0:T(8,128)}, f32[16,32,256]{2,1,0:T(8,128)S(1)}, u32[]{:S(2)}, u32[]{:S(2)}) collective-permute-start(f32[16,32,256]{2,1,0:T(8,128)} %collective-permute-done.5.refs_2_), channel_id=1, source_target_pairs={{0,8},{8,0},{16,24},{24,16},{32,40},{40,32},{48,56},{56,48},{64,72... | collective-permute-start | bytes 1572872 | tf_op jit(solution)/shard_map/ppermute | solution.py:139
  65.9 2.1 %collective-permute-done.7.refs_3_ = f32[16,32,256]{2,1,0:T(8,128)S(1)} collective-permute-done((f32[16,32,256]{2,1,0:T(8,128)}, f32[16,32,256]{2,1,0:T(8,128)S(1)}, u32[]{:S(2)}, u32[]{:S(2)}) %collective-permute-start.7) | collective-permute-done | bytes 524320 | tf_op jit(solution)/shard_map/ppermute | solution.py:172
  68.0 4.3 %collective-permute-start.10 = (f32[16,32,256]{2,1,0:T(8,128)S(1)}, f32[16,32,256]{2,1,0:T(8,128)}, u32[]{:S(2)}, u32[]{:S(2)}) collective-permute-start(f32[16,32,256]{2,1,0:T(8,128)S(1)} %collective-permute-done.7.refs_3_), channel_id=1, source_target_pairs={{0,8},{8,0},{16,24},{24,16},{32,40},{40,32},{48,56},{56,48},{64,72... | collective-permute-start | bytes 1572872 | tf_op jit(solution)/shard_map/ppermute | solution.py:139
  72.3 0.8 copy-done.4
  73.1 0.8 collective-permute-done.10.refs_6_
  73.9 1.9 %shard_map.71.whole_ref = bf16[2,8,256,256]{3,2,1,0:T(8,128)(2,1)S(1)} custom-call(s32[8]{0:T(128)S(1)} %fusion.12.start_ref, f32[9,32,256]{2,1,0:T(8,128)S(1)} %shard_map.68.staged_ref, f32[8,32,256]{2,1,0:T(8,128)} %copy-done.2, f32[16,32,256]{2,1,0:T(8,128)} %copy-done.3, f32[16,32,256]{2,1,0:T(8,128)} %collective-permute-done.5.refs_2_, ...), custom_call_target="tpu_custom_call" | custom-call | bytes 4000000 | tf_op jit(solution)/shard_map/pallas_call | solution.py:209
  75.8 0.9 all-to-all-done.2
  76.8 3.2 %shard_map.72 = (f32[8,32,256]{2,1,0:T(8,128)}, f32[8,32,256]{2,1,0:T(8,128)S(1)}) custom-call(s32[64]{0:T(128)S(1)} %fusion.11.pick_ref, s32[1]{0:T(128)} %bitcast.7.mine_ref, f32[48,32,256]{2,1,0:T(8,128)} %bitcast.8.fetched_ref, f32[4,32,256]{2,1,0:T(8,128)S(1)} %get-tuple-element.51.extra_ref, f32[9,32,256]{2,1,0:T(8,128)S(1)} %shard_map.68.staged_ref, ...), custom_call_target="tpu_custom_call" | custom-call | flops 1000000000 | bytes 5000000 | tf_op jit(solution)/shard_map/pallas_call | solution.py:226
  80.0 16.6 %all_to_all.19 = f32[8,32,256]{2,1,0:T(8,128)S(1)} all-to-all(f32[8,32,256]{2,1,0:T(8,128)S(1)} %get-tuple-element.48), channel_id=1, replica_groups=mesh['snode'=64,'grp'=8] {'grp'}, dimensions={0} | all-to-all | bytes 524288 | tf_op jit(solution)/shard_map/all_to_all | solution.py:238
  96.6 0.6 reduce_sum.68
  (41 shorter events, 0.8 us)
Async XLA Ops:
  0.6 12.9 %copy-start.5 = (s32[1,8,8]{2,1,0:T(8,128)S(1)}, s32[1,8,8]{2,1,0:T(8,128)}, u32[]{:S(2)}) copy-start(s32[1,8,8]{2,1,0:T(8,128)} %param.9) | copy-start | bytes 772
  0.6 16.5 %copy-start = (f32[1,8,32,256]{3,2,1,0:T(8,128)S(1)}, f32[1,8,32,256]{3,2,1,0:T(8,128)}, u32[]{:S(2)}) copy-start(f32[1,8,32,256]{3,2,1,0:T(8,128)} %param.8) | copy-start | bytes 786436
  2.7 42.5 %copy-start.1 = (f32[1,32,256]{2,1,0:T(8,128)S(1)}, f32[1,32,256]{2,1,0:T(8,128)}, u32[]{:S(2)}) copy-start(f32[1,32,256]{2,1,0:T(8,128)} %param.10) | copy-start | bytes 98308
  2.7 40.1 %all-to-all-start.1 = ((f32[8,4,32,256]{3,2,1,0:T(8,128)}), f32[8,4,32,256]{3,2,1,0:T(8,128)S(1)}, u32[]{:S(2)}, u32[]{:S(2)}) async-start(f32[8,4,32,256]{3,2,1,0:T(8,128)} %shard_map.69), calls=%async_computation.1 | async-start | bytes 2097152 | tf_op jit(solution)/shard_map/all_to_all | solution.py:168
  14.1 8.3 %collective-permute-start = (s32[16]{0:T(128)S(1)}, s32[16]{0:T(128)S(1)}, u32[]{:S(2)}, u32[]{:S(2)}) collective-permute-start(s32[16]{0:T(128)S(1)} %select_reduce_fusion.1), channel_id=1, source_target_pairs={{0,128},{8,136},{16,144},{24,152},{32,160},{40,168},{48,176},{56,1... | collective-permute-start | bytes 200 | tf_op jit(solution)/shard_map/ppermute | solution.py:138
  17.2 12.9 %collective-permute-start.3 = (f32[8,32,256]{2,1,0:T(8,128)S(1)}, f32[8,32,256]{2,1,0:T(8,128)S(1)}, u32[]{:S(2)}, u32[]{:S(2)}) collective-permute-start(f32[8,32,256]{2,1,0:T(8,128)S(1)} %bitcast.16), channel_id=1, source_target_pairs={{0,1},{1,2},{2,3},{3,4},{4,5},{5,6},{6,7},{7,0},{8,15},{9,8},{10,9... | collective-permute-start | bytes 786440 | tf_op jit(solution)/shard_map/ppermute | solution.py:172
  22.4 3.4 %collective-permute-start.1 = (f32[8,32,256]{2,1,0:T(8,128)S(1)}, f32[8,32,256]{2,1,0:T(8,128)S(1)}, u32[]{:S(2)}, u32[]{:S(2)}) collective-permute-start(f32[8,32,256]{2,1,0:T(8,128)S(1)} %bitcast.17), channel_id=1, source_target_pairs={{0,8},{8,0},{16,24},{24,16},{32,40},{40,32},{48,56},{56,48},{64,72... | collective-permute-start | bytes 786440 | tf_op jit(solution)/shard_map/ppermute | solution.py:139
  25.8 7.5 %collective-permute-start.2 = (s32[2,16]{1,0:T(2,128)S(1)}, s32[2,16]{1,0:T(2,128)S(1)}, u32[]{:S(2)}, u32[]{:S(2)}) collective-permute-start(s32[2,16]{1,0:T(2,128)S(1)} %pad_add_fusion.1), channel_id=1, source_target_pairs={{0,256},{8,264},{16,272},{24,280},{32,288},{40,296},{48,304},{56,3... | collective-permute-start | bytes 392 | tf_op jit(solution)/shard_map/ppermute | solution.py:143
  30.1 12.6 %copy-start.2 = (f32[8,32,256]{2,1,0:T(8,128)}, f32[8,32,256]{2,1,0:T(8,128)S(1)}, u32[]{:S(2)}) copy-start(f32[8,32,256]{2,1,0:T(8,128)S(1)} %collective-permute-done.3.refs_0_) | copy-start | bytes 786436
  30.2 10.2 %collective-permute-start.4 = (f32[16,32,256]{2,1,0:T(8,128)S(1)}, f32[16,32,256]{2,1,0:T(8,128)S(1)}, u32[]{:S(2)}, u32[]{:S(2)}) collective-permute-start(f32[16,32,256]{2,1,0:T(8,128)S(1)} %pad_maximum_fusion), channel_id=1, source_target_pairs={{0,1},{1,2},{2,3},{3,4},{4,5},{5,6},{6,7},{7,0},{8,15},{9,8},{10,9... | collective-permute-start | bytes 1572872 | tf_op jit(solution)/shard_map/ppermute | solution.py:172
  40.4 16.4 %copy-start.3 = (f32[16,32,256]{2,1,0:T(8,128)}, f32[16,32,256]{2,1,0:T(8,128)S(1)}, u32[]{:S(2)}) copy-start(f32[16,32,256]{2,1,0:T(8,128)S(1)} %collective-permute-done.4.refs_1_) | copy-start | bytes 1572868
  42.8 7.7 %collective-permute-start.6 = (f32[32,32,256]{2,1,0:T(8,128)S(1)}, f32[32,32,256]{2,1,0:T(8,128)S(1)}, u32[]{:S(2)}, u32[]{:S(2)}) collective-permute-start(f32[32,32,256]{2,1,0:T(8,128)S(1)} %bitcast.14), channel_id=1, source_target_pairs={{0,8},{8,0},{16,24},{24,16},{32,40},{40,32},{48,56},{56,48},{64,72... | collective-permute-start | bytes 3145736 | tf_op jit(solution)/shard_map/ppermute | solution.py:139
  45.2 11.7 %collective-permute-start.5 = (f32[16,32,256]{2,1,0:T(8,128)S(1)}, f32[16,32,256]{2,1,0:T(8,128)}, u32[]{:S(2)}, u32[]{:S(2)}) collective-permute-start(f32[16,32,256]{2,1,0:T(8,128)S(1)} %collective-permute-done.4.refs_1_), channel_id=1, source_target_pairs={{0,1},{1,2},{2,3},{3,4},{4,5},{5,6},{6,7},{7,0},{8,15},{9,8},{10,9... | collective-permute-start | bytes 1572872 | tf_op jit(solution)/shard_map/ppermute | solution.py:172
  52.5 19.8 %copy-start.6 = (s32[8]{0:T(128)S(1)}, s32[8]{0:T(128)}, u32[]{:S(2)}) copy-start(s32[8]{0:T(128)} %constant.167.clone) | copy-start | bytes 100
  52.5 24.3 %all-to-all-start.2 = ((f32[4,12,32,256]{3,2,1,0:T(8,128)}), f32[4,12,32,256]{3,2,1,0:T(8,128)}, u32[]{:S(2)}, u32[]{:S(2)}) async-start(f32[4,12,32,256]{3,2,1,0:T(8,128)} %get-tuple-element.39), calls=%async_computation.2 | async-start | bytes 3145728 | tf_op jit(solution)/shard_map/all_to_all | solution.py:204
  56.9 11.1 %collective-permute-start.7 = (f32[16,32,256]{2,1,0:T(8,128)}, f32[16,32,256]{2,1,0:T(8,128)S(1)}, u32[]{:S(2)}, u32[]{:S(2)}) collective-permute-start(f32[16,32,256]{2,1,0:T(8,128)} %collective-permute-done.5.refs_2_), channel_id=1, source_target_pairs={{0,1},{1,2},{2,3},{3,4},{4,5},{5,6},{6,7},{7,0},{8,15},{9,8},{10,9... | collective-permute-start | bytes 1572872 | tf_op jit(solution)/shard_map/ppermute | solution.py:172
  61.5 10.7 %collective-permute-start.8 = (f32[16,32,256]{2,1,0:T(8,128)}, f32[16,32,256]{2,1,0:T(8,128)S(1)}, u32[]{:S(2)}, u32[]{:S(2)}) collective-permute-start(f32[16,32,256]{2,1,0:T(8,128)} %copy-done.3), channel_id=1, source_target_pairs={{0,8},{8,0},{16,24},{24,16},{32,40},{40,32},{48,56},{56,48},{64,72... | collective-permute-start | bytes 1572872 | tf_op jit(solution)/shard_map/ppermute | solution.py:139
  63.5 8.8 %collective-permute-start.9 = (f32[16,32,256]{2,1,0:T(8,128)}, f32[16,32,256]{2,1,0:T(8,128)S(1)}, u32[]{:S(2)}, u32[]{:S(2)}) collective-permute-start(f32[16,32,256]{2,1,0:T(8,128)} %collective-permute-done.5.refs_2_), channel_id=1, source_target_pairs={{0,8},{8,0},{16,24},{24,16},{32,40},{40,32},{48,56},{56,48},{64,72... | collective-permute-start | bytes 1572872 | tf_op jit(solution)/shard_map/ppermute | solution.py:139
  68.0 5.9 %collective-permute-start.10 = (f32[16,32,256]{2,1,0:T(8,128)S(1)}, f32[16,32,256]{2,1,0:T(8,128)}, u32[]{:S(2)}, u32[]{:S(2)}) collective-permute-start(f32[16,32,256]{2,1,0:T(8,128)S(1)} %collective-permute-done.7.refs_3_), channel_id=1, source_target_pairs={{0,8},{8,0},{16,24},{24,16},{32,40},{40,32},{48,56},{56,48},{64,72... | collective-permute-start | bytes 1572872 | tf_op jit(solution)/shard_map/ppermute | solution.py:139
  72.3 0.8 copy-start.4

commit v8 on v7

--- a/solution.py
+++ b/solution.py
@@ -81,23 +81,33 @@
     staged_ref[own_ref.shape[0]] = diag_ref[...]
 
 
+def place_rows(whole_ref, start, rows, piece):
+    start = pl.multiple_of(start, rows)
+    high, low = split(piece)
+    whole_ref[0, :, pl.ds(start, rows), :] = high
+    whole_ref[1, :, pl.ds(start, rows), :] = low
+
+
 def assemble(start_ref, staged_ref, *refs):
     *pieces, whole_ref, raw_ref, sems = refs
     _, kcount, width, _ = whole_ref.shape
     rows = width // NY
-    messages = (len(pieces) - 1) // 2
-    parts = [piece.at[pl.ds(0, kcount)] for piece in pieces[: 1 + messages]]
-    parts += [piece.at[pl.ds(kcount, kcount)] for piece in pieces[1 + messages :]]
+    leads = (len(pieces) + 1) // 2
+    parts = [piece.at[pl.ds(0 if n < leads else kcount, kcount)] for n, piece in enumerate(pieces)]
     copies = [pltpu.make_async_copy(part, raw_ref.at[n], sems.at[n]) for n, part in enumerate(parts)]
     for copy in copies:
         copy.start()
-    for number in range(NY):
-        if number:
-            copies[number - 1].wait()
-        start = pl.multiple_of(start_ref[number], rows)
-        high, low = split(raw_ref[number - 1] if number else staged_ref[:kcount])
-        whole_ref[0, :, pl.ds(start, rows), :] = high
-        whole_ref[1, :, pl.ds(start, rows), :] = low
+    place_rows(whole_ref, start_ref[0], rows, staged_ref[:kcount])
+    for number, copy in enumerate(copies):
+        copy.wait()
+        place_rows(whole_ref, start_ref[number + 1], rows, raw_ref[number])
+
+
+def complete(start_ref, lead_ref, lag_ref, _, whole_ref):
+    _, kcount, width, _ = whole_ref.shape
+    rows = width // NY
+    place_rows(whole_ref, start_ref[NY - 2], rows, lead_ref[:kcount])
+    place_rows(whole_ref, start_ref[NY - 1], rows, lag_ref[kcount:])
 
 
 def products(pick_ref, mine_ref, fetched_ref, extra_ref, staged_ref, whole_ref, off_ref, update_ref, held_ref, sem):
@@ -189,8 +199,7 @@
     messages.append(on(following))
     before, last, _ = lax.optimization_barrier((messages[0], messages[1], following))
     swapped = [twin(before), twin(last), twin(messages[2])]
-    pieces = [lead] + messages + swapped
-    pieces = [in_vmem(piece) if number in (3, 4) else in_hbm(piece) for number, piece in enumerate(pieces)]
+    pieces = [in_hbm(piece) for piece in [lead, *messages[:2], *swapped[:2]]]
 
     few, rest = pl.pallas_call(
         collect,
@@ -205,16 +214,29 @@
         v, "snode", split_axis=0, concat_axis=0, tiled=True, axis_index_groups=X_LINES
     )
     fetched = over_x(few).reshape((NX * FEW,) + block)
-    starts = (y + (2 * c - 1) * jnp.array([0, 1, 2, 3, 4, -1, -2, -3], jnp.int32)) % NY * rows
+    starts = (y + (2 * c - 1) * jnp.array([0, 1, 2, 3, -1, -2, 4, -3], jnp.int32)) % NY * rows
+    whole_shape = pltpu.VMEM((2, kcount, NY * rows, width), jnp.bfloat16)
     whole = pl.pallas_call(
         assemble,
-        out_shape=pltpu.VMEM((2, kcount, NY * rows, width), jnp.bfloat16),
-        in_specs=[SMEM, VMEM] + [VMEM if number in (3, 4) else HBM for number in range(len(pieces))],
+        out_shape=whole_shape,
+        in_specs=[SMEM, VMEM] + [HBM] * len(pieces),
         out_specs=VMEM,
-        scratch_shapes=[pltpu.VMEM((NY - 1, kcount) + block, jnp.float32), pltpu.SemaphoreType.DMA((NY - 1,))],
+        scratch_shapes=[
+            pltpu.VMEM((len(pieces), kcount) + block, jnp.float32),
+            pltpu.SemaphoreType.DMA((len(pieces),)),
+        ],
         compiler_params=PARAMS,
         cost_estimate=pl.CostEstimate(flops=0, bytes_accessed=4_000_000, transcendentals=0),
     )(starts, in_vmem(staged), *pieces)
+    whole = pl.pallas_call(
+        complete,
+        out_shape=whole_shape,
+        in_specs=[SMEM] + [VMEM] * 3,
+        out_specs=VMEM,
+        input_output_aliases={3: 0},
+        compiler_params=PARAMS,
+        cost_estimate=pl.CostEstimate(flops=0, bytes_accessed=1_000_000, transcendentals=0),
+    )(starts, in_vmem(messages[2]), in_vmem(swapped[2]), in_vmem(whole))
     _, rest = lax.optimization_barrier((fetched, rest))
 
     def more(rest, distinct):

time: 98.1 us -> 99.1 us (1.010)
  blocking collectives: 16.6 us -> 17.9 us
    all_to_all x1, blocking collectives: 16.6 us -> 17.9 us  [per_device(): lax.all_to_all(update, 'grp', split_axis=0, concat_axis=0, tiled=True)]
    pallas_call x1 -> x2, Pallas kernels: 1.92 us -> 2.51 us  [the longest x1 1.89 us: per_device(): pl.pallas_call(assemble, out_shape=whole_shape, in_specs=[SMEM, VMEM] + [...]
  transfers between devices with their start and end apart: 13 -> 13, of which waited for: 6 -> 5; matrix products, arithmetic and copies ran while one was open for 3% -> 3% of each run, Pallas kernels for 4% -> 5%
where the time goes in v8:
time: 99.1 us; the launch traced here: 98.5 us
  starting transfers between devices  53.8 us (54%)
  blocking collectives  17.9 us (18%)
  waiting for transfers between devices  11.3 us (11%)
  Pallas kernels  9.76 us (10%)
  other arithmetic  2.6 us (3%)
  between operations  1.68 us (2%)
  local copies, waits for them, and re-layouts  1.56 us (2%)
    ppermute x4, starting transfers between devices, per_device(): on = lambda v: lax.ppermute(v, ('snode', 'grp'), Y_ROUND)  18.2 us
    all_to_all x1, blocking collectives, per_device(): lax.all_to_all(update, 'grp', split_axis=0, concat_axis=0, tiled=True)  17.9 us
    ppermute x5, starting transfers between devices, per_device(): twin = lambda v: lax.ppermute(v, 'snode', TWIN)  12.9 us
    all_to_all x1, starting transfers between devices, per_device(): lax.all_to_all(copies, 'snode', split_axis=0, concat_axis=0, tiled=True,...  10.9 us
    ppermute x4, waiting for transfers between devices, per_device(): on = lambda v: lax.ppermute(v, ('snode', 'grp'), Y_ROUND)  6.68 us
    ppermute x1, starting transfers between devices, per_device(): lists = jnp.concatenate([pair, lax.ppermute(pair, 'snode', X_TWO)])  4.35 us
    all_to_all x1, starting transfers between devices, per_device(): lax.all_to_all(v, 'snode', split_axis=0, concat_axis=0, tiled=True, axis_...  4.35 us
    pallas_call x1, Pallas kernels, per_device(): pl.pallas_call(products, out_shape=(pltpu.HBM((kcount,) + block, jnp.floa...  3.22 us
  transfers between devices with their start and end apart: 13, of which 5 were waited for; matrix products, arithmetic and copies ran while one was open for 3% of the time, Pallas kernels for 5%

profile of v8, /device:TPU:1, one launch (start us, length us, event | category | flops | bytes accessed | tf_op | source)
XLA Modules:
  0.0 98.5 jit_solution(4312139364851885620)
XLA Ops:
  0.7 2.0 %shard_map.69 = f32[8,4,32,256]{3,2,1,0:T(8,128)} custom-call(f32[4,32,256]{2,1,0:T(8,128)} %block_ref.1), custom_call_target="tpu_custom_call" | custom-call | tf_op jit(solution)/shard_map/pallas_call | solution.py:166
  2.7 10.9 %all-to-all-start.1 = ((f32[8,4,32,256]{3,2,1,0:T(8,128)}), f32[8,4,32,256]{3,2,1,0:T(8,128)S(1)}, u32[]{:S(2)}, u32[]{:S(2)}) async-start(f32[8,4,32,256]{3,2,1,0:T(8,128)} %shard_map.69), calls=%async_computation.1 | async-start | bytes 2097152 | tf_op jit(solution)/shard_map/all_to_all | solution.py:178
  13.7 0.2 convert_reduce_fusion.1
  13.9 0.1 select_reduce_fusion.1
  14.1 3.1 %collective-permute-start = (s32[16]{0:T(128)S(1)}, s32[16]{0:T(128)S(1)}, u32[]{:S(2)}, u32[]{:S(2)}) collective-permute-start(s32[16]{0:T(128)S(1)} %select_reduce_fusion.1), channel_id=1, source_target_pairs={{0,128},{8,136},{16,144},{24,152},{32,160},{40,168},{48,176},{56,1... | collective-permute-start | bytes 200 | tf_op jit(solution)/shard_map/ppermute | solution.py:148
  17.2 5.1 %collective-permute-start.3 = (f32[8,32,256]{2,1,0:T(8,128)S(1)}, f32[8,32,256]{2,1,0:T(8,128)S(1)}, u32[]{:S(2)}, u32[]{:S(2)}) collective-permute-start(f32[8,32,256]{2,1,0:T(8,128)S(1)} %bitcast.16), channel_id=1, source_target_pairs={{0,1},{1,2},{2,3},{3,4},{4,5},{5,6},{6,7},{7,0},{8,15},{9,8},{10,9... | collective-permute-start | bytes 786440 | tf_op jit(solution)/shard_map/ppermute | solution.py:182
  22.4 1.9 %collective-permute-start.1 = (f32[8,32,256]{2,1,0:T(8,128)S(1)}, f32[8,32,256]{2,1,0:T(8,128)S(1)}, u32[]{:S(2)}, u32[]{:S(2)}) collective-permute-start(f32[8,32,256]{2,1,0:T(8,128)S(1)} %bitcast.17), channel_id=1, source_target_pairs={{0,8},{8,0},{16,24},{24,16},{32,40},{40,32},{48,56},{56,48},{64,72... | collective-permute-start | bytes 786440 | tf_op jit(solution)/shard_map/ppermute | solution.py:149
  24.3 1.4 %collective-permute-done.1 = f32[8,32,256]{2,1,0:T(8,128)S(1)} collective-permute-done((f32[8,32,256]{2,1,0:T(8,128)S(1)}, f32[8,32,256]{2,1,0:T(8,128)S(1)}, u32[]{:S(2)}, u32[]{:S(2)}) %collective-permute-start.1) | collective-permute-done | bytes 262176 | tf_op jit(solution)/shard_map/ppermute | solution.py:149
  25.8 4.3 %collective-permute-start.2 = (s32[2,16]{1,0:T(2,128)S(1)}, s32[2,16]{1,0:T(2,128)S(1)}, u32[]{:S(2)}, u32[]{:S(2)}) collective-permute-start(s32[2,16]{1,0:T(2,128)S(1)} %pad_add_fusion.1), channel_id=1, source_target_pairs={{0,256},{8,264},{16,272},{24,280},{32,288},{40,296},{48,304},{56,3... | collective-permute-start | bytes 392 | tf_op jit(solution)/shard_map/ppermute | solution.py:153
  30.2 3.1 %collective-permute-start.4 = (f32[16,32,256]{2,1,0:T(8,128)S(1)}, f32[16,32,256]{2,1,0:T(8,128)}, u32[]{:S(2)}, u32[]{:S(2)}) collective-permute-start(f32[16,32,256]{2,1,0:T(8,128)S(1)} %pad_maximum_fusion), channel_id=1, source_target_pairs={{0,1},{1,2},{2,3},{3,4},{4,5},{5,6},{6,7},{7,0},{8,15},{9,8},{10,9... | collective-permute-start | bytes 1572872 | tf_op jit(solution)/shard_map/ppermute | solution.py:182
  33.3 0.6 gather_fusion
  33.9 0.2 convert_reduce_fusion.2
  34.1 0.6 subtract_reduce_fusion
  35.6 0.2 select_reduce_fusion
  35.9 4.6 %collective-permute-done.4.refs_1_ = f32[16,32,256]{2,1,0:T(8,128)} collective-permute-done((f32[16,32,256]{2,1,0:T(8,128)S(1)}, f32[16,32,256]{2,1,0:T(8,128)}, u32[]{:S(2)}, u32[]{:S(2)}) %collective-permute-start.4) | collective-permute-done | bytes 524320 | tf_op jit(solution)/shard_map/ppermute | solution.py:182
  40.5 2.2 %all-to-all-done.1 = f32[8,4,32,256]{3,2,1,0:T(8,128)S(1)} async-done(((f32[8,4,32,256]{3,2,1,0:T(8,128)}), f32[8,4,32,256]{3,2,1,0:T(8,128)S(1)}, u32[]{:S(2)}, u32[]{:S(2)}) %all-to-all-start.1) | async-done | bytes 1048608 | tf_op jit(solution)/shard_map/all_to_all | solution.py:178
  42.8 2.4 %collective-permute-start.6 = (f32[32,32,256]{2,1,0:T(8,128)S(1)}, f32[32,32,256]{2,1,0:T(8,128)S(1)}, u32[]{:S(2)}, u32[]{:S(2)}) collective-permute-start(f32[32,32,256]{2,1,0:T(8,128)S(1)} %bitcast.14), channel_id=1, source_target_pairs={{0,8},{8,0},{16,24},{24,16},{32,40},{40,32},{48,56},{56,48},{64,72... | collective-permute-start | bytes 3145736 | tf_op jit(solution)/shard_map/ppermute | solution.py:149
  45.2 5.1 %collective-permute-start.5 = (f32[16,32,256]{2,1,0:T(8,128)}, f32[16,32,256]{2,1,0:T(8,128)}, u32[]{:S(2)}, u32[]{:S(2)}) collective-permute-start(f32[16,32,256]{2,1,0:T(8,128)} %collective-permute-done.4.refs_1_), channel_id=1, source_target_pairs={{0,1},{1,2},{2,3},{3,4},{4,5},{5,6},{6,7},{7,0},{8,15},{9,8},{10,9... | collective-permute-start | bytes 1572872 | tf_op jit(solution)/shard_map/ppermute | solution.py:182
  50.5 2.0 %shard_map.70 = (f32[4,12,32,256]{3,2,1,0:T(8,128)}, f32[4,4,32,256]{3,2,1,0:T(8,128)}) custom-call(s32[64]{0:T(128)S(1)} %reshape.114.place_ref, f32[32,32,256]{2,1,0:T(8,128)S(1)} %bitcast.15, f32[32,32,256]{2,1,0:T(8,128)S(1)} %collective-permute-done.6.twins_ref), custom_call_target="tpu_custom_call" | custom-call | bytes 4000000 | tf_op jit(solution)/shard_map/pallas_call | solution.py:204
  52.5 4.3 %all-to-all-start.2 = ((f32[4,12,32,256]{3,2,1,0:T(8,128)}), f32[4,12,32,256]{3,2,1,0:T(8,128)}, u32[]{:S(2)}, u32[]{:S(2)}) async-start(f32[4,12,32,256]{3,2,1,0:T(8,128)} %get-tuple-element.39), calls=%async_computation.2 | async-start | bytes 3145728 | tf_op jit(solution)/shard_map/all_to_all | solution.py:213
  56.9 4.9 %collective-permute-start.7 = (f32[16,32,256]{2,1,0:T(8,128)}, f32[16,32,256]{2,1,0:T(8,128)S(1)}, u32[]{:S(2)}, u32[]{:S(2)}) collective-permute-start(f32[16,32,256]{2,1,0:T(8,128)} %collective-permute-done.5.refs_2_), channel_id=1, source_target_pairs={{0,1},{1,2},{2,3},{3,4},{4,5},{5,6},{6,7},{7,0},{8,15},{9,8},{10,9... | collective-permute-start | bytes 1572872 | tf_op jit(solution)/shard_map/ppermute | solution.py:182
  61.7 1.9 %collective-permute-start.9 = (f32[16,32,256]{2,1,0:T(8,128)}, f32[16,32,256]{2,1,0:T(8,128)S(1)}, u32[]{:S(2)}, u32[]{:S(2)}) collective-permute-start(f32[16,32,256]{2,1,0:T(8,128)} %collective-permute-done.4.refs_1_), channel_id=1, source_target_pairs={{0,8},{8,0},{16,24},{24,16},{32,40},{40,32},{48,56},{56,48},{64,72... | collective-permute-start | bytes 1572872 | tf_op jit(solution)/shard_map/ppermute | solution.py:149
  63.7 2.4 %collective-permute-start.10 = (f32[16,32,256]{2,1,0:T(8,128)}, f32[16,32,256]{2,1,0:T(8,128)}, u32[]{:S(2)}, u32[]{:S(2)}) collective-permute-start(f32[16,32,256]{2,1,0:T(8,128)} %collective-permute-done.5.refs_2_), channel_id=1, source_target_pairs={{0,8},{8,0},{16,24},{24,16},{32,40},{40,32},{48,56},{56,48},{64,72... | collective-permute-start | bytes 1572872 | tf_op jit(solution)/shard_map/ppermute | solution.py:149
  66.1 2.1 %collective-permute-done.7.lead_ref = f32[16,32,256]{2,1,0:T(8,128)S(1)} collective-permute-done((f32[16,32,256]{2,1,0:T(8,128)}, f32[16,32,256]{2,1,0:T(8,128)S(1)}, u32[]{:S(2)}, u32[]{:S(2)}) %collective-permute-start.7) | collective-permute-done | bytes 524320 | tf_op jit(solution)/shard_map/ppermute | solution.py:182
  68.2 4.3 %collective-permute-start.8 = (f32[16,32,256]{2,1,0:T(8,128)S(1)}, f32[16,32,256]{2,1,0:T(8,128)S(1)}, u32[]{:S(2)}, u32[]{:S(2)}) collective-permute-start(f32[16,32,256]{2,1,0:T(8,128)S(1)} %collective-permute-done.7.lead_ref), channel_id=1, source_target_pairs={{0,8},{8,0},{16,24},{24,16},{32,40},{40,32},{48,56},{56,48},{64,72... | collective-permute-start | bytes 1572872 | tf_op jit(solution)/shard_map/ppermute | solution.py:149
  72.5 0.8 copy-done.3
  73.3 1.9 %shard_map.71._ = bf16[2,8,256,256]{3,2,1,0:T(8,128)(2,1)S(1)} custom-call(s32[8]{0:T(128)S(1)} %fusion.12.start_ref, f32[9,32,256]{2,1,0:T(8,128)S(1)} %shard_map.68.staged_ref, f32[8,32,256]{2,1,0:T(8,128)} %copy-done.2, f32[16,32,256]{2,1,0:T(8,128)} %collective-permute-done.4.refs_1_, f32[16,32,256]{2,1,0:T(8,128)} %collective-permute-done.5.refs_2_, ...), custom_call_target="tpu_custom_call" | custom-call | bytes 4000000 | tf_op jit(solution)/shard_map/pallas_call | solution.py:219
  75.2 0.6 shard_map.72.whole_ref
  75.8 0.9 all-to-all-done.2
  76.8 3.2 %shard_map.73 = (f32[8,32,256]{2,1,0:T(8,128)}, f32[8,32,256]{2,1,0:T(8,128)S(1)}) custom-call(s32[64]{0:T(128)S(1)} %fusion.11.pick_ref, s32[1]{0:T(128)} %bitcast.7.mine_ref, f32[48,32,256]{2,1,0:T(8,128)} %bitcast.8.fetched_ref, f32[4,32,256]{2,1,0:T(8,128)S(1)} %get-tuple-element.51.extra_ref, f32[9,32,256]{2,1,0:T(8,128)S(1)} %shard_map.68.staged_ref, ...), custom_call_target="tpu_custom_call" | custom-call | flops 1000000000 | bytes 5000000 | tf_op jit(solution)/shard_map/pallas_call | solution.py:248
  80.0 17.9 %all_to_all.19 = f32[8,32,256]{2,1,0:T(8,128)S(1)} all-to-all(f32[8,32,256]{2,1,0:T(8,128)S(1)} %get-tuple-element.48), channel_id=1, replica_groups=mesh['snode'=64,'grp'=8] {'grp'}, dimensions={0} | all-to-all | bytes 524288 | tf_op jit(solution)/shard_map/all_to_all | solution.py:260
  97.9 0.6 reduce_sum.68
  (40 shorter events, 0.8 us)
Async XLA Ops:
  0.6 12.9 %copy-start.4 = (s32[1,8,8]{2,1,0:T(8,128)S(1)}, s32[1,8,8]{2,1,0:T(8,128)}, u32[]{:S(2)}) copy-start(s32[1,8,8]{2,1,0:T(8,128)} %param.9) | copy-start | bytes 772
  0.6 16.5 %copy-start = (f32[1,8,32,256]{3,2,1,0:T(8,128)S(1)}, f32[1,8,32,256]{3,2,1,0:T(8,128)}, u32[]{:S(2)}) copy-start(f32[1,8,32,256]{3,2,1,0:T(8,128)} %param.8) | copy-start | bytes 786436
  0.7 44.5 %copy-start.1 = (f32[1,32,256]{2,1,0:T(8,128)S(1)}, f32[1,32,256]{2,1,0:T(8,128)}, u32[]{:S(2)}) copy-start(f32[1,32,256]{2,1,0:T(8,128)} %param.10) | copy-start | bytes 98308
  2.7 40.1 %all-to-all-start.1 = ((f32[8,4,32,256]{3,2,1,0:T(8,128)}), f32[8,4,32,256]{3,2,1,0:T(8,128)S(1)}, u32[]{:S(2)}, u32[]{:S(2)}) async-start(f32[8,4,32,256]{3,2,1,0:T(8,128)} %shard_map.69), calls=%async_computation.1 | async-start | bytes 2097152 | tf_op jit(solution)/shard_map/all_to_all | solution.py:178
  14.1 8.3 %collective-permute-start = (s32[16]{0:T(128)S(1)}, s32[16]{0:T(128)S(1)}, u32[]{:S(2)}, u32[]{:S(2)}) collective-permute-start(s32[16]{0:T(128)S(1)} %select_reduce_fusion.1), channel_id=1, source_target_pairs={{0,128},{8,136},{16,144},{24,152},{32,160},{40,168},{48,176},{56,1... | collective-permute-start | bytes 200 | tf_op jit(solution)/shard_map/ppermute | solution.py:148
  17.2 12.9 %collective-permute-start.3 = (f32[8,32,256]{2,1,0:T(8,128)S(1)}, f32[8,32,256]{2,1,0:T(8,128)S(1)}, u32[]{:S(2)}, u32[]{:S(2)}) collective-permute-start(f32[8,32,256]{2,1,0:T(8,128)S(1)} %bitcast.16), channel_id=1, source_target_pairs={{0,1},{1,2},{2,3},{3,4},{4,5},{5,6},{6,7},{7,0},{8,15},{9,8},{10,9... | collective-permute-start | bytes 786440 | tf_op jit(solution)/shard_map/ppermute | solution.py:182
  22.4 3.4 %collective-permute-start.1 = (f32[8,32,256]{2,1,0:T(8,128)S(1)}, f32[8,32,256]{2,1,0:T(8,128)S(1)}, u32[]{:S(2)}, u32[]{:S(2)}) collective-permute-start(f32[8,32,256]{2,1,0:T(8,128)S(1)} %bitcast.17), channel_id=1, source_target_pairs={{0,8},{8,0},{16,24},{24,16},{32,40},{40,32},{48,56},{56,48},{64,72... | collective-permute-start | bytes 786440 | tf_op jit(solution)/shard_map/ppermute | solution.py:149
  25.8 7.5 %collective-permute-start.2 = (s32[2,16]{1,0:T(2,128)S(1)}, s32[2,16]{1,0:T(2,128)S(1)}, u32[]{:S(2)}, u32[]{:S(2)}) collective-permute-start(s32[2,16]{1,0:T(2,128)S(1)} %pad_add_fusion.1), channel_id=1, source_target_pairs={{0,256},{8,264},{16,272},{24,280},{32,288},{40,296},{48,304},{56,3... | collective-permute-start | bytes 392 | tf_op jit(solution)/shard_map/ppermute | solution.py:153
  30.1 12.6 %copy-start.2 = (f32[8,32,256]{2,1,0:T(8,128)}, f32[8,32,256]{2,1,0:T(8,128)S(1)}, u32[]{:S(2)}) copy-start(f32[8,32,256]{2,1,0:T(8,128)S(1)} %collective-permute-done.3.refs_0_) | copy-start | bytes 786436
  30.2 10.3 %collective-permute-start.4 = (f32[16,32,256]{2,1,0:T(8,128)S(1)}, f32[16,32,256]{2,1,0:T(8,128)}, u32[]{:S(2)}, u32[]{:S(2)}) collective-permute-start(f32[16,32,256]{2,1,0:T(8,128)S(1)} %pad_maximum_fusion), channel_id=1, source_target_pairs={{0,1},{1,2},{2,3},{3,4},{4,5},{5,6},{6,7},{7,0},{8,15},{9,8},{10,9... | collective-permute-start | bytes 1572872 | tf_op jit(solution)/shard_map/ppermute | solution.py:182
  42.8 7.7 %collective-permute-start.6 = (f32[32,32,256]{2,1,0:T(8,128)S(1)}, f32[32,32,256]{2,1,0:T(8,128)S(1)}, u32[]{:S(2)}, u32[]{:S(2)}) collective-permute-start(f32[32,32,256]{2,1,0:T(8,128)S(1)} %bitcast.14), channel_id=1, source_target_pairs={{0,8},{8,0},{16,24},{24,16},{32,40},{40,32},{48,56},{56,48},{64,72... | collective-permute-start | bytes 3145736 | tf_op jit(solution)/shard_map/ppermute | solution.py:149
  45.2 11.7 %collective-permute-start.5 = (f32[16,32,256]{2,1,0:T(8,128)}, f32[16,32,256]{2,1,0:T(8,128)}, u32[]{:S(2)}, u32[]{:S(2)}) collective-permute-start(f32[16,32,256]{2,1,0:T(8,128)} %collective-permute-done.4.refs_1_), channel_id=1, source_target_pairs={{0,1},{1,2},{2,3},{3,4},{4,5},{5,6},{6,7},{7,0},{8,15},{9,8},{10,9... | collective-permute-start | bytes 1572872 | tf_op jit(solution)/shard_map/ppermute | solution.py:182
  52.5 20.0 %copy-start.5 = (s32[8]{0:T(128)S(1)}, s32[8]{0:T(128)}, u32[]{:S(2)}) copy-start(s32[8]{0:T(128)} %constant.167.clone) | copy-start | bytes 100
  52.5 24.3 %all-to-all-start.2 = ((f32[4,12,32,256]{3,2,1,0:T(8,128)}), f32[4,12,32,256]{3,2,1,0:T(8,128)}, u32[]{:S(2)}, u32[]{:S(2)}) async-start(f32[4,12,32,256]{3,2,1,0:T(8,128)} %get-tuple-element.39), calls=%async_computation.2 | async-start | bytes 3145728 | tf_op jit(solution)/shard_map/all_to_all | solution.py:213
  56.9 11.3 %collective-permute-start.7 = (f32[16,32,256]{2,1,0:T(8,128)}, f32[16,32,256]{2,1,0:T(8,128)S(1)}, u32[]{:S(2)}, u32[]{:S(2)}) collective-permute-start(f32[16,32,256]{2,1,0:T(8,128)} %collective-permute-done.5.refs_2_), channel_id=1, source_target_pairs={{0,1},{1,2},{2,3},{3,4},{4,5},{5,6},{6,7},{7,0},{8,15},{9,8},{10,9... | collective-permute-start | bytes 1572872 | tf_op jit(solution)/shard_map/ppermute | solution.py:182
  61.7 10.7 %collective-permute-start.9 = (f32[16,32,256]{2,1,0:T(8,128)}, f32[16,32,256]{2,1,0:T(8,128)S(1)}, u32[]{:S(2)}, u32[]{:S(2)}) collective-permute-start(f32[16,32,256]{2,1,0:T(8,128)} %collective-permute-done.4.refs_1_), channel_id=1, source_target_pairs={{0,8},{8,0},{16,24},{24,16},{32,40},{40,32},{48,56},{56,48},{64,72... | collective-permute-start | bytes 1572872 | tf_op jit(solution)/shard_map/ppermute | solution.py:149
  63.7 9.6 %collective-permute-start.10 = (f32[16,32,256]{2,1,0:T(8,128)}, f32[16,32,256]{2,1,0:T(8,128)}, u32[]{:S(2)}, u32[]{:S(2)}) collective-permute-start(f32[16,32,256]{2,1,0:T(8,128)} %collective-permute-done.5.refs_2_), channel_id=1, source_target_pairs={{0,8},{8,0},{16,24},{24,16},{32,40},{40,32},{48,56},{56,48},{64,72... | collective-permute-start | bytes 1572872 | tf_op jit(solution)/shard_map/ppermute | solution.py:149
  68.2 7.0 %collective-permute-start.8 = (f32[16,32,256]{2,1,0:T(8,128)S(1)}, f32[16,32,256]{2,1,0:T(8,128)S(1)}, u32[]{:S(2)}, u32[]{:S(2)}) collective-permute-start(f32[16,32,256]{2,1,0:T(8,128)S(1)} %collective-permute-done.7.lead_ref), channel_id=1, source_target_pairs={{0,8},{8,0},{16,24},{24,16},{32,40},{40,32},{48,56},{56,48},{64,72... | collective-permute-start | bytes 1572872 | tf_op jit(solution)/shard_map/ppermute | solution.py:149
  72.5 0.8 copy-start.3
